TPU v7x, 32 devices: a whole 2x2x4 slice. The times are simulated.
32 devices in a mesh: row: 4 (over y, core), col: 8 (over z, x).
Axes of the slice: x: 2, y: 2, z: 4, core: 2. Of those that a mesh axis runs over, the one named last changes fastest.
Arguments:
- rhs_low: bfloat16 [8192, 512], P(('row', 'col')), may hold values from -6 to 6
- rhs_top: bfloat16 [4096, 512], P('row'), may hold values from -6 to 6
- lower_blocks: bfloat16 [64, 64, 128, 128], P('row', 'col'), may hold values from -0.046875 to 0.046875
- upper_blocks: bfloat16 [64, 64, 128, 128], P('row', 'col'), may hold values from -0.0625 to 0.0625
- block_target: int32 [64, 64], P('row', 'col'), may hold values from 0 to 7
- inv_lower_low: bfloat16 [64, 128, 128], P(('row', 'col')), as said below
- inv_upper_low: bfloat16 [64, 128, 128], P(('row', 'col')), as said below
- inv_lower_top: bfloat16 [32, 128, 128], P('row'), as said below
- inv_upper_top: bfloat16 [32, 128, 128], P('row'), as said below
Outputs:
- sol_low: bfloat16 [8192, 512], P(('row', 'col'))
- sol_top: bfloat16 [4096, 512], P(('row', 'col'))
Inputs may be any that keep to these rules, and one draw needn't show every extreme that they name: `inv_lower_low`: lower triangular with nonzero diagonal. `inv_upper_low`: upper triangular with nonzero diagonal. `inv_lower_top`: lower triangular with nonzero diagonal. `inv_upper_top`: upper triangular with nonzero diagonal.
All inputs are finite; a program needn't handle non-finite values.
Results may differ from a plain program's by a relative error of at most 0.024.
Values may be sent and summed in bfloat16 or wider, within the bound.
No kernel may reach another device: no remote copies, remote signals or barrier semaphores. Data moves between devices by JAX's collectives and lax.ppermute only.
A program may use at most 128 MiB of HBM per device.

v0:
```python
import jax
import jax.numpy as jnp
from jax import lax
from jax.sharding import PartitionSpec as P


def body(
    rhs_low,
    rhs_top,
    lower_blocks,
    upper_blocks,
    block_target,
    inv_lower_low,
    inv_upper_low,
    inv_lower_top,
    inv_upper_top,
):
    width = inv_lower_low.shape[1]
    own_low = inv_lower_low.shape[0]
    rhs_count = rhs_low.shape[1]
    top_count = inv_lower_top.shape[0]
    own_top = top_count // lax.axis_size("col")
    rhs_blocks = rhs_low.reshape(own_low, width, rhs_count)
    fwd_low = jnp.einsum(
        "kab,kbj->kaj", inv_lower_low, rhs_blocks, preferred_element_type=jnp.float32
    ).astype(jnp.bfloat16)
    empty = jnp.zeros((top_count, width, rhs_count), jnp.float32)
    piece = lax.all_gather(fwd_low, "row", axis=0, tiled=True)
    blocks = lower_blocks
    targets = block_target

    def add_step(acc, item):
        blk, tgt = item
        prod = jnp.einsum("kab,kbj->kaj", blk, piece, preferred_element_type=jnp.float32)
        return (acc.at[tgt].add(prod), None)

    result, _ = lax.scan(add_step, empty, (blocks, targets))
    partial_top = result
    rhs_blocks_top = rhs_top.reshape(top_count, width, rhs_count)
    place = lax.axis_index("col") * own_top
    lsum = lax.psum_scatter(
        partial_top.astype(jnp.bfloat16), "col", scatter_dimension=0, tiled=True
    ).astype(jnp.float32)
    own_rhs = lax.dynamic_slice_in_dim(rhs_blocks_top, place, own_top, 0)
    own_lower = lax.dynamic_slice_in_dim(inv_lower_top, place, own_top, 0)
    own_upper = lax.dynamic_slice_in_dim(inv_upper_top, place, own_top, 0)
    resid_top = (own_rhs.astype(jnp.float32) - lsum).astype(jnp.bfloat16)
    fwd_top = jnp.einsum(
        "kab,kbj->kaj", own_lower, resid_top, preferred_element_type=jnp.float32
    ).astype(jnp.bfloat16)
    sol_top = jnp.einsum(
        "kab,kbj->kaj", own_upper, fwd_top, preferred_element_type=jnp.float32
    ).astype(jnp.bfloat16)
    solved_row = lax.all_gather(sol_top, "col", axis=0, tiled=True)
    blocks = upper_blocks
    targets = block_target

    def upper_step(acc, item):
        blk, tgt = item
        picked = jnp.take(solved_row, tgt, axis=0)
        return (
            acc + jnp.einsum("kab,kbj->kaj", blk, picked, preferred_element_type=jnp.float32),
            None,
        )

    begin = jnp.zeros((lax.axis_size("row") * own_low, width, rhs_count), jnp.float32)
    result, _ = lax.scan(upper_step, begin, (blocks, targets))
    usum = lax.psum_scatter(
        result.astype(jnp.bfloat16), "row", scatter_dimension=0, tiled=True
    ).astype(jnp.float32)
    resid_low = (fwd_low.astype(jnp.float32) - usum).astype(jnp.bfloat16)
    sol_low = jnp.einsum(
        "kab,kbj->kaj", inv_upper_low, resid_low, preferred_element_type=jnp.float32
    ).astype(jnp.bfloat16)
    return (
        sol_low.reshape(own_low * width, rhs_count),
        sol_top.reshape(own_top * width, rhs_count),
    )


def solution(mesh):
    placed = (
        P(("row", "col"), None),
        P("row", None),
        P("row", "col", None, None),
        P("row", "col", None, None),
        P("row", "col"),
        P(("row", "col"), None, None),
        P(("row", "col"), None, None),
        P("row", None, None),
        P("row", None, None),
    )
    return jax.shard_map(
        body,
        mesh=mesh,
        in_specs=placed,
        out_specs=(P(("row", "col"), None), P(("row", "col"), None)),
        check_vma=False,
    )
```

profile of v0, /device:TPU:0, one launch (start us, length us, event | category | flops | bytes accessed | tf_op | source)
XLA Modules:
  0.0 321.7 jit_solution(15269043530853626718)
XLA Ops:
  10.7 18.9 %all-gather.4.cloned.1.call-done = bf16[8,128,512]{2,1,0:T(8,128)(2,1)} async-done(((bf16[2,128,512]{2,1,0:T(8,128)(2,1)}), bf16[8,128,512]{2,1,0:T(8,128)(2,1)}) %all-gather.4.cloned.1.call-update) | async-done | bytes 1048592 | tf_op jit(solution)/shard_map/all_gather | solution.py:28
  31.2 89.0 %while.21 = (s32[]{:T(128)}, f32[8,128,512]{2,1,0:T(8,128)}, s32[16,8]{1,0:T(8,128)S(1)}, bf16[16,8,128,128]{3,2,1,0:T(8,128)(2,1)}, bf16[8,128,512]{2,1,0:T(8,128)(2,1)S(1)}, /*index=5*/s32[]{:T(128)}) while((s32[]{:T(128)}, f32[8,128,512]{2,1,0:T(8,128)}, s32[16,8]{1,0:T(8,128)S(1)}, bf16[16,8,128,128]{3,2,1,0:T(8,128)(2,1)}, ...), condition=%wide.region_2.3_spmd, body=%wide.region_0.2_spmd.sunk | while | flops 134742048 | bytes 9700009 | solution.py:37
  32.6 4.2 %scatter_fusion = f32[8,128,512]{2,1,0:T(8,128)} fusion(f32[8,128,512]{2,1,0:T(8,128)} %get-tuple-element.185, s32[8]{0:T(128)S(1)} %fusion.39, f32[8,128,512]{2,1,0:T(8,128)S(1)} %fusion.40), kind=kCustom, calls=%fused_computation.1.clone.1 | custom fusion | flops 524288 | bytes 6291488 | tf_op jit(solution)/shard_map/while/body/eval_jaxpr/scatter-add | solution.py:35
  38.2 4.1 %scatter_fusion = f32[8,128,512]{2,1,0:T(8,128)} fusion(f32[8,128,512]{2,1,0:T(8,128)} %get-tuple-element.185, s32[8]{0:T(128)S(1)} %fusion.39, f32[8,128,512]{2,1,0:T(8,128)S(1)} %fusion.40), kind=kCustom, calls=%fused_computation.1.clone.1 | custom fusion | flops 524288 | bytes 6291488 | tf_op jit(solution)/shard_map/while/body/eval_jaxpr/scatter-add | solution.py:35
  43.7 4.2 %scatter_fusion = f32[8,128,512]{2,1,0:T(8,128)} fusion(f32[8,128,512]{2,1,0:T(8,128)} %get-tuple-element.185, s32[8]{0:T(128)S(1)} %fusion.39, f32[8,128,512]{2,1,0:T(8,128)S(1)} %fusion.40), kind=kCustom, calls=%fused_computation.1.clone.1 | custom fusion | flops 524288 | bytes 6291488 | tf_op jit(solution)/shard_map/while/body/eval_jaxpr/scatter-add | solution.py:35
  49.3 4.2 %scatter_fusion = f32[8,128,512]{2,1,0:T(8,128)} fusion(f32[8,128,512]{2,1,0:T(8,128)} %get-tuple-element.185, s32[8]{0:T(128)S(1)} %fusion.39, f32[8,128,512]{2,1,0:T(8,128)S(1)} %fusion.40), kind=kCustom, calls=%fused_computation.1.clone.1 | custom fusion | flops 524288 | bytes 6291488 | tf_op jit(solution)/shard_map/while/body/eval_jaxpr/scatter-add | solution.py:35
  54.9 4.2 %scatter_fusion = f32[8,128,512]{2,1,0:T(8,128)} fusion(f32[8,128,512]{2,1,0:T(8,128)} %get-tuple-element.185, s32[8]{0:T(128)S(1)} %fusion.39, f32[8,128,512]{2,1,0:T(8,128)S(1)} %fusion.40), kind=kCustom, calls=%fused_computation.1.clone.1 | custom fusion | flops 524288 | bytes 6291488 | tf_op jit(solution)/shard_map/while/body/eval_jaxpr/scatter-add | solution.py:35
  60.5 4.1 %scatter_fusion = f32[8,128,512]{2,1,0:T(8,128)} fusion(f32[8,128,512]{2,1,0:T(8,128)} %get-tuple-element.185, s32[8]{0:T(128)S(1)} %fusion.39, f32[8,128,512]{2,1,0:T(8,128)S(1)} %fusion.40), kind=kCustom, calls=%fused_computation.1.clone.1 | custom fusion | flops 524288 | bytes 6291488 | tf_op jit(solution)/shard_map/while/body/eval_jaxpr/scatter-add | solution.py:35
  66.1 4.2 %scatter_fusion = f32[8,128,512]{2,1,0:T(8,128)} fusion(f32[8,128,512]{2,1,0:T(8,128)} %get-tuple-element.185, s32[8]{0:T(128)S(1)} %fusion.39, f32[8,128,512]{2,1,0:T(8,128)S(1)} %fusion.40), kind=kCustom, calls=%fused_computation.1.clone.1 | custom fusion | flops 524288 | bytes 6291488 | tf_op jit(solution)/shard_map/while/body/eval_jaxpr/scatter-add | solution.py:35
  71.6 4.1 %scatter_fusion = f32[8,128,512]{2,1,0:T(8,128)} fusion(f32[8,128,512]{2,1,0:T(8,128)} %get-tuple-element.185, s32[8]{0:T(128)S(1)} %fusion.39, f32[8,128,512]{2,1,0:T(8,128)S(1)} %fusion.40), kind=kCustom, calls=%fused_computation.1.clone.1 | custom fusion | flops 524288 | bytes 6291488 | tf_op jit(solution)/shard_map/while/body/eval_jaxpr/scatter-add | solution.py:35
  77.1 4.2 %scatter_fusion = f32[8,128,512]{2,1,0:T(8,128)} fusion(f32[8,128,512]{2,1,0:T(8,128)} %get-tuple-element.185, s32[8]{0:T(128)S(1)} %fusion.39, f32[8,128,512]{2,1,0:T(8,128)S(1)} %fusion.40), kind=kCustom, calls=%fused_computation.1.clone.1 | custom fusion | flops 524288 | bytes 6291488 | tf_op jit(solution)/shard_map/while/body/eval_jaxpr/scatter-add | solution.py:35
  82.7 4.1 %scatter_fusion = f32[8,128,512]{2,1,0:T(8,128)} fusion(f32[8,128,512]{2,1,0:T(8,128)} %get-tuple-element.185, s32[8]{0:T(128)S(1)} %fusion.39, f32[8,128,512]{2,1,0:T(8,128)S(1)} %fusion.40), kind=kCustom, calls=%fused_computation.1.clone.1 | custom fusion | flops 524288 | bytes 6291488 | tf_op jit(solution)/shard_map/while/body/eval_jaxpr/scatter-add | solution.py:35
  88.2 4.1 %scatter_fusion = f32[8,128,512]{2,1,0:T(8,128)} fusion(f32[8,128,512]{2,1,0:T(8,128)} %get-tuple-element.185, s32[8]{0:T(128)S(1)} %fusion.39, f32[8,128,512]{2,1,0:T(8,128)S(1)} %fusion.40), kind=kCustom, calls=%fused_computation.1.clone.1 | custom fusion | flops 524288 | bytes 6291488 | tf_op jit(solution)/shard_map/while/body/eval_jaxpr/scatter-add | solution.py:35
  93.7 4.2 %scatter_fusion = f32[8,128,512]{2,1,0:T(8,128)} fusion(f32[8,128,512]{2,1,0:T(8,128)} %get-tuple-element.185, s32[8]{0:T(128)S(1)} %fusion.39, f32[8,128,512]{2,1,0:T(8,128)S(1)} %fusion.40), kind=kCustom, calls=%fused_computation.1.clone.1 | custom fusion | flops 524288 | bytes 6291488 | tf_op jit(solution)/shard_map/while/body/eval_jaxpr/scatter-add | solution.py:35
  99.3 4.2 %scatter_fusion = f32[8,128,512]{2,1,0:T(8,128)} fusion(f32[8,128,512]{2,1,0:T(8,128)} %get-tuple-element.185, s32[8]{0:T(128)S(1)} %fusion.39, f32[8,128,512]{2,1,0:T(8,128)S(1)} %fusion.40), kind=kCustom, calls=%fused_computation.1.clone.1 | custom fusion | flops 524288 | bytes 6291488 | tf_op jit(solution)/shard_map/while/body/eval_jaxpr/scatter-add | solution.py:35
  104.9 4.3 %scatter_fusion = f32[8,128,512]{2,1,0:T(8,128)} fusion(f32[8,128,512]{2,1,0:T(8,128)} %get-tuple-element.185, s32[8]{0:T(128)S(1)} %fusion.39, f32[8,128,512]{2,1,0:T(8,128)S(1)} %fusion.40), kind=kCustom, calls=%fused_computation.1.clone.1 | custom fusion | flops 524288 | bytes 6291488 | tf_op jit(solution)/shard_map/while/body/eval_jaxpr/scatter-add | solution.py:35
  110.6 4.2 %scatter_fusion = f32[8,128,512]{2,1,0:T(8,128)} fusion(f32[8,128,512]{2,1,0:T(8,128)} %get-tuple-element.185, s32[8]{0:T(128)S(1)} %fusion.39, f32[8,128,512]{2,1,0:T(8,128)S(1)} %fusion.40), kind=kCustom, calls=%fused_computation.1.clone.1 | custom fusion | flops 524288 | bytes 6291488 | tf_op jit(solution)/shard_map/while/body/eval_jaxpr/scatter-add | solution.py:35
  116.2 4.0 %scatter_fusion = f32[8,128,512]{2,1,0:T(8,128)} fusion(f32[8,128,512]{2,1,0:T(8,128)} %get-tuple-element.185, s32[8]{0:T(128)S(1)} %fusion.39, f32[8,128,512]{2,1,0:T(8,128)S(1)} %fusion.40), kind=kCustom, calls=%fused_computation.1.clone.1 | custom fusion | flops 524288 | bytes 6291488 | tf_op jit(solution)/shard_map/while/body/eval_jaxpr/scatter-add | solution.py:35
  120.2 2.7 convert_element_type.46
  123.0 63.9 %reduce-scatter.3.cloned.1.call-done = bf16[1,128,512]{2,1,0:T(8,128)(2,1)} async-done(((bf16[8,128,512]{2,1,0:T(8,128)(2,1)}), bf16[1,128,512]{2,1,0:T(8,128)(2,1)}) %reduce-scatter.3.cloned.1.call-update) | async-done | bytes 131088 | tf_op jit(solution)/shard_map/reduce_scatter | solution.py:41
  186.8 2.0 convolution_convert_fusion.2
  188.9 40.0 %all-gather.6.cloned.1.call-done = bf16[1024,512]{1,0:T(8,128)(2,1)} async-done(((bf16[128,512]{1,0:T(8,128)(2,1)}), bf16[1024,512]{1,0:T(8,128)(2,1)}) %all-gather.6.cloned.1.call-update) | async-done | bytes 1048592 | tf_op jit(solution)/shard_map/all_gather | solution.py:54
  229.0 59.3 %while.22 = (s32[]{:T(128)}, f32[8,128,512]{2,1,0:T(8,128)S(1)}, bf16[16,8,128,128]{3,2,1,0:T(8,128)(2,1)}, s32[16,8]{1,0:T(8,128)S(1)}, bf16[8,128,512]{2,1,0:T(8,128)(2,1)}, /*index=5*/s32[]{:T(128)}, s32[]{:T(128)}) while((s32[]{:T(128)}, f32[8,128,512]{2,1,0:T(8,128)S(1)}, bf16[16,8,128,128]{3,2,1,0:T(8,128)(2,1)}, ...), condition=%wide.region_5.6_spmd.clone, body=%wide.region_4.5_spmd.clone.sunk | while | flops 135791696 | bytes 7607055 | solution.py:67
  229.0 1.8 gather_fusion
  230.8 1.8 select_add_fusion.2
  232.7 1.8 gather_fusion
  236.4 1.8 gather_fusion
  240.1 1.8 gather_fusion
  242.0 1.8 select_add_fusion.2
  243.8 1.8 gather_fusion
  245.7 1.8 select_add_fusion.2
  247.5 1.8 gather_fusion
  251.2 1.8 gather_fusion
  253.1 1.8 select_add_fusion.2
  254.9 1.8 gather_fusion
  258.6 1.8 gather_fusion
  262.3 1.8 gather_fusion
  264.2 1.8 select_add_fusion.2
  266.1 1.8 gather_fusion
  269.8 1.8 gather_fusion
  273.5 1.8 gather_fusion
  275.3 1.8 select_add_fusion.2
  277.2 1.8 gather_fusion
  280.9 1.8 gather_fusion
  284.6 1.8 gather_fusion
  286.5 1.8 select_add_fusion.2
  289.4 23.8 %reduce-scatter.5.cloned.1.call-done = bf16[2,128,512]{2,1,0:T(8,128)(2,1)} async-done(((bf16[8,128,512]{2,1,0:T(8,128)(2,1)}), bf16[2,128,512]{2,1,0:T(8,128)(2,1)}) %reduce-scatter.5.cloned.1.call-update) | async-done | bytes 262160 | tf_op jit(solution)/shard_map/reduce_scatter | solution.py:68
  313.2 1.9 convolution_convert_fusion
  (110 shorter events, 45.0 us)
Async XLA Ops:
  7.2 1.0 copy-start
  7.2 22.4 %all-gather.4.cloned.1.call-start = ((), (), s32[]{:S(2)}) async-start(), calls=%async_computation.2 | async-start | bytes 1310720 | tf_op jit(solution)/shard_map/all_gather | solution.py:28
  9.9 176.9 %reduce-scatter.3.cloned.1.call-start = ((), (), s32[]{:S(2)}) async-start(), calls=%async_computation.3 | async-start | bytes 1179648 | tf_op jit(solution)/shard_map/reduce_scatter | solution.py:41
  29.6 1.6 copy-start.1
  122.9 106.0 %all-gather.6.cloned.1.call-start = ((), (), s32[]{:S(2)}) async-start(), calls=%async_computation.5 | async-start | bytes 1179648 | tf_op jit(solution)/shard_map/all_gather | solution.py:54
  188.9 124.4 %reduce-scatter.5.cloned.1.call-start = ((), (), s32[]{:S(2)}) async-start(), calls=%async_computation.4 | async-start | bytes 1310720 | tf_op jit(solution)/shard_map/reduce_scatter | solution.py:68
  288.3 25.0 %copy-start.2 = (bf16[2,128,512]{2,1,0:T(8,128)(2,1)S(1)}, bf16[2,128,512]{2,1,0:T(8,128)(2,1)}, u32[]{:S(2)}) copy-start(bf16[2,128,512]{2,1,0:T(8,128)(2,1)} %convolution_convert_fusion.1) | copy-start | bytes 786436
  288.3 25.0 %copy-start.3 = (bf16[2,128,128]{2,1,0:T(8,128)(2,1)S(1)}, bf16[2,128,128]{2,1,0:T(8,128)(2,1)}, u32[]{:S(2)}) copy-start(bf16[2,128,128]{2,1,0:T(8,128)(2,1)} %param.19) | copy-start | bytes 196612
Sparse Core Ops, SparseCore 0:
  10.1 19.4 all-gather.3
  123.0 63.7 reduce-scatter.2
  189.8 39.1 all-gather.5
  289.5 23.6 reduce-scatter.4
where the time goes:
time: 324 us; the launch traced here: 322 us
  waiting for transfers between devices  147 us (45%)
  other arithmetic  71.3 us (22%)
  matrix products  56 us (17%)
  local copies, waits for them, and re-layouts  32.7 us (10%)
  between operations  13.8 us (4%)
    scatter-add x16, other arithmetic, add_step(): return (acc.at[tgt].add(prod), None)  66.8 us
    reduce_scatter x1, waiting for transfers between devices, body(): lax.psum_scatter(partial_top.astype(jnp.bfloat16), 'col', scatter_dimensi...  63.9 us
    all_gather x1, waiting for transfers between devices, body(): solved_row = lax.all_gather(sol_top, 'col', axis=0, tiled=True)  40 us
    gather x16, local copies, waits for them, and re-layouts, upper_step(): picked = jnp.take(solved_row, tgt, axis=0)  29.4 us
    dot_general x16, matrix products, upper_step(): jnp.einsum('kab,kbj->kaj', blk, picked, preferred_element_type=jnp.float32)  28.5 us
    reduce_scatter x1, waiting for transfers between devices, body(): lax.psum_scatter(result.astype(jnp.bfloat16), 'row', scatter_dimension=0,...  23.8 us
    dot_general x16, matrix products, add_step(): jnp.einsum('kab,kbj->kaj', blk, piece, preferred_element_type=jnp.float32)  21.8 us
    all_gather x1, waiting for transfers between devices, body(): piece = lax.all_gather(fwd_low, 'row', axis=0, tiled=True)  18.9 us
  transfers between devices with their start and end apart: 4, of which 4 were waited for; matrix products, arithmetic and copies ran while one was open for 0% of the time, Pallas kernels for 0%

commit v1 on v0

v1 whole, which is shorter than its diff:
```python
import functools

import jax
import jax.numpy as jnp
from jax import lax
from jax.experimental import pallas as pl
from jax.experimental.pallas import tpu as pltpu
from jax.sharding import PartitionSpec as P

BF = jnp.bfloat16
F32 = jnp.float32
CHUNKS = 1
SLOT = {3: 0, 1: 1, 2: 2, 0: 3}
ORDER = (3, 1, 2, 0)
MIB = 1 << 20


def params(mib, **kw):
    return pltpu.CompilerParams(vmem_limit_bytes=mib * MIB, **kw)


def place_of(rel, count):
    low = rel & 3
    slot = jnp.where(low == 0, 3, jnp.where(low == 3, 0, low))
    return slot * (count // 4) + (rel >> 2)


def fwd_kernel(inv_ref, rhs_ref, *outs):
    own, width, _ = inv_ref.shape
    per = rhs_ref.shape[1] // len(outs)
    for j in range(own):
        rows = slice(j * width, (j + 1) * width)
        for i, out in enumerate(outs):
            out[rows, :] = jnp.dot(
                inv_ref[j], rhs_ref[rows, i * per : (i + 1) * per], preferred_element_type=F32
            ).astype(BF)


def solve_fwd(inv, rhs, chunks):
    rows, cols = rhs.shape
    return pl.pallas_call(
        fwd_kernel,
        out_shape=[jax.ShapeDtypeStruct((rows, cols // chunks), BF)] * chunks,
        compiler_params=params(8),
        name="fwd_low",
    )(inv, rhs)


def sum_kernel(lower, rows, tops, own, steps, ids_ref, tgt_ref, blk_ref, out_ref, acc_ref):
    step = pl.program_id(0)
    per, count, width, _ = blk_ref.shape
    me_row, me_col = ids_ref[0], ids_ref[1]

    @pl.when(step == 0)
    def _():
        acc_ref[...] = jnp.zeros(acc_ref.shape, F32)

    for e in range(per):
        for m in range(count):
            rel_top = tgt_ref[m, step * per + e] ^ me_col
            rel_row = (m // own) ^ me_row
            blk = blk_ref[e, m].astype(F32)
            if lower:
                at = pl.multiple_of(place_of(rel_top, tops) * width, width)
                lanes = slice((m % own) * width, (m % own + 1) * width)
                acc_ref[rel_row, pl.ds(at, width), lanes] += blk
            else:
                at = pl.multiple_of((place_of(rel_row, rows) * own + m % own) * width, width)
                acc_ref[rel_top, pl.ds(at, width), :] += blk

    @pl.when(step == steps - 1)
    def _():
        for i in range(out_ref.shape[0]):
            out_ref[i] = acc_ref[i].astype(BF)


def sum_blocks(lower, ids, targets, blocks, rows, tops, own):
    slots, count, width, _ = blocks.shape
    steps = 4
    shape = (rows, tops * width, own * width) if lower else (tops, rows * own * width, width)
    return pl.pallas_call(
        functools.partial(sum_kernel, lower, rows, tops, own, steps),
        grid_spec=pltpu.PrefetchScalarGridSpec(
            num_scalar_prefetch=2,
            grid=(steps,),
            in_specs=[
                pl.BlockSpec((slots // steps, count, width, width), lambda i, a, b: (i, 0, 0, 0)),
            ],
            out_specs=pl.BlockSpec(shape, lambda i, a, b: (0, 0, 0)),
            scratch_shapes=[pltpu.VMEM(shape, F32)],
        ),
        out_shape=jax.ShapeDtypeStruct(shape, BF),
        compiler_params=params(40),
        name="sum_lower" if lower else "sum_upper",
        cost_estimate=pl.CostEstimate(flops=4 * blocks.size, bytes_accessed=3 * blocks.size, transcendentals=0),
    )(ids, targets, blocks)


def lower_kernel(mat_ref, p0, p1, p2, p3, *outs):
    pieces = (p0, p1, p2, p3)
    per = outs[0].shape[0]
    deep = mat_ref.shape[2]
    for i, out in enumerate(outs):
        total = None
        for s in range(mat_ref.shape[0]):
            part = jnp.dot(
                mat_ref[s, i * per : (i + 1) * per, :],
                pieces[s % 4][(s // 4) * deep : (s // 4 + 1) * deep, :],
                preferred_element_type=F32,
            )
            total = part if total is None else total + part
        out[...] = total.astype(BF)


def apply_lower(mat, pieces):
    rows, cols = mat.shape[1], pieces[0].shape[1]
    return pl.pallas_call(
        lower_kernel,
        out_shape=[jax.ShapeDtypeStruct((rows // 4, cols), BF)] * 4,
        compiler_params=params(32),
        name="apply_lower",
        cost_estimate=pl.CostEstimate(
            flops=2 * mat.size * cols, bytes_accessed=2 * mat.size + 4 * rows * cols, transcendentals=0
        ),
    )(mat, *pieces)


def upper_kernel(mat_ref, p0, p1, p2, p3, first, two, zero):
    pieces = (p0, p1, p2, p3)
    rows = mat_ref.shape[1]
    per = rows // 4
    groups = mat_ref.shape[0] // 4
    for i in range(4):
        total = None
        for g in range(4):
            left = jnp.concatenate(
                [mat_ref[g + 4 * h, i * per : (i + 1) * per, :] for h in range(groups)], axis=1
            )
            part = jnp.dot(left, pieces[g][...], preferred_element_type=F32)
            total = part if total is None else total + part
        total = total.astype(BF)
        if i < 2:
            first[i * per : (i + 1) * per, :] = total
        elif i == 2:
            two[...] = total
        else:
            zero[...] = total


def apply_upper(mat, pieces):
    rows, cols = mat.shape[1], pieces[0].shape[1]
    return pl.pallas_call(
        upper_kernel,
        out_shape=[
            jax.ShapeDtypeStruct((rows // 2, cols), BF),
            jax.ShapeDtypeStruct((rows // 4, cols), BF),
            jax.ShapeDtypeStruct((rows // 4, cols), BF),
        ],
        compiler_params=params(32),
        name="apply_upper",
        cost_estimate=pl.CostEstimate(
            flops=2 * mat.size * cols, bytes_accessed=2 * mat.size + 4 * rows * cols, transcendentals=0
        ),
    )(mat, *pieces)


def top_kernel(parts, own, aliased, ids_ref, rhs_ref, low_ref, up_ref, *refs):
    terms, out, copy = refs[:parts], refs[-2], refs[-1]
    width = low_ref.shape[1]
    for k in range(own):
        rows = slice(k * width, (k + 1) * width)
        lsum = terms[0][rows, :].astype(F32)
        for term in terms[1:]:
            lsum = lsum + term[rows, :].astype(F32)
        resid = (rhs_ref[rows, :].astype(F32) - lsum).astype(BF)
        fwd = jnp.dot(low_ref[k], resid, preferred_element_type=F32).astype(BF)
        sol = jnp.dot(up_ref[k], fwd, preferred_element_type=F32).astype(BF)
        out[rows, :] = sol
        copy[rows, :] = sol


def solve_top(ids, rhs_top, inv_low, inv_up, terms, into, chunk, chunks):
    tops, width, _ = inv_low.shape
    own, cols = terms[0].shape[0] // width, terms[0].shape[1]
    whole = jax.ShapeDtypeStruct((own * width, cols * chunks), BF)
    more = [] if into is None else [into]
    return pl.pallas_call(
        functools.partial(top_kernel, len(terms), own, bool(more)),
        grid_spec=pltpu.PrefetchScalarGridSpec(
            num_scalar_prefetch=1,
            grid=(1,),
            in_specs=[
                pl.BlockSpec((own * width, cols), lambda i, a: (a[1], chunk)),
                pl.BlockSpec((own, width, width), lambda i, a: (a[1], 0, 0)),
                pl.BlockSpec((own, width, width), lambda i, a: (a[1], 0, 0)),
            ]
            + [pl.BlockSpec((own * width, cols), lambda i, a: (0, 0))] * len(terms)
            + [pl.BlockSpec(memory_space=pl.ANY)] * len(more),
            out_specs=[
                pl.BlockSpec((own * width, cols), lambda i, a: (0, chunk)),
                pl.BlockSpec((own * width, cols), lambda i, a: (0, 0)),
            ],
        ),
        out_shape=[whole, jax.ShapeDtypeStruct((own * width, cols), BF)],
        input_output_aliases={4 + len(terms): 0} if more else {},
        compiler_params=params(8),
        name="solve_top",
    )(ids, rhs_top, inv_low, inv_up, *terms, *more)


def low_kernel(parts, inv_ref, fwd_ref, *refs):
    terms, out = refs[:parts], refs[-1]
    own, width, _ = inv_ref.shape
    for j in range(own):
        rows = slice(j * width, (j + 1) * width)
        usum = terms[0][rows, :].astype(F32)
        for term in terms[1:]:
            usum = usum + term[rows, :].astype(F32)
        resid = (fwd_ref[rows, :].astype(F32) - usum).astype(BF)
        out[rows, :] = jnp.dot(inv_ref[j], resid, preferred_element_type=F32).astype(BF)


def solve_low(inv, fwd, terms, into, chunk, chunks):
    rows, cols = fwd.shape
    more = [] if into is None else [into]
    return pl.pallas_call(
        functools.partial(low_kernel, len(terms)),
        grid=(1,),
        in_specs=[
            pl.BlockSpec(inv.shape, lambda i: (0, 0, 0)),
            pl.BlockSpec((rows, cols), lambda i: (0, 0)),
        ]
        + [pl.BlockSpec((rows, cols), lambda i, at=at: (at, 0)) for _, at in terms]
        + [pl.BlockSpec(memory_space=pl.ANY)] * len(more),
        out_specs=pl.BlockSpec((rows, cols), lambda i: (0, chunk)),
        out_shape=jax.ShapeDtypeStruct((rows, cols * chunks), BF),
        input_output_aliases={2 + len(terms): 0} if more else {},
        compiler_params=params(8),
        name="solve_low",
    )(inv, fwd, *[t for t, _ in terms], *more)


def swap(x, axis, bit):
    size = lax.axis_size(axis)
    return lax.ppermute(x, axis, [(i, i ^ (1 << bit)) for i in range(size)])


def add(*xs):
    total = xs[0].astype(F32)
    for x in xs[1:]:
        total = total + x.astype(F32)
    return total.astype(BF)


def gather(own, axis):
    bits = lax.axis_size(axis).bit_length() - 1
    held = own
    for bit in reversed(range(2, bits)):
        got = swap(held, axis, bit)
        n, w = own.shape
        held = jnp.concatenate([held.reshape(-1, 1, n, w), got.reshape(-1, 1, n, w)], axis=1).reshape(-1, w)
    two = swap(held, axis, 1)
    one = swap(held, axis, 0)
    three = swap(two, axis, 0)
    return held, one, two, three


def odd(x, size):
    return x.reshape(-1, 2, size, x.shape[1])[:, 1].reshape(-1, x.shape[1])


def even(x, size):
    return x.reshape(-1, 2, size, x.shape[1])[:, 0].reshape(-1, x.shape[1])


def scatter_rest(terms, axis, size):
    bits = lax.axis_size(axis).bit_length() - 1
    for bit in range(2, bits):
        got = swap(add(*[odd(t, size) for t in terms]), axis, bit)
        terms = [even(t, size) for t in terms] + [got]
    return terms


def body(
    rhs_low,
    rhs_top,
    lower_blocks,
    upper_blocks,
    block_target,
    inv_lower_low,
    inv_upper_low,
    inv_lower_top,
    inv_upper_top,
):
    own, width, _ = inv_lower_low.shape
    rows, cols = lax.axis_size("row"), lax.axis_size("col")
    tops = inv_lower_top.shape[0]
    own_top = tops // cols
    ids = jnp.stack([lax.axis_index("row"), lax.axis_index("col")]).astype(jnp.int32)
    targets = block_target.T

    fwds = solve_fwd(inv_lower_low, rhs_low, CHUNKS)
    got = [gather(fwd, "row") for fwd in fwds]
    mat_l = sum_blocks(True, ids, targets, lower_blocks, rows, tops, own)
    mat_u = sum_blocks(False, ids, targets, upper_blocks, rows, tops, own)
    sol_top = sol_low = None
    solved = []
    for i in range(CHUNKS):
        three, one, two, zero = apply_lower(mat_l, got[i])
        xa = swap(three, "col", 0)
        xb = swap(one, "col", 0)
        z1 = swap(add(two, xa), "col", 1)
        terms = scatter_rest([zero, xb, z1], "col", own_top * width)
        sol_top, sol = solve_top(ids, rhs_top, inv_lower_top, inv_upper_top, terms, sol_top, i, CHUNKS)
        solved.append(gather(sol, "col"))
    for i in range(CHUNKS):
        first, two, zero = apply_upper(mat_u, solved[i])
        per = two.shape[0]
        core = swap(first, "row", 0)
        yy = swap(add(two, core[:per]), "row", 1)
        if rows == 4:
            terms = [(zero, 0), (core, 1), (yy, 0)]
        else:
            terms = [(t, 0) for t in scatter_rest([zero, core[per:], yy], "row", own * width)]
        sol_low = solve_low(inv_upper_low, fwds[i], terms, sol_low, i, CHUNKS)
    return sol_low, sol_top


def solution(mesh):
    placed = (
        P(("row", "col"), None),
        P("row", None),
        P("row", "col", None, None),
        P("row", "col", None, None),
        P("row", "col"),
        P(("row", "col"), None, None),
        P(("row", "col"), None, None),
        P("row", None, None),
        P("row", None, None),
    )
    return jax.shard_map(
        body,
        mesh=mesh,
        in_specs=placed,
        out_specs=(P(("row", "col"), None), P(("row", "col"), None)),
        check_vma=False,
    )
```

time: 324 us -> 78.1 us (0.24)
  waiting for transfers between devices: 147 us -> 46.5 us
  other arithmetic: 71.3 us -> 0.28 us
  matrix products: 56 us -> 0 us
  local copies, waits for them, and re-layouts: 32.7 us -> 4.72 us
  starting transfers between devices: 0.16 us -> 15.7 us
  between operations: 13.8 us -> 0.8 us
  Pallas kernels: 0 us -> 9.83 us
    reduce_scatter x2 -> x0, waiting for transfers between devices: 87.7 us -> none  [the longest x1 63.9 us: body(): lax.psum_scatter(partial_top.astype(jnp.bfloat16), 'col', scatter_dimensi...]
    scatter-add x16 -> x0, other arithmetic: 66.8 us -> none  [add_step(): return (acc.at[tgt].add(prod), None)]
    all_gather x2 -> x0, waiting for transfers between devices: 58.9 us -> none  [the longest x1 40 us: body(): solved_row = lax.all_gather(sol_top, 'col', axis=0, tiled=True)]
    dot_general x35 -> x0, matrix products: 56 us -> none  [the longest x16 28.5 us: upper_step(): jnp.einsum('kab,kbj->kaj', blk, picked, preferred_element_type=jnp.float32)]
    ppermute x0 -> x13, waiting for transfers between devices: none -> 46.5 us  [swap(): return lax.ppermute(x, axis, [(i, i ^ 1 << bit) for i in range(size)])]
    gather x16 -> x0, local copies, waits for them, and re-layouts: 29.4 us -> none  [upper_step(): picked = jnp.take(solved_row, tgt, axis=0)]
    ppermute x0 -> x13, starting transfers between devices: none -> 15.7 us  [swap(): return lax.ppermute(x, axis, [(i, i ^ 1 << bit) for i in range(size)])]
    pallas_call x0 -> x7, Pallas kernels: none -> 9.83 us  [the longest x2 4.52 us: sum_blocks(): pl.pallas_call(functools.partial(sum_kernel, lower, rows, tops, own, step...]
  transfers between devices with their start and end apart: 4 -> 13, of which waited for: 4 -> 10; matrix products, arithmetic and copies ran while one was open for 0% -> 0% of each run, Pallas kernels for 0% -> 6%
where the time goes in v1:
time: 78.1 us; the launch traced here: 77.8 us
  waiting for transfers between devices  46.5 us (60%)
  starting transfers between devices  15.7 us (20%)
  Pallas kernels  9.83 us (13%)
  local copies, waits for them, and re-layouts  4.72 us (6%)
  between operations  0.8 us (1%)
    ppermute x13, waiting for transfers between devices, swap(): return lax.ppermute(x, axis, [(i, i ^ 1 << bit) for i in range(size)])  46.5 us
    ppermute x13, starting transfers between devices, swap(): return lax.ppermute(x, axis, [(i, i ^ 1 << bit) for i in range(size)])  15.7 us
    unnamed x18, local copies, waits for them, and re-layouts  4.69 us
    pallas_call x2, Pallas kernels, sum_blocks(): pl.pallas_call(functools.partial(sum_kernel, lower, rows, tops, own, step...  4.52 us
    pallas_call x1, Pallas kernels, solve_top(): pl.pallas_call(functools.partial(top_kernel, len(terms), own, bool(more))...  1.6 us
  transfers between devices with their start and end apart: 13, of which 10 were waited for; matrix products, arithmetic and copies ran while one was open for 0% of the time, Pallas kernels for 6%

profile of v1, /device:TPU:0, one launch (start us, length us, event | category | flops | bytes accessed | tf_op | source)
XLA Modules:
  0.0 77.8 jit_solution(6687479210473907779)
XLA Ops:
  0.6 0.0 copy-start.5
  0.6 0.9 %copy-done.5 = bf16[256,512]{1,0:T(8,128)(2,1)S(1)} copy-done((bf16[256,512]{1,0:T(8,128)(2,1)S(1)}, bf16[256,512]{1,0:T(8,128)(2,1)}, u32[]{:S(2)}) %copy-start.5) | copy-done | bytes 262168
  1.6 0.8 %copy-done.6 = bf16[2,128,128]{2,1,0:T(8,128)(2,1)S(1)} copy-done((bf16[2,128,128]{2,1,0:T(8,128)(2,1)S(1)}, bf16[2,128,128]{2,1,0:T(8,128)(2,1)}, u32[]{:S(2)}) %copy-start.6) | copy-done | bytes 65560
  2.4 0.2 fwd_low.1.p0.fwd_ref
  2.6 3.0 %collective-permute-start.1 = (bf16[256,512]{1,0:T(8,128)(2,1)S(1)}, bf16[256,512]{1,0:T(8,128)(2,1)S(1)}, u32[]{:S(2)}, u32[]{:S(2)}) collective-permute-start(bf16[256,512]{1,0:T(8,128)(2,1)S(1)} %fwd_low.1.p0.fwd_ref), channel_id=1, source_target_pairs={{0,16},{8,24},{16,0},{24,8},{1,17},{9,25},{17,1},{25,9},{2,18},{10... | collective-permute-start | bytes 786440 | tf_op jit(solution)/shard_map/ppermute | solution.py:245
  5.7 0.0 collective-permute-start
  5.7 6.3 %collective-permute-done.1.p2 = bf16[256,512]{1,0:T(8,128)(2,1)S(1)} collective-permute-done((bf16[256,512]{1,0:T(8,128)(2,1)S(1)}, bf16[256,512]{1,0:T(8,128)(2,1)S(1)}, u32[]{:S(2)}, u32[]{:S(2)}) %collective-permute-start.1) | collective-permute-done | bytes 262176 | tf_op jit(solution)/shard_map/ppermute | solution.py:245
  12.0 0.0 collective-permute-start.2
  12.0 0.1 pad_add_fusion.ids_ref
  12.1 2.2 %copy-done = bf16[16,8,128,128]{3,2,1,0:T(8,128)(2,1)S(1)} copy-done((bf16[16,8,128,128]{3,2,1,0:T(8,128)(2,1)S(1)}, bf16[16,8,128,128]{3,2,1,0:T(8,128)(2,1)}, u32[]{:S(2)}) %copy-start) | copy-done | bytes 4194328
  14.2 0.7 copy-done.8
  14.9 2.3 %sum_lower.1.mat_ref = bf16[4,1024,256]{2,1,0:T(8,128)(2,1)S(1)} custom-call(s32[2]{0:T(128)S(1)} %pad_add_fusion.ids_ref, s32[8,16]{1,0:T(8,128)S(1)} %bitcast.23, bf16[16,8,128,128]{3,2,1,0:T(8,128)(2,1)S(1)} %copy-done), custom_call_target="tpu_custom_call" | custom-call | flops 8388608 | bytes 6291456 | tf_op jit(solution)/shard_map/sum_lower/pallas_call | solution.py:81
  17.2 0.0 copy-start.2
  17.2 0.0 copy-start.3
  17.2 0.0 copy-start.4
  17.3 0.0 copy-start.1
  17.3 0.0 collective-permute-done.p1
  17.3 0.0 collective-permute-done.2.p3
  17.3 1.2 %apply_lower.1 = (bf16[256,512]{1,0:T(8,128)(2,1)S(1)}, bf16[256,512]{1,0:T(8,128)(2,1)S(1)}, bf16[256,512]{1,0:T(8,128)(2,1)S(1)}, bf16[256,512]{1,0:T(8,128)(2,1)S(1)}) custom-call(bf16[4,1024,256]{2,1,0:T(8,128)(2,1)S(1)} %sum_lower.1.mat_ref, bf16[256,512]{1,0:T(8,128)(2,1)S(1)} %fwd_low.1.p0.fwd_ref, bf16[256,512]{1,0:T(8,128)(2,1)S(1)} %collective-permute-done.p1, ...), custom_call_target="tpu_custom_call" | custom-call | flops 1073741824 | bytes 4194304 | tf_op jit(solution)/shard_map/apply_lower/pallas_call | solution.py:117
  18.5 1.8 %collective-permute-start.4 = (bf16[256,512]{1,0:T(8,128)(2,1)S(1)}, bf16[256,512]{1,0:T(8,128)(2,1)S(1)}, u32[]{:S(2)}, u32[]{:S(2)}) collective-permute-start(bf16[256,512]{1,0:T(8,128)(2,1)S(1)} %get-tuple-element.14), channel_id=1, source_target_pairs={{0,1},{1,0},{2,3},{3,2},{4,5},{5,4},{6,7},{7,6},{8,9},{9,8},{10,11... | collective-permute-start | bytes 786440 | tf_op jit(solution)/shard_map/ppermute | solution.py:245
  20.3 0.3 collective-permute-start.3
  20.6 7.1 %collective-permute-done.4 = bf16[256,512]{1,0:T(8,128)(2,1)S(1)} collective-permute-done((bf16[256,512]{1,0:T(8,128)(2,1)S(1)}, bf16[256,512]{1,0:T(8,128)(2,1)S(1)}, u32[]{:S(2)}, u32[]{:S(2)}) %collective-permute-start.4) | collective-permute-done | bytes 262176 | tf_op jit(solution)/shard_map/ppermute | solution.py:245
  27.7 0.1 add_convert_fusion.1
  27.8 1.9 %collective-permute-start.5 = (bf16[256,512]{1,0:T(8,128)(2,1)S(1)}, bf16[256,512]{1,0:T(8,128)(2,1)S(1)}, u32[]{:S(2)}, u32[]{:S(2)}) collective-permute-start(bf16[256,512]{1,0:T(8,128)(2,1)S(1)} %add_convert_fusion.1), channel_id=1, source_target_pairs={{0,2},{1,3},{2,0},{3,1},{4,6},{5,7},{6,4},{7,5},{8,10},{9,11},{10,... | collective-permute-start | bytes 786440 | tf_op jit(solution)/shard_map/ppermute | solution.py:245
  29.7 3.3 %collective-permute-done.3 = bf16[256,512]{1,0:T(8,128)(2,1)S(1)} collective-permute-done((bf16[256,512]{1,0:T(8,128)(2,1)S(1)}, bf16[256,512]{1,0:T(8,128)(2,1)S(1)}, u32[]{:S(2)}, u32[]{:S(2)}) %collective-permute-start.3) | collective-permute-done | bytes 262176 | tf_op jit(solution)/shard_map/ppermute | solution.py:245
  33.0 2.5 %collective-permute-done.5 = bf16[256,512]{1,0:T(8,128)(2,1)S(1)} collective-permute-done((bf16[256,512]{1,0:T(8,128)(2,1)S(1)}, bf16[256,512]{1,0:T(8,128)(2,1)S(1)}, u32[]{:S(2)}, u32[]{:S(2)}) %collective-permute-start.5) | collective-permute-done | bytes 262176 | tf_op jit(solution)/shard_map/ppermute | solution.py:245
  35.5 0.1 fusion
  35.5 2.8 %collective-permute-start.6 = (bf16[128,512]{1,0:T(8,128)(2,1)S(1)}, bf16[128,512]{1,0:T(8,128)(2,1)S(1)}, u32[]{:S(2)}, u32[]{:S(2)}) collective-permute-start(bf16[128,512]{1,0:T(8,128)(2,1)S(1)} %fusion), channel_id=1, source_target_pairs={{0,4},{1,5},{2,6},{3,7},{4,0},{5,1},{6,2},{7,3},{8,12},{9,13},{10,... | collective-permute-start | bytes 393224 | tf_op jit(solution)/shard_map/ppermute | solution.py:245
  38.3 4.9 %collective-permute-done.6.refs_3_ = bf16[128,512]{1,0:T(8,128)(2,1)S(1)} collective-permute-done((bf16[128,512]{1,0:T(8,128)(2,1)S(1)}, bf16[128,512]{1,0:T(8,128)(2,1)S(1)}, u32[]{:S(2)}, u32[]{:S(2)}) %collective-permute-start.6) | collective-permute-done | bytes 131104 | tf_op jit(solution)/shard_map/ppermute | solution.py:245
  43.2 1.6 %solve_top.1 = (bf16[128,512]{1,0:T(8,128)(2,1)}, bf16[128,512]{1,0:T(8,128)(2,1)S(1)}) custom-call(s32[2]{0:T(128)S(1)} %pad_add_fusion.ids_ref, bf16[1024,512]{1,0:T(8,128)(2,1)S(1)} %copy-done.2, bf16[8,128,128]{2,1,0:T(8,128)(2,1)S(1)} %copy-done.3, bf16[8,128,128]{2,1,0:T(8,128)(2,1)S(1)} %copy-done.4, ...), custom_call_target="tpu_custom_call" | custom-call | tf_op jit(solution)/shard_map/solve_top/pallas_call | solution.py:187
  44.8 1.1 %collective-permute-start.7 = (bf16[128,512]{1,0:T(8,128)(2,1)S(1)}, bf16[128,512]{1,0:T(8,128)(2,1)S(1)}, u32[]{:S(2)}, u32[]{:S(2)}) collective-permute-start(bf16[128,512]{1,0:T(8,128)(2,1)S(1)} %get-tuple-element.15), channel_id=1, source_target_pairs={{0,4},{1,5},{2,6},{3,7},{4,0},{5,1},{6,2},{7,3},{8,12},{9,13},{10,... | collective-permute-start | bytes 393224 | tf_op jit(solution)/shard_map/ppermute | solution.py:245
  45.9 6.3 %collective-permute-done.7 = bf16[128,512]{1,0:T(8,128)(2,1)S(1)} collective-permute-done((bf16[128,512]{1,0:T(8,128)(2,1)S(1)}, bf16[128,512]{1,0:T(8,128)(2,1)S(1)}, u32[]{:S(2)}, u32[]{:S(2)}) %collective-permute-start.7) | collective-permute-done | bytes 131104 | tf_op jit(solution)/shard_map/ppermute | solution.py:245
  52.3 0.0 copy-start.7
  52.3 0.1 collective-permute-start.9
  52.4 1.6 %collective-permute-start.8 = (bf16[256,512]{1,0:T(8,128)(2,1)S(1)}, bf16[256,512]{1,0:T(8,128)(2,1)S(1)}, u32[]{:S(2)}, u32[]{:S(2)}) collective-permute-start(bf16[256,512]{1,0:T(8,128)(2,1)S(1)} %bitcast.18), channel_id=1, source_target_pairs={{0,1},{1,0},{2,3},{3,2},{4,5},{5,4},{6,7},{7,6},{8,9},{9,8},{10,11... | collective-permute-start | bytes 786440 | tf_op jit(solution)/shard_map/ppermute | solution.py:245
  53.9 4.8 %collective-permute-done.9.p2 = bf16[256,512]{1,0:T(8,128)(2,1)S(1)} collective-permute-done((bf16[256,512]{1,0:T(8,128)(2,1)S(1)}, bf16[256,512]{1,0:T(8,128)(2,1)S(1)}, u32[]{:S(2)}, u32[]{:S(2)}) %collective-permute-start.9) | collective-permute-done | bytes 262176 | tf_op jit(solution)/shard_map/ppermute | solution.py:245
  58.7 1.5 %collective-permute-start.10 = (bf16[256,512]{1,0:T(8,128)(2,1)S(1)}, bf16[256,512]{1,0:T(8,128)(2,1)S(1)}, u32[]{:S(2)}, u32[]{:S(2)}) collective-permute-start(bf16[256,512]{1,0:T(8,128)(2,1)S(1)} %collective-permute-done.9.p2), channel_id=1, source_target_pairs={{0,1},{1,0},{2,3},{3,2},{4,5},{5,4},{6,7},{7,6},{8,9},{9,8},{10,11... | collective-permute-start | bytes 786440 | tf_op jit(solution)/shard_map/ppermute | solution.py:245
  60.2 2.2 %sum_upper.1.mat_ref = bf16[8,1024,128]{2,1,0:T(8,128)(2,1)S(1)} custom-call(s32[2]{0:T(128)S(1)} %pad_add_fusion.ids_ref, s32[8,16]{1,0:T(8,128)S(1)} %bitcast.24, bf16[16,8,128,128]{3,2,1,0:T(8,128)(2,1)S(1)} %copy-done.1), custom_call_target="tpu_custom_call" | custom-call | flops 8388608 | bytes 6291456 | tf_op jit(solution)/shard_map/sum_upper/pallas_call | solution.py:81
  62.5 0.0 collective-permute-done.8.p1
  62.5 2.6 %collective-permute-done.10.p3 = bf16[256,512]{1,0:T(8,128)(2,1)S(1)} collective-permute-done((bf16[256,512]{1,0:T(8,128)(2,1)S(1)}, bf16[256,512]{1,0:T(8,128)(2,1)S(1)}, u32[]{:S(2)}, u32[]{:S(2)}) %collective-permute-start.10) | collective-permute-done | bytes 262176 | tf_op jit(solution)/shard_map/ppermute | solution.py:245
  65.1 1.2 %apply_upper.1 = (bf16[512,512]{1,0:T(8,128)(2,1)S(1)}, bf16[256,512]{1,0:T(8,128)(2,1)S(1)}, bf16[256,512]{1,0:T(8,128)(2,1)S(1)}) custom-call(bf16[8,1024,128]{2,1,0:T(8,128)(2,1)S(1)} %sum_upper.1.mat_ref, bf16[256,512]{1,0:T(8,128)(2,1)S(1)} %bitcast.19, bf16[256,512]{1,0:T(8,128)(2,1)S(1)} %collective-permute-done.8.p1, ...), custom_call_target="tpu_custom_call" | custom-call | flops 1073741824 | bytes 4194304 | tf_op jit(solution)/shard_map/apply_upper/pallas_call | solution.py:152
  66.3 0.1 collective-permute-start.11
  66.4 1.9 %collective-permute-done.11.refs_1_ = bf16[512,512]{1,0:T(8,128)(2,1)S(1)} collective-permute-done((bf16[512,512]{1,0:T(8,128)(2,1)S(1)}, bf16[512,512]{1,0:T(8,128)(2,1)S(1)}, u32[]{:S(2)}, u32[]{:S(2)}) %collective-permute-start.11) | collective-permute-done | bytes 524320 | tf_op jit(solution)/shard_map/ppermute | solution.py:245
  68.3 0.1 add_convert_fusion
  68.4 1.6 %collective-permute-start.12 = (bf16[256,512]{1,0:T(8,128)(2,1)S(1)}, bf16[256,512]{1,0:T(8,128)(2,1)S(1)}, u32[]{:S(2)}, u32[]{:S(2)}) collective-permute-start(bf16[256,512]{1,0:T(8,128)(2,1)S(1)} %add_convert_fusion), channel_id=1, source_target_pairs={{0,16},{8,24},{16,0},{24,8},{1,17},{9,25},{17,1},{25,9},{2,18},{10... | collective-permute-start | bytes 786440 | tf_op jit(solution)/shard_map/ppermute | solution.py:245
  70.0 6.8 %collective-permute-done.12.refs_2_ = bf16[256,512]{1,0:T(8,128)(2,1)S(1)} collective-permute-done((bf16[256,512]{1,0:T(8,128)(2,1)S(1)}, bf16[256,512]{1,0:T(8,128)(2,1)S(1)}, u32[]{:S(2)}, u32[]{:S(2)}) %collective-permute-start.12) | collective-permute-done | bytes 262176 | tf_op jit(solution)/shard_map/ppermute | solution.py:245
  76.8 0.0 copy-done.7
  76.8 1.0 %solve_low.1 = bf16[256,512]{1,0:T(8,128)(2,1)} custom-call(bf16[2,128,128]{2,1,0:T(8,128)(2,1)S(1)} %copy-done.7, bf16[256,512]{1,0:T(8,128)(2,1)S(1)} %fwd_low.1.p0.fwd_ref, bf16[256,512]{1,0:T(8,128)(2,1)S(1)} %get-tuple-element.16.refs_0_, bf16[512,512]{1,0:T(8,128)(2,1)S(1)} %collective-permute-done.11.refs_1_, ...), custom_call_target="tpu_custom_call" | custom-call | tf_op jit(solution)/shard_map/solve_low/pallas_call | solution.py:226
  (11 shorter events, 0.1 us)
Async XLA Ops:
  0.6 1.0 %copy-start.5 = (bf16[256,512]{1,0:T(8,128)(2,1)S(1)}, bf16[256,512]{1,0:T(8,128)(2,1)}, u32[]{:S(2)}) copy-start(bf16[256,512]{1,0:T(8,128)(2,1)} %rhs_ref.2) | copy-start | bytes 786436
  1.6 0.8 %copy-start.6 = (bf16[2,128,128]{2,1,0:T(8,128)(2,1)S(1)}, bf16[2,128,128]{2,1,0:T(8,128)(2,1)}, u32[]{:S(2)}) copy-start(bf16[2,128,128]{2,1,0:T(8,128)(2,1)} %inv_ref.2) | copy-start | bytes 196612
  2.6 9.3 %collective-permute-start.1 = (bf16[256,512]{1,0:T(8,128)(2,1)S(1)}, bf16[256,512]{1,0:T(8,128)(2,1)S(1)}, u32[]{:S(2)}, u32[]{:S(2)}) collective-permute-start(bf16[256,512]{1,0:T(8,128)(2,1)S(1)} %fwd_low.1.p0.fwd_ref), channel_id=1, source_target_pairs={{0,16},{8,24},{16,0},{24,8},{1,17},{9,25},{17,1},{25,9},{2,18},{10... | collective-permute-start | bytes 786440 | tf_op jit(solution)/shard_map/ppermute | solution.py:245
  5.7 11.6 %collective-permute-start = (bf16[256,512]{1,0:T(8,128)(2,1)S(1)}, bf16[256,512]{1,0:T(8,128)(2,1)S(1)}, u32[]{:S(2)}, u32[]{:S(2)}) collective-permute-start(bf16[256,512]{1,0:T(8,128)(2,1)S(1)} %fwd_low.1.p0.fwd_ref), channel_id=1, source_target_pairs={{0,8},{8,0},{16,24},{24,16},{1,9},{9,1},{17,25},{25,17},{2,10},{10... | collective-permute-start | bytes 786440 | tf_op jit(solution)/shard_map/ppermute | solution.py:245
  12.0 5.3 %collective-permute-start.2 = (bf16[256,512]{1,0:T(8,128)(2,1)S(1)}, bf16[256,512]{1,0:T(8,128)(2,1)S(1)}, u32[]{:S(2)}, u32[]{:S(2)}) collective-permute-start(bf16[256,512]{1,0:T(8,128)(2,1)S(1)} %collective-permute-done.1.p2), channel_id=1, source_target_pairs={{0,8},{8,0},{16,24},{24,16},{1,9},{9,1},{17,25},{25,17},{2,10},{10... | collective-permute-start | bytes 786440 | tf_op jit(solution)/shard_map/ppermute | solution.py:245
  12.1 2.2 %copy-start = (bf16[16,8,128,128]{3,2,1,0:T(8,128)(2,1)S(1)}, bf16[16,8,128,128]{3,2,1,0:T(8,128)(2,1)}, u32[]{:S(2)}) copy-start(bf16[16,8,128,128]{3,2,1,0:T(8,128)(2,1)} %blk_ref.3) | copy-start | bytes 12582916
  14.2 0.7 copy-start.8
  17.2 26.0 %copy-start.2 = (bf16[1024,512]{1,0:T(8,128)(2,1)S(1)}, bf16[1024,512]{1,0:T(8,128)(2,1)}, u32[]{:S(2)}) copy-start(bf16[1024,512]{1,0:T(8,128)(2,1)} %rhs_ref.3) | copy-start | bytes 3145732
  17.2 26.0 %copy-start.3 = (bf16[8,128,128]{2,1,0:T(8,128)(2,1)S(1)}, bf16[8,128,128]{2,1,0:T(8,128)(2,1)}, u32[]{:S(2)}) copy-start(bf16[8,128,128]{2,1,0:T(8,128)(2,1)} %low_ref.1) | copy-start | bytes 786436
  17.2 26.0 %copy-start.4 = (bf16[8,128,128]{2,1,0:T(8,128)(2,1)S(1)}, bf16[8,128,128]{2,1,0:T(8,128)(2,1)}, u32[]{:S(2)}) copy-start(bf16[8,128,128]{2,1,0:T(8,128)(2,1)} %up_ref.1) | copy-start | bytes 786436
  17.3 43.0 %copy-start.1 = (bf16[16,8,128,128]{3,2,1,0:T(8,128)(2,1)S(1)}, bf16[16,8,128,128]{3,2,1,0:T(8,128)(2,1)}, u32[]{:S(2)}) copy-start(bf16[16,8,128,128]{3,2,1,0:T(8,128)(2,1)} %blk_ref.2) | copy-start | bytes 12582916
  18.5 9.2 %collective-permute-start.4 = (bf16[256,512]{1,0:T(8,128)(2,1)S(1)}, bf16[256,512]{1,0:T(8,128)(2,1)S(1)}, u32[]{:S(2)}, u32[]{:S(2)}) collective-permute-start(bf16[256,512]{1,0:T(8,128)(2,1)S(1)} %get-tuple-element.14), channel_id=1, source_target_pairs={{0,1},{1,0},{2,3},{3,2},{4,5},{5,4},{6,7},{7,6},{8,9},{9,8},{10,11... | collective-permute-start | bytes 786440 | tf_op jit(solution)/shard_map/ppermute | solution.py:245
  20.3 12.6 %collective-permute-start.3 = (bf16[256,512]{1,0:T(8,128)(2,1)S(1)}, bf16[256,512]{1,0:T(8,128)(2,1)S(1)}, u32[]{:S(2)}, u32[]{:S(2)}) collective-permute-start(bf16[256,512]{1,0:T(8,128)(2,1)S(1)} %get-tuple-element.12), channel_id=1, source_target_pairs={{0,1},{1,0},{2,3},{3,2},{4,5},{5,4},{6,7},{7,6},{8,9},{9,8},{10,11... | collective-permute-start | bytes 786440 | tf_op jit(solution)/shard_map/ppermute | solution.py:245
  27.8 7.7 %collective-permute-start.5 = (bf16[256,512]{1,0:T(8,128)(2,1)S(1)}, bf16[256,512]{1,0:T(8,128)(2,1)S(1)}, u32[]{:S(2)}, u32[]{:S(2)}) collective-permute-start(bf16[256,512]{1,0:T(8,128)(2,1)S(1)} %add_convert_fusion.1), channel_id=1, source_target_pairs={{0,2},{1,3},{2,0},{3,1},{4,6},{5,7},{6,4},{7,5},{8,10},{9,11},{10,... | collective-permute-start | bytes 786440 | tf_op jit(solution)/shard_map/ppermute | solution.py:245
  35.5 7.7 %collective-permute-start.6 = (bf16[128,512]{1,0:T(8,128)(2,1)S(1)}, bf16[128,512]{1,0:T(8,128)(2,1)S(1)}, u32[]{:S(2)}, u32[]{:S(2)}) collective-permute-start(bf16[128,512]{1,0:T(8,128)(2,1)S(1)} %fusion), channel_id=1, source_target_pairs={{0,4},{1,5},{2,6},{3,7},{4,0},{5,1},{6,2},{7,3},{8,12},{9,13},{10,... | collective-permute-start | bytes 393224 | tf_op jit(solution)/shard_map/ppermute | solution.py:245
  44.8 7.4 %collective-permute-start.7 = (bf16[128,512]{1,0:T(8,128)(2,1)S(1)}, bf16[128,512]{1,0:T(8,128)(2,1)S(1)}, u32[]{:S(2)}, u32[]{:S(2)}) collective-permute-start(bf16[128,512]{1,0:T(8,128)(2,1)S(1)} %get-tuple-element.15), channel_id=1, source_target_pairs={{0,4},{1,5},{2,6},{3,7},{4,0},{5,1},{6,2},{7,3},{8,12},{9,13},{10,... | collective-permute-start | bytes 393224 | tf_op jit(solution)/shard_map/ppermute | solution.py:245
  52.3 24.5 %copy-start.7 = (bf16[2,128,128]{2,1,0:T(8,128)(2,1)S(1)}, bf16[2,128,128]{2,1,0:T(8,128)(2,1)}, u32[]{:S(2)}) copy-start(bf16[2,128,128]{2,1,0:T(8,128)(2,1)} %inv_ref.3) | copy-start | bytes 196612
  52.3 6.4 %collective-permute-start.9 = (bf16[256,512]{1,0:T(8,128)(2,1)S(1)}, bf16[256,512]{1,0:T(8,128)(2,1)S(1)}, u32[]{:S(2)}, u32[]{:S(2)}) collective-permute-start(bf16[256,512]{1,0:T(8,128)(2,1)S(1)} %bitcast.17), channel_id=1, source_target_pairs={{0,2},{1,3},{2,0},{3,1},{4,6},{5,7},{6,4},{7,5},{8,10},{9,11},{10,... | collective-permute-start | bytes 786440 | tf_op jit(solution)/shard_map/ppermute | solution.py:245
  52.4 10.1 %collective-permute-start.8 = (bf16[256,512]{1,0:T(8,128)(2,1)S(1)}, bf16[256,512]{1,0:T(8,128)(2,1)S(1)}, u32[]{:S(2)}, u32[]{:S(2)}) collective-permute-start(bf16[256,512]{1,0:T(8,128)(2,1)S(1)} %bitcast.18), channel_id=1, source_target_pairs={{0,1},{1,0},{2,3},{3,2},{4,5},{5,4},{6,7},{7,6},{8,9},{9,8},{10,11... | collective-permute-start | bytes 786440 | tf_op jit(solution)/shard_map/ppermute | solution.py:245
  58.7 6.4 %collective-permute-start.10 = (bf16[256,512]{1,0:T(8,128)(2,1)S(1)}, bf16[256,512]{1,0:T(8,128)(2,1)S(1)}, u32[]{:S(2)}, u32[]{:S(2)}) collective-permute-start(bf16[256,512]{1,0:T(8,128)(2,1)S(1)} %collective-permute-done.9.p2), channel_id=1, source_target_pairs={{0,1},{1,0},{2,3},{3,2},{4,5},{5,4},{6,7},{7,6},{8,9},{9,8},{10,11... | collective-permute-start | bytes 786440 | tf_op jit(solution)/shard_map/ppermute | solution.py:245
  66.3 2.0 %collective-permute-start.11 = (bf16[512,512]{1,0:T(8,128)(2,1)S(1)}, bf16[512,512]{1,0:T(8,128)(2,1)S(1)}, u32[]{:S(2)}, u32[]{:S(2)}) collective-permute-start(bf16[512,512]{1,0:T(8,128)(2,1)S(1)} %get-tuple-element.17), channel_id=1, source_target_pairs={{0,8},{8,0},{16,24},{24,16},{1,9},{9,1},{17,25},{25,17},{2,10},{10... | collective-permute-start | bytes 1572872 | tf_op jit(solution)/shard_map/ppermute | solution.py:245
  68.4 8.4 %collective-permute-start.12 = (bf16[256,512]{1,0:T(8,128)(2,1)S(1)}, bf16[256,512]{1,0:T(8,128)(2,1)S(1)}, u32[]{:S(2)}, u32[]{:S(2)}) collective-permute-start(bf16[256,512]{1,0:T(8,128)(2,1)S(1)} %add_convert_fusion), channel_id=1, source_target_pairs={{0,16},{8,24},{16,0},{24,8},{1,17},{9,25},{17,1},{25,9},{2,18},{10... | collective-permute-start | bytes 786440 | tf_op jit(solution)/shard_map/ppermute | solution.py:245

commit v2 on v1

v2 whole, which is shorter than its diff:
```python
import functools

import jax
import jax.numpy as jnp
from jax import lax
from jax.experimental import pallas as pl
from jax.experimental.pallas import tpu as pltpu
from jax.sharding import PartitionSpec as P

BF = jnp.bfloat16
F32 = jnp.float32
CHUNKS = 2
FLIP = 1
MIB = 1 << 20
TINY = pl.CostEstimate(flops=1, bytes_accessed=1, transcendentals=0)


def params(mib, **kw):
    return pltpu.CompilerParams(vmem_limit_bytes=mib * MIB, **kw)


def place_of(low, high, count):
    slot = jnp.where(low == 0, 3, jnp.where(low == 3, 0, low))
    return slot * (count // 4) + high


def fwd_kernel(inv_hbm, rhs_hbm, *refs):
    outs, (inv_ref, rhs_ref, sems) = refs[:-3], refs[-3:]
    wide = rhs_ref.shape[1] // len(outs)
    first = pltpu.make_async_copy(inv_hbm, inv_ref, sems.at[0])
    second = pltpu.make_async_copy(rhs_hbm, rhs_ref, sems.at[1])
    first.start()
    second.start()
    first.wait()
    second.wait()
    own, width, _ = inv_ref.shape
    for i, out in enumerate(outs):
        for j in range(own):
            rows = slice(j * width, (j + 1) * width)
            out[rows, :] = jnp.dot(
                inv_ref[j], rhs_ref[rows, i * wide : (i + 1) * wide], preferred_element_type=F32
            ).astype(BF)


def solve_fwd(inv, rhs):
    return pl.pallas_call(
        fwd_kernel,
        in_specs=[pl.BlockSpec(memory_space=pltpu.HBM)] * 2,
        out_shape=[jax.ShapeDtypeStruct((rhs.shape[0], rhs.shape[1] // CHUNKS), BF)] * CHUNKS,
        scratch_shapes=[pltpu.VMEM(inv.shape, BF), pltpu.VMEM(rhs.shape, BF), pltpu.SemaphoreType.DMA((2,))],
        compiler_params=params(8),
        cost_estimate=TINY,
        name="fwd_low",
    )(inv, rhs)


def sum_kernel(lower, rows, tops, own, ids_ref, tgt_ref, blk_hbm, out_ref, acc_ref, blk_ref, sems):
    steps, per, count, width, _ = blk_ref.shape
    copies = [
        pltpu.make_async_copy(blk_hbm.at[pl.ds(i * per, per)], blk_ref.at[i], sems.at[i]) for i in range(steps)
    ]
    for copy in copies:
        copy.start()
    me_row, me_col = ids_ref[0], ids_ref[1]
    other = (me_row & 1) == 1
    acc_ref[...] = jnp.zeros(acc_ref.shape, F32)
    for i in range(steps):
        copies[i].wait()
        for e in range(per):
            for m in range(count):
                rel = tgt_ref[m, i * per + e] ^ me_col
                low, high = rel & 3, rel >> 2
                low = jnp.where(other & ((low == 1) | (low == 2)), 3 - low, low)
                rel_row = (m // own) ^ me_row
                blk = blk_ref[i, e, m].astype(F32)
                if lower:
                    at = pl.multiple_of(place_of(low, high, tops) * width, width)
                    lanes = slice((m % own) * width, (m % own + 1) * width)
                    acc_ref[rel_row, pl.ds(at, width), lanes] += blk
                else:
                    at = (place_of(rel_row & 3, rel_row >> 2, rows) * own + m % own) * width
                    acc_ref[4 * high + low, pl.ds(pl.multiple_of(at, width), width), :] += blk
    for i in range(out_ref.shape[0]):
        out_ref[i] = acc_ref[i].astype(BF)


def sum_blocks(lower, ids, targets, blocks, rows, tops, own):
    slots, count, width, _ = blocks.shape
    steps = 4
    shape = (rows, tops * width, own * width) if lower else (tops, rows * own * width, width)
    return pl.pallas_call(
        functools.partial(sum_kernel, lower, rows, tops, own),
        in_specs=[
            pl.BlockSpec(memory_space=pltpu.SMEM),
            pl.BlockSpec(memory_space=pltpu.SMEM),
            pl.BlockSpec(memory_space=pltpu.HBM),
        ],
        out_shape=jax.ShapeDtypeStruct(shape, BF),
        scratch_shapes=[
            pltpu.VMEM(shape, F32),
            pltpu.VMEM((steps, slots // steps, count, width, width), BF),
            pltpu.SemaphoreType.DMA((steps,)),
        ],
        compiler_params=params(48),
        cost_estimate=TINY,
        name="sum_lower" if lower else "sum_upper",
    )(ids, targets, blocks)


def pick_kernel(apart, ids_ref, rhs_hbm, low_hbm, up_hbm, rhs_ref, low_ref, up_ref, sems):
    width = low_ref.shape[1]
    copies = []
    for k in range(2):
        at = ids_ref[1] ^ (k * apart)
        for n, (src, dst) in enumerate(
            [
                (rhs_hbm.at[pl.ds(pl.multiple_of(at * width, width), width)], rhs_ref.at[pl.ds(k * width, width)]),
                (low_hbm.at[at], low_ref.at[k]),
                (up_hbm.at[at], up_ref.at[k]),
            ]
        ):
            copies.append(pltpu.make_async_copy(src, dst, sems.at[3 * k + n]))
    for copy in copies:
        copy.start()
    for copy in copies:
        copy.wait()


def pick_top(ids, rhs_top, inv_low, inv_up, apart):
    _, width, _ = inv_low.shape
    return pl.pallas_call(
        functools.partial(pick_kernel, apart),
        in_specs=[pl.BlockSpec(memory_space=pltpu.SMEM)] + [pl.BlockSpec(memory_space=pltpu.HBM)] * 3,
        out_shape=[
            jax.ShapeDtypeStruct((2 * width, rhs_top.shape[1]), BF),
            jax.ShapeDtypeStruct((2, width, width), BF),
            jax.ShapeDtypeStruct((2, width, width), BF),
        ],
        scratch_shapes=[pltpu.SemaphoreType.DMA((6,))],
        compiler_params=params(8),
        cost_estimate=TINY,
        name="pick_top",
    )(ids, rhs_top, inv_low, inv_up)


def put(i, value, flip, first, two, zero):
    per = two.shape[0]
    if i == 0:
        first[:per, :] = value
    elif i == 3:
        zero[...] = value
    elif (i == 1) == (flip == 0):
        first[per:, :] = value
    else:
        two[...] = value


def lower_kernel(flip, mat_ref, p0, p1, p2, p3, first, two, zero):
    pieces = (p0, p1, p2, p3)
    per = two.shape[0]
    deep = mat_ref.shape[2]
    for i in range(4):
        total = None
        for s in range(mat_ref.shape[0]):
            part = jnp.dot(
                mat_ref[s, i * per : (i + 1) * per, :],
                pieces[s % 4][(s // 4) * deep : (s // 4 + 1) * deep, :],
                preferred_element_type=F32,
            )
            total = part if total is None else total + part
        put(i, total.astype(BF), flip, first, two, zero)


def upper_kernel(flip, mat_ref, near_ref, far_ref, first, two, zero):
    half = near_ref.shape[0] // 2
    pieces = [near_ref.at[:half], far_ref.at[:half], near_ref.at[half:], far_ref.at[half:]]
    if flip:
        pieces[1], pieces[2] = pieces[2], pieces[1]
    per = two.shape[0]
    groups = mat_ref.shape[0] // 4
    for i in range(4):
        total = None
        for g in range(4):
            left = jnp.concatenate(
                [mat_ref[g + 4 * h, i * per : (i + 1) * per, :] for h in range(groups)], axis=1
            )
            part = jnp.dot(left, pieces[g][...], preferred_element_type=F32)
            total = part if total is None else total + part
        put(i, total.astype(BF), 0, first, two, zero)


def apply(kernel, mat, pieces, name):
    rows, cols = mat.shape[1], pieces[0].shape[1]
    return pl.pallas_call(
        kernel,
        out_shape=[
            jax.ShapeDtypeStruct((rows // 2, cols), BF),
            jax.ShapeDtypeStruct((rows // 4, cols), BF),
            jax.ShapeDtypeStruct((rows // 4, cols), BF),
        ],
        compiler_params=params(32 if mat.size * 2 > 4 * MIB else 10),
        name=name,
    )(mat, *pieces)


def top_kernel(rhs_ref, low_ref, up_ref, mine_ref, got_ref, *refs):
    out, copy = refs[-2:]
    width = low_ref.shape[1]
    for k in range(2):
        rows, cross = slice(k * width, (k + 1) * width), slice((1 - k) * width, (2 - k) * width)
        lsum = mine_ref[rows, :].astype(F32) + got_ref[cross, :].astype(F32)
        resid = (rhs_ref[rows, :].astype(F32) - lsum).astype(BF)
        fwd = jnp.dot(low_ref[k], resid, preferred_element_type=F32).astype(BF)
        sol = jnp.dot(up_ref[k], fwd, preferred_element_type=F32).astype(BF)
        copy[rows, :] = sol
        if k == 0:
            out[...] = sol


def solve_top(picked, mine, got, into, chunk, chunks):
    rhs, inv_low, inv_up = picked
    rows, cols = mine.shape
    more = [] if into is None else [into]
    return pl.pallas_call(
        top_kernel,
        grid=(1,),
        in_specs=[
            pl.BlockSpec((rows, cols), lambda i: (0, chunk)),
            pl.BlockSpec(inv_low.shape, lambda i: (0, 0, 0)),
            pl.BlockSpec(inv_up.shape, lambda i: (0, 0, 0)),
            pl.BlockSpec((rows, cols), lambda i: (0, 0)),
            pl.BlockSpec((rows, cols), lambda i: (0, 0)),
        ]
        + [pl.BlockSpec(memory_space=pl.ANY)] * len(more),
        out_specs=[
            pl.BlockSpec((rows // 2, cols), lambda i: (0, chunk)),
            pl.BlockSpec((rows, cols), lambda i: (0, 0)),
        ],
        out_shape=[
            jax.ShapeDtypeStruct((rows // 2, cols * chunks), BF),
            jax.ShapeDtypeStruct((rows, cols), BF),
        ],
        input_output_aliases={5: 0} if more else {},
        compiler_params=params(8),
        cost_estimate=TINY,
        name="solve_top",
    )(rhs, inv_low, inv_up, mine, got, *more)


def low_kernel(parts, inv_ref, fwd_ref, *refs):
    terms, out = refs[:parts], refs[-1]
    own, width, _ = inv_ref.shape
    for j in range(own):
        rows = slice(j * width, (j + 1) * width)
        usum = terms[0][rows, :].astype(F32)
        for term in terms[1:]:
            usum = usum + term[rows, :].astype(F32)
        resid = (fwd_ref[rows, :].astype(F32) - usum).astype(BF)
        out[rows, :] = jnp.dot(inv_ref[j], resid, preferred_element_type=F32).astype(BF)


def solve_low(inv, fwd, terms, into, chunk, chunks):
    rows, cols = fwd.shape
    more = [] if into is None else [into]
    return pl.pallas_call(
        functools.partial(low_kernel, len(terms)),
        grid=(1,),
        in_specs=[
            pl.BlockSpec(inv.shape, lambda i: (0, 0, 0)),
            pl.BlockSpec((rows, cols), lambda i: (0, 0)),
        ]
        + [pl.BlockSpec((rows, cols), lambda i, at=at: (at, 0)) for _, at in terms]
        + [pl.BlockSpec(memory_space=pl.ANY)] * len(more),
        out_specs=pl.BlockSpec((rows, cols), lambda i: (0, chunk)),
        out_shape=jax.ShapeDtypeStruct((rows, cols * chunks), BF),
        input_output_aliases={2 + len(terms): 0} if more else {},
        compiler_params=params(8),
        cost_estimate=TINY,
        name="solve_low",
    )(inv, fwd, *[t for t, _ in terms], *more)


def swap(x, axis, bit):
    size = lax.axis_size(axis)
    return lax.ppermute(x, axis, [(i, i ^ (1 << bit)) for i in range(size)])


def cross(x, bit, flip):
    rows, cols = lax.axis_size("row"), lax.axis_size("col")
    pairs = [(r * cols + c, r * cols + (c ^ (1 << (bit ^ flip ^ (r & 1))))) for r in range(rows) for c in range(cols)]
    return lax.ppermute(x, ("row", "col"), pairs)


def add(*xs):
    total = xs[0].astype(F32)
    for x in xs[1:]:
        total = total + x.astype(F32)
    return total.astype(BF)


def weave(x, y, size):
    w = x.shape[1]
    return jnp.concatenate([x.reshape(-1, 1, size, w), y.reshape(-1, 1, size, w)], axis=1).reshape(-1, w)


def odd(x, size):
    return x.reshape(-1, 2, size, x.shape[1])[:, 1].reshape(-1, x.shape[1])


def even(x, size):
    return x.reshape(-1, 2, size, x.shape[1])[:, 0].reshape(-1, x.shape[1])


def after(x, *done):
    return lax.optimization_barrier((x, *done))[0]


def far_row(own):
    held = own
    for bit in reversed(range(2, lax.axis_size("row").bit_length() - 1)):
        held = weave(held, swap(held, "row", bit), own.shape[0])
    return held, swap(held, "row", 1)


def sums_col(terms, size):
    for bit in range(2, lax.axis_size("col").bit_length() - 2):
        new = swap(add(*[odd(t, size) for t in terms]), "col", bit)
        terms = [even(t, size) for t in terms] + [new]
    return add(*terms)


def widen_col(held, size):
    for bit in reversed(range(2, lax.axis_size("col").bit_length() - 2)):
        held = weave(held, swap(held, "col", bit), size)
    return held


def sums_row(zero, core, more, size):
    per = zero.shape[0]
    if per == size:
        return [(zero, 0), (core, 1), (more, 0)]
    terms = [zero, core[per:], more]
    for bit in range(2, lax.axis_size("row").bit_length() - 1):
        new = swap(add(*[odd(t, size) for t in terms]), "row", bit)
        terms = [even(t, size) for t in terms] + [new]
    return [(t, 0) for t in terms]


def body(
    rhs_low,
    rhs_top,
    lower_blocks,
    upper_blocks,
    block_target,
    inv_lower_low,
    inv_upper_low,
    inv_lower_top,
    inv_upper_top,
):
    own, width, _ = inv_lower_low.shape
    rows, cols = lax.axis_size("row"), lax.axis_size("col")
    tops = inv_lower_top.shape[0]
    assert tops == cols and rows >= 4 and cols >= 8
    last = cols.bit_length() - 2
    ids = jnp.stack([lax.axis_index("row"), lax.axis_index("col")]).astype(jnp.int32)
    targets = block_target.T

    fwds = solve_fwd(inv_lower_low, rhs_low)
    near, far = zip(*[far_row(fwd) for fwd in fwds])
    side = [swap(x, "row", 0) for x in near]
    mat_l = sum_blocks(True, ids, targets, lower_blocks, rows, tops, own)
    far_side = [swap(after(x, mat_l), "row", 0) for x in far]
    flips = [i % 2 * FLIP for i in range(CHUNKS)]
    parts = [
        apply(functools.partial(lower_kernel, flip), mat_l, pieces, "apply_lower")
        for flip, pieces in zip(flips, zip(near, side, far, far_side))
    ]
    mat_u = sum_blocks(False, after(ids, parts[-1][0]), targets, upper_blocks, rows, tops, own)
    picked = pick_top(ids, rhs_top, inv_lower_top, inv_upper_top, cols // 2)
    sol_top = sol_low = None
    solved = []
    for i, (flip, (first, two, zero)) in enumerate(zip(flips, parts)):
        got = after(cross(first, 0, flip), mat_u)
        more = cross(add(two, got[: two.shape[0]]), 1, flip)
        mine = sums_col([zero, got[two.shape[0] :], more], width)
        other = swap(mine, "col", last)
        sol_top, both = solve_top(picked, mine, other, sol_top, i, CHUNKS)
        held = widen_col(both, width)
        held = jnp.concatenate([held, cross(held, 1, flip)], axis=0)
        solved.append((held, cross(held, 0, flip)))
    for i, (flip, pieces) in enumerate(zip(flips, solved)):
        first, two, zero = apply(functools.partial(upper_kernel, flip), mat_u, pieces, "apply_upper")
        core = swap(first, "row", 0)
        more = swap(add(two, core[: two.shape[0]]), "row", 1)
        terms = sums_row(zero, core, more, own * width)
        sol_low = solve_low(inv_upper_low, fwds[i], terms, sol_low, i, CHUNKS)
    return sol_low, sol_top


def solution(mesh):
    placed = (
        P(("row", "col"), None),
        P("row", None),
        P("row", "col", None, None),
        P("row", "col", None, None),
        P("row", "col"),
        P(("row", "col"), None, None),
        P(("row", "col"), None, None),
        P("row", None, None),
        P("row", None, None),
    )
    return jax.shard_map(
        body,
        mesh=mesh,
        in_specs=placed,
        out_specs=(P(("row", "col"), None), P(("row", "col"), None)),
        check_vma=False,
    )
```

time: 78.1 us -> 66.1 us (0.85)
  waiting for transfers between devices: 46.5 us -> 27.3 us
  Pallas kernels: 9.83 us -> 14.5 us
  starting transfers between devices: 15.7 us -> 20.3 us
  local copies, waits for them, and re-layouts: 4.72 us -> 2.53 us
    ppermute x13 -> x12, waiting for transfers between devices: 46.5 us -> 14.4 us  [swap(): return lax.ppermute(x, axis, [(i, i ^ 1 << bit) for i in range(size)])]
    ppermute x0 -> x8, waiting for transfers between devices: none -> 12.9 us  [cross(): return lax.ppermute(x, ('row', 'col'), pairs)]
    ppermute x0 -> x8, starting transfers between devices: none -> 10 us  [cross(): return lax.ppermute(x, ('row', 'col'), pairs)]
    ppermute x13 -> x12, starting transfers between devices: 15.7 us -> 10.3 us  [swap(): return lax.ppermute(x, axis, [(i, i ^ 1 << bit) for i in range(size)])]
    pallas_call x6 -> x10, Pallas kernels: 8.82 us -> 12.8 us  [the longest x2 6.57 us: sum_blocks(): pl.pallas_call(functools.partial(sum_kernel, lower, rows, tops, own), in_...]
    unnamed x18 -> x16, local copies, waits for them, and re-layouts: 4.69 us -> 2.51 us
    pallas_call x1 -> x2, Pallas kernels: 1.02 us -> 1.77 us  [solve_low(): pl.pallas_call(functools.partial(low_kernel, len(terms)), grid=(1,), in_s...]
  transfers between devices with their start and end apart: 13 -> 20, of which waited for: 10 -> 10; matrix products, arithmetic and copies ran while one was open for 0% -> 0% of each run, Pallas kernels for 6% -> 20%
where the time goes in v2:
time: 66.1 us; the launch traced here: 65.8 us
  waiting for transfers between devices  27.3 us (41%)
  starting transfers between devices  20.3 us (31%)
  Pallas kernels  14.5 us (22%)
  local copies, waits for them, and re-layouts  2.53 us (4%)
  between operations  0.83 us (1%)
    ppermute x12, waiting for transfers between devices, swap(): return lax.ppermute(x, axis, [(i, i ^ 1 << bit) for i in range(size)])  14.4 us
    ppermute x8, waiting for transfers between devices, cross(): return lax.ppermute(x, ('row', 'col'), pairs)  12.9 us
    ppermute x12, starting transfers between devices, swap(): return lax.ppermute(x, axis, [(i, i ^ 1 << bit) for i in range(size)])  10.3 us
    ppermute x8, starting transfers between devices, cross(): return lax.ppermute(x, ('row', 'col'), pairs)  10 us
    pallas_call x2, Pallas kernels, sum_blocks(): pl.pallas_call(functools.partial(sum_kernel, lower, rows, tops, own), in_...  6.57 us
    pallas_call x4, Pallas kernels, apply(): pl.pallas_call(kernel, out_shape=[jax.ShapeDtypeStruct((rows // 2, cols),...  2.84 us
    unnamed x16, local copies, waits for them, and re-layouts  2.51 us
    pallas_call x2, Pallas kernels, solve_top(): pl.pallas_call(top_kernel, grid=(1,), in_specs=[pl.BlockSpec((rows, cols)...  1.92 us
  transfers between devices with their start and end apart: 20, of which 10 were waited for; matrix products, arithmetic and copies ran while one was open for 0% of the time, Pallas kernels for 20%

profile of v2, /device:TPU:0, one launch (start us, length us, event | category | flops | bytes accessed | tf_op | source)
XLA Modules:
  0.0 65.8 jit_solution(5130558712841485358)
XLA Ops:
  0.6 0.9 %copy-done.1 = bf16[256,512]{1,0:T(8,128)(2,1)S(1)} copy-done((bf16[256,512]{1,0:T(8,128)(2,1)S(1)}, bf16[256,512]{1,0:T(8,128)(2,1)}, u32[]{:S(2)}) %copy-start.1) | copy-done | bytes 262168
  1.6 0.8 %copy-done.5 = bf16[2,128,128]{2,1,0:T(8,128)(2,1)S(1)} copy-done((bf16[2,128,128]{2,1,0:T(8,128)(2,1)S(1)}, bf16[2,128,128]{2,1,0:T(8,128)(2,1)}, u32[]{:S(2)}) %copy-start.5) | copy-done | bytes 65560
  2.4 0.3 fwd_low.1
  2.7 3.0 %collective-permute-start.7 = (bf16[256,256]{1,0:T(8,128)(2,1)S(1)}, bf16[256,256]{1,0:T(8,128)(2,1)S(1)}, u32[]{:S(2)}, u32[]{:S(2)}) collective-permute-start(bf16[256,256]{1,0:T(8,128)(2,1)S(1)} %get-tuple-element.38.p0.fwd_ref), channel_id=1, source_target_pairs={{0,16},{8,24},{16,0},{24,8},{1,17},{9,25},{17,1},{25,9},{2,18},{10... | collective-permute-start | bytes 393224 | tf_op jit(solution)/shard_map/ppermute | solution.py:285
  5.8 0.1 collective-permute-start.1
  5.9 0.5 collective-permute-start.6
  6.4 0.1 pad_add_fusion.ids_ref
  6.4 0.7 %copy-done.6 = s32[16,8]{0,1:T(8,128)S(1)} copy-done((s32[16,8]{0,1:T(8,128)S(1)}, s32[16,8]{0,1:T(8,128)}, u32[]{:S(2)}) %copy-start.6) | copy-done | bytes 536
  7.1 3.3 %sum_lower.1.mat_ref = bf16[4,1024,256]{2,1,0:T(8,128)(2,1)S(1)} custom-call(s32[2]{0:T(128)S(1)} %pad_add_fusion.ids_ref, s32[8,16]{1,0:T(8,128)S(1)} %bitcast.3, bf16[16,8,128,128]{3,2,1,0:T(8,128)(2,1)} %blk_hbm.2), custom_call_target="tpu_custom_call" | custom-call | flops 1 | bytes 1 | tf_op jit(solution)/shard_map/sum_lower/pallas_call | solution.py:91
  10.4 0.1 collective-permute-start.8
  10.5 1.6 %collective-permute-done.1.p2 = bf16[256,256]{1,0:T(8,128)(2,1)S(1)} collective-permute-done((bf16[256,256]{1,0:T(8,128)(2,1)S(1)}, bf16[256,256]{1,0:T(8,128)(2,1)S(1)}, u32[]{:S(2)}, u32[]{:S(2)}) %collective-permute-start.1) | collective-permute-done | bytes 131104 | tf_op jit(solution)/shard_map/ppermute | solution.py:285
  12.1 0.7 %apply_lower.3 = (bf16[512,256]{1,0:T(8,128)(2,1)S(1)}, bf16[256,256]{1,0:T(8,128)(2,1)S(1)}, bf16[256,256]{1,0:T(8,128)(2,1)S(1)}) custom-call(bf16[4,1024,256]{2,1,0:T(8,128)(2,1)S(1)} %sum_lower.1.mat_ref, bf16[256,256]{1,0:T(8,128)(2,1)S(1)} %get-tuple-element.38.p0.fwd_ref, bf16[256,256]{1,0:T(8,128)(2,1)S(1)} %collective-permute-done.6.p1, ...), custom_call_target="tpu_custom_call" | custom-call | tf_op jit(solution)/shard_map/apply_lower/pallas_call | solution.py:194
  12.8 1.8 %collective-permute-start.9 = (bf16[512,256]{1,0:T(8,128)(2,1)S(1)}, bf16[512,256]{1,0:T(8,128)(2,1)S(1)}, u32[]{:S(2)}, u32[]{:S(2)}) collective-permute-start(bf16[512,256]{1,0:T(8,128)(2,1)S(1)} %get-tuple-element.41), channel_id=1, source_target_pairs={{0,1},{1,0},{2,3},{3,2},{4,5},{5,4},{6,7},{7,6},{8,10},{9,11},{10,... | collective-permute-start | bytes 786440 | tf_op jit(solution)/shard_map/ppermute | solution.py:291
  14.6 0.7 %apply_lower.2 = (bf16[512,256]{1,0:T(8,128)(2,1)S(1)}, bf16[256,256]{1,0:T(8,128)(2,1)S(1)}, bf16[256,256]{1,0:T(8,128)(2,1)S(1)}) custom-call(bf16[4,1024,256]{2,1,0:T(8,128)(2,1)S(1)} %sum_lower.1.mat_ref, bf16[256,256]{1,0:T(8,128)(2,1)S(1)} %get-tuple-element.28.p0.fwd_ref, bf16[256,256]{1,0:T(8,128)(2,1)S(1)} %collective-permute-done.p1, ...), custom_call_target="tpu_custom_call" | custom-call | tf_op jit(solution)/shard_map/apply_lower/pallas_call | solution.py:194
  15.3 0.0 copy-start.3
  15.3 1.6 %collective-permute-start.3 = (bf16[512,256]{1,0:T(8,128)(2,1)S(1)}, bf16[512,256]{1,0:T(8,128)(2,1)S(1)}, u32[]{:S(2)}, u32[]{:S(2)}) collective-permute-start(bf16[512,256]{1,0:T(8,128)(2,1)S(1)} %get-tuple-element.30), channel_id=1, source_target_pairs={{0,2},{1,3},{2,0},{3,1},{4,6},{5,7},{6,4},{7,5},{8,9},{9,8},{10,11... | collective-permute-start | bytes 786440 | tf_op jit(solution)/shard_map/ppermute | solution.py:291
  17.0 3.3 %sum_upper.1.mat_ref = bf16[8,1024,128]{2,1,0:T(8,128)(2,1)S(1)} custom-call(s32[2]{0:T(128)S(1)} %pad_add_fusion.ids_ref, s32[8,16]{1,0:T(8,128)S(1)} %bitcast.4, bf16[16,8,128,128]{3,2,1,0:T(8,128)(2,1)} %blk_hbm.3), custom_call_target="tpu_custom_call" | custom-call | flops 1 | bytes 1 | tf_op jit(solution)/shard_map/sum_upper/pallas_call | solution.py:91
  20.3 1.5 %collective-permute-done.3 = bf16[512,256]{1,0:T(8,128)(2,1)S(1)} collective-permute-done((bf16[512,256]{1,0:T(8,128)(2,1)S(1)}, bf16[512,256]{1,0:T(8,128)(2,1)S(1)}, u32[]{:S(2)}, u32[]{:S(2)}) %collective-permute-start.3) | collective-permute-done | bytes 262176 | tf_op jit(solution)/shard_map/ppermute | solution.py:291
  21.8 1.7 %collective-permute-start.10 = (bf16[256,256]{1,0:T(8,128)(2,1)S(1)}, bf16[256,256]{1,0:T(8,128)(2,1)S(1)}, u32[]{:S(2)}, u32[]{:S(2)}) collective-permute-start(bf16[256,256]{1,0:T(8,128)(2,1)S(1)} %add_convert_fusion.3), channel_id=1, source_target_pairs={{0,2},{1,3},{2,0},{3,1},{4,6},{5,7},{6,4},{7,5},{8,9},{9,8},{10,11... | collective-permute-start | bytes 393224 | tf_op jit(solution)/shard_map/ppermute | solution.py:291
  23.5 1.6 %collective-permute-start.4 = (bf16[256,256]{1,0:T(8,128)(2,1)S(1)}, bf16[256,256]{1,0:T(8,128)(2,1)S(1)}, u32[]{:S(2)}, u32[]{:S(2)}) collective-permute-start(bf16[256,256]{1,0:T(8,128)(2,1)S(1)} %add_convert_fusion.5), channel_id=1, source_target_pairs={{0,1},{1,0},{2,3},{3,2},{4,5},{5,4},{6,7},{7,6},{8,10},{9,11},{10,... | collective-permute-start | bytes 393224 | tf_op jit(solution)/shard_map/ppermute | solution.py:291
  25.1 2.6 %collective-permute-done.10 = bf16[256,256]{1,0:T(8,128)(2,1)S(1)} collective-permute-done((bf16[256,256]{1,0:T(8,128)(2,1)S(1)}, bf16[256,256]{1,0:T(8,128)(2,1)S(1)}, u32[]{:S(2)}, u32[]{:S(2)}) %collective-permute-start.10) | collective-permute-done | bytes 131104 | tf_op jit(solution)/shard_map/ppermute | solution.py:291
  27.7 0.1 add_convert_fusion.2.mine_ref
  27.7 2.7 %collective-permute-start.11 = (bf16[256,256]{1,0:T(8,128)(2,1)S(1)}, bf16[256,256]{1,0:T(8,128)(2,1)S(1)}, u32[]{:S(2)}, u32[]{:S(2)}) collective-permute-start(bf16[256,256]{1,0:T(8,128)(2,1)S(1)} %add_convert_fusion.2.mine_ref), channel_id=1, source_target_pairs={{0,4},{1,5},{2,6},{3,7},{4,0},{5,1},{6,2},{7,3},{8,12},{9,13},{10,... | collective-permute-start | bytes 393224 | tf_op jit(solution)/shard_map/ppermute | solution.py:285
  30.4 0.1 add_convert_fusion.4.mine_ref
  30.5 0.8 %collective-permute-start.5 = (bf16[256,256]{1,0:T(8,128)(2,1)S(1)}, bf16[256,256]{1,0:T(8,128)(2,1)S(1)}, u32[]{:S(2)}, u32[]{:S(2)}) collective-permute-start(bf16[256,256]{1,0:T(8,128)(2,1)S(1)} %add_convert_fusion.4.mine_ref), channel_id=1, source_target_pairs={{0,4},{1,5},{2,6},{3,7},{4,0},{5,1},{6,2},{7,3},{8,12},{9,13},{10,... | collective-permute-start | bytes 393224 | tf_op jit(solution)/shard_map/ppermute | solution.py:285
  31.3 1.1 %pick_top.1 = (bf16[256,512]{1,0:T(8,128)(2,1)S(1)}, bf16[2,128,128]{2,1,0:T(8,128)(2,1)S(1)}, bf16[2,128,128]{2,1,0:T(8,128)(2,1)S(1)}) custom-call(s32[2]{0:T(128)S(1)} %pad_add_fusion.ids_ref, bf16[1024,512]{1,0:T(8,128)(2,1)S(1)} %copy-done, bf16[8,128,128]{2,1,0:T(8,128)(2,1)S(1)} %copy-done.2, bf16[8,128,128]{2,1,0:T(8,128)(2,1)S(1)} %copy-done.3), custom_call_target="tpu_custom_call" | custom-call | flops 1 | bytes 1 | tf_op jit(solution)/shard_map/pick_top/pallas_call | solution.py:131
  32.4 7.3 %collective-permute-done.11.got_ref = bf16[256,256]{1,0:T(8,128)(2,1)S(1)} collective-permute-done((bf16[256,256]{1,0:T(8,128)(2,1)S(1)}, bf16[256,256]{1,0:T(8,128)(2,1)S(1)}, u32[]{:S(2)}, u32[]{:S(2)}) %collective-permute-start.11) | collective-permute-done | bytes 131104 | tf_op jit(solution)/shard_map/ppermute | solution.py:285
  39.7 1.0 %solve_top.2 = (bf16[128,512]{1,0:T(8,128)(2,1)}, bf16[256,256]{1,0:T(8,128)(2,1)S(1)}) custom-call(bf16[256,512]{1,0:T(8,128)(2,1)S(1)} %get-tuple-element.32.rhs_ref, bf16[2,128,128]{2,1,0:T(8,128)(2,1)S(1)} %get-tuple-element.33.low_ref, bf16[2,128,128]{2,1,0:T(8,128)(2,1)S(1)} %get-tuple-element.34.up_ref, ...), custom_call_target="tpu_custom_call" | custom-call | flops 1 | bytes 1 | tf_op jit(solution)/shard_map/solve_top/pallas_call | solution.py:224
  40.6 0.2 collective-permute-start.16
  40.8 0.3 collective-permute-done.5.got_ref
  41.1 1.0 %solve_top.3 = (bf16[128,512]{1,0:T(8,128)(2,1)}, bf16[256,256]{1,0:T(8,128)(2,1)S(1)}) custom-call(bf16[256,512]{1,0:T(8,128)(2,1)S(1)} %get-tuple-element.32.rhs_ref, bf16[2,128,128]{2,1,0:T(8,128)(2,1)S(1)} %get-tuple-element.33.low_ref, bf16[2,128,128]{2,1,0:T(8,128)(2,1)S(1)} %get-tuple-element.34.up_ref, ...), custom_call_target="tpu_custom_call", output_to_operand_aliasing={{0}: (5, {})} | custom-call | flops 1 | bytes 1 | tf_op jit(solution)/shard_map/solve_top/pallas_call | solution.py:224
  42.1 1.5 %collective-permute-start.12 = (bf16[256,256]{1,0:T(8,128)(2,1)S(1)}, bf16[256,256]{1,0:T(8,128)(2,1)S(1)}, u32[]{:S(2)}, u32[]{:S(2)}) collective-permute-start(bf16[256,256]{1,0:T(8,128)(2,1)S(1)} %get-tuple-element.45), channel_id=1, source_target_pairs={{0,1},{1,0},{2,3},{3,2},{4,5},{5,4},{6,7},{7,6},{8,10},{9,11},{10,... | collective-permute-start | bytes 393224 | tf_op jit(solution)/shard_map/ppermute | solution.py:291
  43.6 3.4 %collective-permute-done.16 = bf16[256,256]{1,0:T(8,128)(2,1)S(1)} collective-permute-done((bf16[256,256]{1,0:T(8,128)(2,1)S(1)}, bf16[256,256]{1,0:T(8,128)(2,1)S(1)}, u32[]{:S(2)}, u32[]{:S(2)}) %collective-permute-start.16) | collective-permute-done | bytes 131104 | tf_op jit(solution)/shard_map/ppermute | solution.py:291
  47.0 1.5 %collective-permute-start.17 = (bf16[512,256]{1,0:T(8,128)(2,1)S(1)}, bf16[512,256]{1,0:T(8,128)(2,1)S(1)}, u32[]{:S(2)}, u32[]{:S(2)}) collective-permute-start(bf16[512,256]{1,0:T(8,128)(2,1)S(1)} %constant_dynamic-update-slice_fusion.2.near_ref), channel_id=1, source_target_pairs={{0,1},{1,0},{2,3},{3,2},{4,5},{5,4},{6,7},{7,6},{8,10},{9,11},{10,... | collective-permute-start | bytes 786440 | tf_op jit(solution)/shard_map/ppermute | solution.py:291
  48.5 0.2 collective-permute-start.13
  48.7 5.5 %collective-permute-done.17.far_ref = bf16[512,256]{1,0:T(8,128)(2,1)S(1)} collective-permute-done((bf16[512,256]{1,0:T(8,128)(2,1)S(1)}, bf16[512,256]{1,0:T(8,128)(2,1)S(1)}, u32[]{:S(2)}, u32[]{:S(2)}) %collective-permute-start.17) | collective-permute-done | bytes 262176 | tf_op jit(solution)/shard_map/ppermute | solution.py:291
  54.2 0.7 %apply_upper.3 = (bf16[512,256]{1,0:T(8,128)(2,1)S(1)}, bf16[256,256]{1,0:T(8,128)(2,1)S(1)}, bf16[256,256]{1,0:T(8,128)(2,1)S(1)}) custom-call(bf16[8,1024,128]{2,1,0:T(8,128)(2,1)S(1)} %sum_upper.1.mat_ref, bf16[512,256]{1,0:T(8,128)(2,1)S(1)} %constant_dynamic-update-slice_fusion.2.near_ref, bf16[512,256]{1,0:T(8,128)(2,1)S(1)} %collective-permute-done.17.far_ref), custom_call_target="tpu_custom_call" | custom-call | tf_op jit(solution)/shard_map/apply_upper/pallas_call | solution.py:194
  54.9 0.1 collective-permute-start.18
  55.0 0.0 collective-permute-done.13.far_ref
  55.0 0.7 %apply_upper.2 = (bf16[512,256]{1,0:T(8,128)(2,1)S(1)}, bf16[256,256]{1,0:T(8,128)(2,1)S(1)}, bf16[256,256]{1,0:T(8,128)(2,1)S(1)}) custom-call(bf16[8,1024,128]{2,1,0:T(8,128)(2,1)S(1)} %sum_upper.1.mat_ref, bf16[512,256]{1,0:T(8,128)(2,1)S(1)} %constant_dynamic-update-slice_fusion.near_ref, bf16[512,256]{1,0:T(8,128)(2,1)S(1)} %collective-permute-done.13.far_ref), custom_call_target="tpu_custom_call" | custom-call | tf_op jit(solution)/shard_map/apply_upper/pallas_call | solution.py:194
  55.7 0.6 collective-permute-start.14
  56.2 0.2 collective-permute-done.18.refs_1_
  56.5 1.6 %collective-permute-start.19 = (bf16[256,256]{1,0:T(8,128)(2,1)S(1)}, bf16[256,256]{1,0:T(8,128)(2,1)S(1)}, u32[]{:S(2)}, u32[]{:S(2)}) collective-permute-start(bf16[256,256]{1,0:T(8,128)(2,1)S(1)} %add_convert_fusion), channel_id=1, source_target_pairs={{0,16},{8,24},{16,0},{24,8},{1,17},{9,25},{17,1},{25,9},{2,18},{10... | collective-permute-start | bytes 393224 | tf_op jit(solution)/shard_map/ppermute | solution.py:285
  58.1 0.9 %collective-permute-start.15 = (bf16[256,256]{1,0:T(8,128)(2,1)S(1)}, bf16[256,256]{1,0:T(8,128)(2,1)S(1)}, u32[]{:S(2)}, u32[]{:S(2)}) collective-permute-start(bf16[256,256]{1,0:T(8,128)(2,1)S(1)} %add_convert_fusion.1), channel_id=1, source_target_pairs={{0,16},{8,24},{16,0},{24,8},{1,17},{9,25},{17,1},{25,9},{2,18},{10... | collective-permute-start | bytes 393224 | tf_op jit(solution)/shard_map/ppermute | solution.py:285
  59.0 3.9 %collective-permute-done.19.refs_2_ = bf16[256,256]{1,0:T(8,128)(2,1)S(1)} collective-permute-done((bf16[256,256]{1,0:T(8,128)(2,1)S(1)}, bf16[256,256]{1,0:T(8,128)(2,1)S(1)}, u32[]{:S(2)}, u32[]{:S(2)}) %collective-permute-start.19) | collective-permute-done | bytes 131104 | tf_op jit(solution)/shard_map/ppermute | solution.py:285
  62.9 0.9 %solve_low.2.refs_3_ = bf16[256,512]{1,0:T(8,128)(2,1)} custom-call(bf16[2,128,128]{2,1,0:T(8,128)(2,1)S(1)} %copy-done.4, bf16[256,256]{1,0:T(8,128)(2,1)S(1)} %get-tuple-element.38.p0.fwd_ref, bf16[256,256]{1,0:T(8,128)(2,1)S(1)} %get-tuple-element.50.refs_0_, bf16[512,256]{1,0:T(8,128)(2,1)S(1)} %collective-permute-done.18.refs_1_, ...), custom_call_target="tpu_custom_call" | custom-call | flops 1 | bytes 1 | tf_op jit(solution)/shard_map/solve_low/pallas_call | solution.py:265
  63.8 1.1 %collective-permute-done.15.refs_2_ = bf16[256,256]{1,0:T(8,128)(2,1)S(1)} collective-permute-done((bf16[256,256]{1,0:T(8,128)(2,1)S(1)}, bf16[256,256]{1,0:T(8,128)(2,1)S(1)}, u32[]{:S(2)}, u32[]{:S(2)}) %collective-permute-start.15) | collective-permute-done | bytes 131104 | tf_op jit(solution)/shard_map/ppermute | solution.py:285
  64.9 0.9 %solve_low.3 = bf16[256,512]{1,0:T(8,128)(2,1)} custom-call(bf16[2,128,128]{2,1,0:T(8,128)(2,1)S(1)} %copy-done.4, bf16[256,256]{1,0:T(8,128)(2,1)S(1)} %get-tuple-element.28.p0.fwd_ref, bf16[256,256]{1,0:T(8,128)(2,1)S(1)} %get-tuple-element.46.refs_0_, bf16[512,256]{1,0:T(8,128)(2,1)S(1)} %collective-permute-done.14.refs_1_, ...), custom_call_target="tpu_custom_call", output_to_operand_aliasing={{}: (5, {})} | custom-call | flops 1 | bytes 1 | tf_op jit(solution)/shard_map/solve_low/pallas_call | solution.py:265
  (29 shorter events, 0.2 us)
Async XLA Ops:
  0.6 1.0 %copy-start.1 = (bf16[256,512]{1,0:T(8,128)(2,1)S(1)}, bf16[256,512]{1,0:T(8,128)(2,1)}, u32[]{:S(2)}) copy-start(bf16[256,512]{1,0:T(8,128)(2,1)} %rhs_hbm.2) | copy-start | bytes 786436
  1.6 0.8 %copy-start.5 = (bf16[2,128,128]{2,1,0:T(8,128)(2,1)S(1)}, bf16[2,128,128]{2,1,0:T(8,128)(2,1)}, u32[]{:S(2)}) copy-start(bf16[2,128,128]{2,1,0:T(8,128)(2,1)} %inv_hbm.1) | copy-start | bytes 196612
  2.7 7.7 %collective-permute-start.7 = (bf16[256,256]{1,0:T(8,128)(2,1)S(1)}, bf16[256,256]{1,0:T(8,128)(2,1)S(1)}, u32[]{:S(2)}, u32[]{:S(2)}) collective-permute-start(bf16[256,256]{1,0:T(8,128)(2,1)S(1)} %get-tuple-element.38.p0.fwd_ref), channel_id=1, source_target_pairs={{0,16},{8,24},{16,0},{24,8},{1,17},{9,25},{17,1},{25,9},{2,18},{10... | collective-permute-start | bytes 393224 | tf_op jit(solution)/shard_map/ppermute | solution.py:285
  5.8 6.3 %collective-permute-start.1 = (bf16[256,256]{1,0:T(8,128)(2,1)S(1)}, bf16[256,256]{1,0:T(8,128)(2,1)S(1)}, u32[]{:S(2)}, u32[]{:S(2)}) collective-permute-start(bf16[256,256]{1,0:T(8,128)(2,1)S(1)} %get-tuple-element.28.p0.fwd_ref), channel_id=1, source_target_pairs={{0,16},{8,24},{16,0},{24,8},{1,17},{9,25},{17,1},{25,9},{2,18},{10... | collective-permute-start | bytes 393224 | tf_op jit(solution)/shard_map/ppermute | solution.py:285
  5.8 8.7 %collective-permute-start = (bf16[256,256]{1,0:T(8,128)(2,1)S(1)}, bf16[256,256]{1,0:T(8,128)(2,1)S(1)}, u32[]{:S(2)}, u32[]{:S(2)}) collective-permute-start(bf16[256,256]{1,0:T(8,128)(2,1)S(1)} %get-tuple-element.28.p0.fwd_ref), channel_id=1, source_target_pairs={{0,8},{8,0},{16,24},{24,16},{1,9},{9,1},{17,25},{25,17},{2,10},{10... | collective-permute-start | bytes 393224 | tf_op jit(solution)/shard_map/ppermute | solution.py:285
  5.9 6.2 %collective-permute-start.6 = (bf16[256,256]{1,0:T(8,128)(2,1)S(1)}, bf16[256,256]{1,0:T(8,128)(2,1)S(1)}, u32[]{:S(2)}, u32[]{:S(2)}) collective-permute-start(bf16[256,256]{1,0:T(8,128)(2,1)S(1)} %get-tuple-element.38.p0.fwd_ref), channel_id=1, source_target_pairs={{0,8},{8,0},{16,24},{24,16},{1,9},{9,1},{17,25},{25,17},{2,10},{10... | collective-permute-start | bytes 393224 | tf_op jit(solution)/shard_map/ppermute | solution.py:285
  6.4 0.7 %copy-start.6 = (s32[16,8]{0,1:T(8,128)S(1)}, s32[16,8]{0,1:T(8,128)}, u32[]{:S(2)}) copy-start(s32[16,8]{0,1:T(8,128)} %param.13) | copy-start | bytes 1540
  10.4 1.7 %collective-permute-start.8 = (bf16[256,256]{1,0:T(8,128)(2,1)S(1)}, bf16[256,256]{1,0:T(8,128)(2,1)S(1)}, u32[]{:S(2)}, u32[]{:S(2)}) collective-permute-start(bf16[256,256]{1,0:T(8,128)(2,1)S(1)} %collective-permute-done.7.p2), channel_id=1, source_target_pairs={{0,8},{8,0},{16,24},{24,16},{1,9},{9,1},{17,25},{25,17},{2,10},{10... | collective-permute-start | bytes 393224 | tf_op jit(solution)/shard_map/ppermute | solution.py:285
  12.1 2.5 %collective-permute-start.2 = (bf16[256,256]{1,0:T(8,128)(2,1)S(1)}, bf16[256,256]{1,0:T(8,128)(2,1)S(1)}, u32[]{:S(2)}, u32[]{:S(2)}) collective-permute-start(bf16[256,256]{1,0:T(8,128)(2,1)S(1)} %collective-permute-done.1.p2), channel_id=1, source_target_pairs={{0,8},{8,0},{16,24},{24,16},{1,9},{9,1},{17,25},{25,17},{2,10},{10... | collective-permute-start | bytes 393224 | tf_op jit(solution)/shard_map/ppermute | solution.py:285
  12.8 7.5 %collective-permute-start.9 = (bf16[512,256]{1,0:T(8,128)(2,1)S(1)}, bf16[512,256]{1,0:T(8,128)(2,1)S(1)}, u32[]{:S(2)}, u32[]{:S(2)}) collective-permute-start(bf16[512,256]{1,0:T(8,128)(2,1)S(1)} %get-tuple-element.41), channel_id=1, source_target_pairs={{0,1},{1,0},{2,3},{3,2},{4,5},{5,4},{6,7},{7,6},{8,10},{9,11},{10,... | collective-permute-start | bytes 786440 | tf_op jit(solution)/shard_map/ppermute | solution.py:291
  15.3 16.0 %copy-start = (bf16[1024,512]{1,0:T(8,128)(2,1)S(1)}, bf16[1024,512]{1,0:T(8,128)(2,1)}, u32[]{:S(2)}) copy-start(bf16[1024,512]{1,0:T(8,128)(2,1)} %rhs_hbm.3) | copy-start | bytes 3145732
  15.3 16.0 %copy-start.2 = (bf16[8,128,128]{2,1,0:T(8,128)(2,1)S(1)}, bf16[8,128,128]{2,1,0:T(8,128)(2,1)}, u32[]{:S(2)}) copy-start(bf16[8,128,128]{2,1,0:T(8,128)(2,1)} %low_hbm.1) | copy-start | bytes 786436
  15.3 15.9 %copy-start.3 = (bf16[8,128,128]{2,1,0:T(8,128)(2,1)S(1)}, bf16[8,128,128]{2,1,0:T(8,128)(2,1)}, u32[]{:S(2)}) copy-start(bf16[8,128,128]{2,1,0:T(8,128)(2,1)} %up_hbm.1) | copy-start | bytes 786436
  15.3 6.4 %collective-permute-start.3 = (bf16[512,256]{1,0:T(8,128)(2,1)S(1)}, bf16[512,256]{1,0:T(8,128)(2,1)S(1)}, u32[]{:S(2)}, u32[]{:S(2)}) collective-permute-start(bf16[512,256]{1,0:T(8,128)(2,1)S(1)} %get-tuple-element.30), channel_id=1, source_target_pairs={{0,2},{1,3},{2,0},{3,1},{4,6},{5,7},{6,4},{7,5},{8,9},{9,8},{10,11... | collective-permute-start | bytes 786440 | tf_op jit(solution)/shard_map/ppermute | solution.py:291
  21.8 5.8 %collective-permute-start.10 = (bf16[256,256]{1,0:T(8,128)(2,1)S(1)}, bf16[256,256]{1,0:T(8,128)(2,1)S(1)}, u32[]{:S(2)}, u32[]{:S(2)}) collective-permute-start(bf16[256,256]{1,0:T(8,128)(2,1)S(1)} %add_convert_fusion.3), channel_id=1, source_target_pairs={{0,2},{1,3},{2,0},{3,1},{4,6},{5,7},{6,4},{7,5},{8,9},{9,8},{10,11... | collective-permute-start | bytes 393224 | tf_op jit(solution)/shard_map/ppermute | solution.py:291
  23.5 6.9 %collective-permute-start.4 = (bf16[256,256]{1,0:T(8,128)(2,1)S(1)}, bf16[256,256]{1,0:T(8,128)(2,1)S(1)}, u32[]{:S(2)}, u32[]{:S(2)}) collective-permute-start(bf16[256,256]{1,0:T(8,128)(2,1)S(1)} %add_convert_fusion.5), channel_id=1, source_target_pairs={{0,1},{1,0},{2,3},{3,2},{4,5},{5,4},{6,7},{7,6},{8,10},{9,11},{10,... | collective-permute-start | bytes 393224 | tf_op jit(solution)/shard_map/ppermute | solution.py:291
  27.7 12.0 %collective-permute-start.11 = (bf16[256,256]{1,0:T(8,128)(2,1)S(1)}, bf16[256,256]{1,0:T(8,128)(2,1)S(1)}, u32[]{:S(2)}, u32[]{:S(2)}) collective-permute-start(bf16[256,256]{1,0:T(8,128)(2,1)S(1)} %add_convert_fusion.2.mine_ref), channel_id=1, source_target_pairs={{0,4},{1,5},{2,6},{3,7},{4,0},{5,1},{6,2},{7,3},{8,12},{9,13},{10,... | collective-permute-start | bytes 393224 | tf_op jit(solution)/shard_map/ppermute | solution.py:285
  30.5 10.6 %collective-permute-start.5 = (bf16[256,256]{1,0:T(8,128)(2,1)S(1)}, bf16[256,256]{1,0:T(8,128)(2,1)S(1)}, u32[]{:S(2)}, u32[]{:S(2)}) collective-permute-start(bf16[256,256]{1,0:T(8,128)(2,1)S(1)} %add_convert_fusion.4.mine_ref), channel_id=1, source_target_pairs={{0,4},{1,5},{2,6},{3,7},{4,0},{5,1},{6,2},{7,3},{8,12},{9,13},{10,... | collective-permute-start | bytes 393224 | tf_op jit(solution)/shard_map/ppermute | solution.py:285
  39.7 23.2 %copy-start.4 = (bf16[2,128,128]{2,1,0:T(8,128)(2,1)S(1)}, bf16[2,128,128]{2,1,0:T(8,128)(2,1)}, u32[]{:S(2)}) copy-start(bf16[2,128,128]{2,1,0:T(8,128)(2,1)} %inv_ref.3) | copy-start | bytes 196612
  40.6 6.3 %collective-permute-start.16 = (bf16[256,256]{1,0:T(8,128)(2,1)S(1)}, bf16[256,256]{1,0:T(8,128)(2,1)S(1)}, u32[]{:S(2)}, u32[]{:S(2)}) collective-permute-start(bf16[256,256]{1,0:T(8,128)(2,1)S(1)} %get-tuple-element.49), channel_id=1, source_target_pairs={{0,2},{1,3},{2,0},{3,1},{4,6},{5,7},{6,4},{7,5},{8,9},{9,8},{10,11... | collective-permute-start | bytes 393224 | tf_op jit(solution)/shard_map/ppermute | solution.py:291
  42.1 6.4 %collective-permute-start.12 = (bf16[256,256]{1,0:T(8,128)(2,1)S(1)}, bf16[256,256]{1,0:T(8,128)(2,1)S(1)}, u32[]{:S(2)}, u32[]{:S(2)}) collective-permute-start(bf16[256,256]{1,0:T(8,128)(2,1)S(1)} %get-tuple-element.45), channel_id=1, source_target_pairs={{0,1},{1,0},{2,3},{3,2},{4,5},{5,4},{6,7},{7,6},{8,10},{9,11},{10,... | collective-permute-start | bytes 393224 | tf_op jit(solution)/shard_map/ppermute | solution.py:291
  47.0 7.2 %collective-permute-start.17 = (bf16[512,256]{1,0:T(8,128)(2,1)S(1)}, bf16[512,256]{1,0:T(8,128)(2,1)S(1)}, u32[]{:S(2)}, u32[]{:S(2)}) collective-permute-start(bf16[512,256]{1,0:T(8,128)(2,1)S(1)} %constant_dynamic-update-slice_fusion.2.near_ref), channel_id=1, source_target_pairs={{0,1},{1,0},{2,3},{3,2},{4,5},{5,4},{6,7},{7,6},{8,10},{9,11},{10,... | collective-permute-start | bytes 786440 | tf_op jit(solution)/shard_map/ppermute | solution.py:291
  48.5 6.4 %collective-permute-start.13 = (bf16[512,256]{1,0:T(8,128)(2,1)S(1)}, bf16[512,256]{1,0:T(8,128)(2,1)S(1)}, u32[]{:S(2)}, u32[]{:S(2)}) collective-permute-start(bf16[512,256]{1,0:T(8,128)(2,1)S(1)} %constant_dynamic-update-slice_fusion.near_ref), channel_id=1, source_target_pairs={{0,2},{1,3},{2,0},{3,1},{4,6},{5,7},{6,4},{7,5},{8,9},{9,8},{10,11... | collective-permute-start | bytes 786440 | tf_op jit(solution)/shard_map/ppermute | solution.py:291
  54.9 1.6 %collective-permute-start.18 = (bf16[512,256]{1,0:T(8,128)(2,1)S(1)}, bf16[512,256]{1,0:T(8,128)(2,1)S(1)}, u32[]{:S(2)}, u32[]{:S(2)}) collective-permute-start(bf16[512,256]{1,0:T(8,128)(2,1)S(1)} %get-tuple-element.51), channel_id=1, source_target_pairs={{0,8},{8,0},{16,24},{24,16},{1,9},{9,1},{17,25},{25,17},{2,10},{10... | collective-permute-start | bytes 786440 | tf_op jit(solution)/shard_map/ppermute | solution.py:285
  55.7 2.4 %collective-permute-start.14 = (bf16[512,256]{1,0:T(8,128)(2,1)S(1)}, bf16[512,256]{1,0:T(8,128)(2,1)S(1)}, u32[]{:S(2)}, u32[]{:S(2)}) collective-permute-start(bf16[512,256]{1,0:T(8,128)(2,1)S(1)} %get-tuple-element.47), channel_id=1, source_target_pairs={{0,8},{8,0},{16,24},{24,16},{1,9},{9,1},{17,25},{25,17},{2,10},{10... | collective-permute-start | bytes 786440 | tf_op jit(solution)/shard_map/ppermute | solution.py:285
  56.5 6.4 %collective-permute-start.19 = (bf16[256,256]{1,0:T(8,128)(2,1)S(1)}, bf16[256,256]{1,0:T(8,128)(2,1)S(1)}, u32[]{:S(2)}, u32[]{:S(2)}) collective-permute-start(bf16[256,256]{1,0:T(8,128)(2,1)S(1)} %add_convert_fusion), channel_id=1, source_target_pairs={{0,16},{8,24},{16,0},{24,8},{1,17},{9,25},{17,1},{25,9},{2,18},{10... | collective-permute-start | bytes 393224 | tf_op jit(solution)/shard_map/ppermute | solution.py:285
  58.1 6.8 %collective-permute-start.15 = (bf16[256,256]{1,0:T(8,128)(2,1)S(1)}, bf16[256,256]{1,0:T(8,128)(2,1)S(1)}, u32[]{:S(2)}, u32[]{:S(2)}) collective-permute-start(bf16[256,256]{1,0:T(8,128)(2,1)S(1)} %add_convert_fusion.1), channel_id=1, source_target_pairs={{0,16},{8,24},{16,0},{24,8},{1,17},{9,25},{17,1},{25,9},{2,18},{10... | collective-permute-start | bytes 393224 | tf_op jit(solution)/shard_map/ppermute | solution.py:285

commit v3 on v2

--- a/solution.py
+++ b/solution.py
@@ -9,10 +9,8 @@
 
 BF = jnp.bfloat16
 F32 = jnp.float32
-CHUNKS = 2
-FLIP = 1
+FLIPS = (0, 1)
 MIB = 1 << 20
-TINY = pl.CostEstimate(flops=1, bytes_accessed=1, transcendentals=0)
 
 
 def params(mib, **kw):
@@ -46,10 +44,9 @@
     return pl.pallas_call(
         fwd_kernel,
         in_specs=[pl.BlockSpec(memory_space=pltpu.HBM)] * 2,
-        out_shape=[jax.ShapeDtypeStruct((rhs.shape[0], rhs.shape[1] // CHUNKS), BF)] * CHUNKS,
+        out_shape=[jax.ShapeDtypeStruct((rhs.shape[0], rhs.shape[1] // len(FLIPS)), BF)] * len(FLIPS),
         scratch_shapes=[pltpu.VMEM(inv.shape, BF), pltpu.VMEM(rhs.shape, BF), pltpu.SemaphoreType.DMA((2,))],
         compiler_params=params(8),
-        cost_estimate=TINY,
         name="fwd_low",
     )(inv, rhs)
 
@@ -102,7 +99,6 @@
             pltpu.SemaphoreType.DMA((steps,)),
         ],
         compiler_params=params(48),
-        cost_estimate=TINY,
         name="sum_lower" if lower else "sum_upper",
     )(ids, targets, blocks)
 
@@ -138,28 +134,15 @@
         ],
         scratch_shapes=[pltpu.SemaphoreType.DMA((6,))],
         compiler_params=params(8),
-        cost_estimate=TINY,
         name="pick_top",
     )(ids, rhs_top, inv_low, inv_up)
 
 
-def put(i, value, flip, first, two, zero):
-    per = two.shape[0]
-    if i == 0:
-        first[:per, :] = value
-    elif i == 3:
-        zero[...] = value
-    elif (i == 1) == (flip == 0):
-        first[per:, :] = value
-    else:
-        two[...] = value
-
-
-def lower_kernel(flip, mat_ref, p0, p1, p2, p3, first, two, zero):
+def lower_kernel(begin, mat_ref, p0, p1, p2, p3, *outs):
     pieces = (p0, p1, p2, p3)
-    per = two.shape[0]
+    per = outs[0].shape[0]
     deep = mat_ref.shape[2]
-    for i in range(4):
+    for i, out in enumerate(outs, begin):
         total = None
         for s in range(mat_ref.shape[0]):
             part = jnp.dot(
@@ -168,17 +151,14 @@
                 preferred_element_type=F32,
             )
             total = part if total is None else total + part
-        put(i, total.astype(BF), flip, first, two, zero)
-
-
-def upper_kernel(flip, mat_ref, near_ref, far_ref, first, two, zero):
-    half = near_ref.shape[0] // 2
-    pieces = [near_ref.at[:half], far_ref.at[:half], near_ref.at[half:], far_ref.at[half:]]
-    if flip:
-        pieces[1], pieces[2] = pieces[2], pieces[1]
-    per = two.shape[0]
+        out[...] = total.astype(BF)
+
+
+def upper_kernel(begin, mat_ref, p0, p1, p2, p3, *outs):
+    pieces = (p0, p1, p2, p3)
+    per = outs[0].shape[0]
     groups = mat_ref.shape[0] // 4
-    for i in range(4):
+    for i, out in enumerate(outs, begin):
         total = None
         for g in range(4):
             left = jnp.concatenate(
@@ -186,41 +166,32 @@
             )
             part = jnp.dot(left, pieces[g][...], preferred_element_type=F32)
             total = part if total is None else total + part
-        put(i, total.astype(BF), 0, first, two, zero)
-
-
-def apply(kernel, mat, pieces, name):
+        out[...] = total.astype(BF)
+
+
+def apply(kernel, mat, pieces, begin, end, name):
     rows, cols = mat.shape[1], pieces[0].shape[1]
     return pl.pallas_call(
-        kernel,
-        out_shape=[
-            jax.ShapeDtypeStruct((rows // 2, cols), BF),
-            jax.ShapeDtypeStruct((rows // 4, cols), BF),
-            jax.ShapeDtypeStruct((rows // 4, cols), BF),
-        ],
+        functools.partial(kernel, begin),
+        out_shape=[jax.ShapeDtypeStruct((rows // 4, cols), BF)] * (end - begin),
         compiler_params=params(32 if mat.size * 2 > 4 * MIB else 10),
         name=name,
     )(mat, *pieces)
 
 
-def top_kernel(rhs_ref, low_ref, up_ref, mine_ref, got_ref, *refs):
-    out, copy = refs[-2:]
+def top_kernel(rhs_ref, low_ref, up_ref, mine_ref, got_ref, out_ref):
     width = low_ref.shape[1]
     for k in range(2):
         rows, cross = slice(k * width, (k + 1) * width), slice((1 - k) * width, (2 - k) * width)
         lsum = mine_ref[rows, :].astype(F32) + got_ref[cross, :].astype(F32)
         resid = (rhs_ref[rows, :].astype(F32) - lsum).astype(BF)
         fwd = jnp.dot(low_ref[k], resid, preferred_element_type=F32).astype(BF)
-        sol = jnp.dot(up_ref[k], fwd, preferred_element_type=F32).astype(BF)
-        copy[rows, :] = sol
-        if k == 0:
-            out[...] = sol
-
-
-def solve_top(picked, mine, got, into, chunk, chunks):
+        out_ref[rows, :] = jnp.dot(up_ref[k], fwd, preferred_element_type=F32).astype(BF)
+
+
+def solve_top(picked, mine, got, chunk):
     rhs, inv_low, inv_up = picked
     rows, cols = mine.shape
-    more = [] if into is None else [into]
     return pl.pallas_call(
         top_kernel,
         grid=(1,),
@@ -230,21 +201,12 @@
             pl.BlockSpec(inv_up.shape, lambda i: (0, 0, 0)),
             pl.BlockSpec((rows, cols), lambda i: (0, 0)),
             pl.BlockSpec((rows, cols), lambda i: (0, 0)),
-        ]
-        + [pl.BlockSpec(memory_space=pl.ANY)] * len(more),
-        out_specs=[
-            pl.BlockSpec((rows // 2, cols), lambda i: (0, chunk)),
-            pl.BlockSpec((rows, cols), lambda i: (0, 0)),
         ],
-        out_shape=[
-            jax.ShapeDtypeStruct((rows // 2, cols * chunks), BF),
-            jax.ShapeDtypeStruct((rows, cols), BF),
-        ],
-        input_output_aliases={5: 0} if more else {},
+        out_specs=pl.BlockSpec((rows, cols), lambda i: (0, 0)),
+        out_shape=jax.ShapeDtypeStruct((rows, cols), BF),
         compiler_params=params(8),
-        cost_estimate=TINY,
         name="solve_top",
-    )(rhs, inv_low, inv_up, mine, got, *more)
+    )(rhs, inv_low, inv_up, mine, got)
 
 
 def low_kernel(parts, inv_ref, fwd_ref, *refs):
@@ -269,15 +231,14 @@
             pl.BlockSpec(inv.shape, lambda i: (0, 0, 0)),
             pl.BlockSpec((rows, cols), lambda i: (0, 0)),
         ]
-        + [pl.BlockSpec((rows, cols), lambda i, at=at: (at, 0)) for _, at in terms]
+        + [pl.BlockSpec((rows, cols), lambda i: (0, 0))] * len(terms)
         + [pl.BlockSpec(memory_space=pl.ANY)] * len(more),
         out_specs=pl.BlockSpec((rows, cols), lambda i: (0, chunk)),
         out_shape=jax.ShapeDtypeStruct((rows, cols * chunks), BF),
         input_output_aliases={2 + len(terms): 0} if more else {},
         compiler_params=params(8),
-        cost_estimate=TINY,
         name="solve_low",
-    )(inv, fwd, *[t for t, _ in terms], *more)
+    )(inv, fwd, *terms, *more)
 
 
 def swap(x, axis, bit):
@@ -335,15 +296,11 @@
     return held
 
 
-def sums_row(zero, core, more, size):
-    per = zero.shape[0]
-    if per == size:
-        return [(zero, 0), (core, 1), (more, 0)]
-    terms = [zero, core[per:], more]
+def sums_row(terms, size):
     for bit in range(2, lax.axis_size("row").bit_length() - 1):
         new = swap(add(*[odd(t, size) for t in terms]), "row", bit)
         terms = [even(t, size) for t in terms] + [new]
-    return [(t, 0) for t in terms]
+    return terms
 
 
 def body(
@@ -370,31 +327,41 @@
     side = [swap(x, "row", 0) for x in near]
     mat_l = sum_blocks(True, ids, targets, lower_blocks, rows, tops, own)
     far_side = [swap(after(x, mat_l), "row", 0) for x in far]
-    flips = [i % 2 * FLIP for i in range(CHUNKS)]
-    parts = [
-        apply(functools.partial(lower_kernel, flip), mat_l, pieces, "apply_lower")
-        for flip, pieces in zip(flips, zip(near, side, far, far_side))
-    ]
-    mat_u = sum_blocks(False, after(ids, parts[-1][0]), targets, upper_blocks, rows, tops, own)
-    picked = pick_top(ids, rhs_top, inv_lower_top, inv_upper_top, cols // 2)
-    sol_top = sol_low = None
-    solved = []
-    for i, (flip, (first, two, zero)) in enumerate(zip(flips, parts)):
-        got = after(cross(first, 0, flip), mat_u)
-        more = cross(add(two, got[: two.shape[0]]), 1, flip)
-        mine = sums_col([zero, got[two.shape[0] :], more], width)
-        other = swap(mine, "col", last)
-        sol_top, both = solve_top(picked, mine, other, sol_top, i, CHUNKS)
-        held = widen_col(both, width)
-        held = jnp.concatenate([held, cross(held, 1, flip)], axis=0)
-        solved.append((held, cross(held, 0, flip)))
-    for i, (flip, pieces) in enumerate(zip(flips, solved)):
-        first, two, zero = apply(functools.partial(upper_kernel, flip), mat_u, pieces, "apply_upper")
-        core = swap(first, "row", 0)
-        more = swap(add(two, core[: two.shape[0]]), "row", 1)
-        terms = sums_row(zero, core, more, own * width)
-        sol_low = solve_low(inv_upper_low, fwds[i], terms, sol_low, i, CHUNKS)
-    return sol_low, sol_top
+    pieces = list(zip(near, side, far, far_side))
+    parts = [apply(lower_kernel, mat_l, p, 0, 1, "first_lower") for p in pieces]
+    parts = [x + apply(lower_kernel, mat_l, p, 1, 4, "apply_lower") for x, p in zip(parts, pieces)]
+    mine = []
+    for i, (three, one, two, zero) in enumerate(parts):
+        flip = FLIPS[i]
+        if flip:
+            one, two = two, one
+        got = cross(three, 0, flip)
+        rest = cross(one, 0, flip)
+        more = cross(add(two, got), 1, flip)
+        mine.append(sums_col([zero, rest, more], width))
+    other = [swap(x, "col", last) for x in mine]
+    mat_u = sum_blocks(False, after(ids, mine[-1]), targets, upper_blocks, rows, tops, own)
+    picked = pick_top(after(ids, mat_u), rhs_top, inv_lower_top, inv_upper_top, cols // 2)
+    sol_low = None
+    top_parts, solved = [], []
+    for i, flip in enumerate(FLIPS):
+        both = solve_top(picked, mine[i], other[i], i)
+        top_parts.append(both[:width])
+        zero = widen_col(both, width)
+        two = cross(zero, 1, flip)
+        one = cross(zero, 0, flip)
+        three = cross(two, 0, flip)
+        if flip:
+            one, two = two, one
+        solved.append((zero, one, two, three))
+    for i, pieces in enumerate(solved):
+        (three,) = apply(upper_kernel, mat_u, pieces, 0, 1, "first_upper")
+        one, two, zero = apply(upper_kernel, mat_u, pieces, 1, 4, "apply_upper")
+        got, rest = swap(three, "row", 0), swap(one, "row", 0)
+        more = swap(add(two, got), "row", 1)
+        terms = sums_row([zero, rest, more], own * width)
+        sol_low = solve_low(inv_upper_low, fwds[i], terms, sol_low, i, len(FLIPS))
+    return sol_low, jnp.concatenate(top_parts, axis=1)
 
 
 def solution(mesh):

time: 66.1 us -> 62.4 us (0.944)
  waiting for transfers between devices: 27.3 us -> 20.3 us
  starting transfers between devices: 20.3 us -> 23.5 us
    ppermute x8 -> x12, waiting for transfers between devices: 12.9 us -> 8.8 us  [cross(): return lax.ppermute(x, ('row', 'col'), pairs)]
    ppermute x8 -> x12, starting transfers between devices: 10 us -> 13 us  [cross(): return lax.ppermute(x, ('row', 'col'), pairs)]
    ppermute x12 -> x14, waiting for transfers between devices: 14.4 us -> 11.5 us  [swap(): return lax.ppermute(x, axis, [(i, i ^ 1 << bit) for i in range(size)])]
    pallas_call x2, Pallas kernels: 1.92 us -> 0.72 us  [solve_top(): pl.pallas_call(top_kernel, grid=(1,), in_specs=[pl.BlockSpec((rows, cols)...]
    pallas_call x4 -> x8, Pallas kernels: 2.84 us -> 3.55 us  [apply(): pl.pallas_call(functools.partial(kernel, begin), out_shape=[jax.ShapeDtyp...]
    concatenate x0 -> x1, other arithmetic: none -> 0.67 us  [body(): return (sol_low, jnp.concatenate(top_parts, axis=1))]
    ppermute x12 -> x14, starting transfers between devices: 10.3 us -> 10.5 us  [swap(): return lax.ppermute(x, axis, [(i, i ^ 1 << bit) for i in range(size)])]
    unnamed x16 -> x14, local copies, waits for them, and re-layouts: 2.51 us -> 2.49 us
  transfers between devices with their start and end apart: 20 -> 26, of which waited for: 10 -> 11; matrix products, arithmetic and copies ran while one was open for 0% -> 2% of each run, Pallas kernels for 20% -> 21%
where the time goes in v3:
time: 62.4 us; the launch traced here: 62.2 us
  starting transfers between devices  23.5 us (38%)
  waiting for transfers between devices  20.3 us (33%)
  Pallas kernels  14 us (22%)
  local copies, waits for them, and re-layouts  2.5 us (4%)
  other arithmetic  0.98 us (2%)
  between operations  0.88 us (1%)
    ppermute x12, starting transfers between devices, cross(): return lax.ppermute(x, ('row', 'col'), pairs)  13 us
    ppermute x14, waiting for transfers between devices, swap(): return lax.ppermute(x, axis, [(i, i ^ 1 << bit) for i in range(size)])  11.5 us
    ppermute x14, starting transfers between devices, swap(): return lax.ppermute(x, axis, [(i, i ^ 1 << bit) for i in range(size)])  10.5 us
    ppermute x12, waiting for transfers between devices, cross(): return lax.ppermute(x, ('row', 'col'), pairs)  8.8 us
    pallas_call x2, Pallas kernels, sum_blocks(): pl.pallas_call(functools.partial(sum_kernel, lower, rows, tops, own), in_...  6.57 us
    pallas_call x8, Pallas kernels, apply(): pl.pallas_call(functools.partial(kernel, begin), out_shape=[jax.ShapeDtyp...  3.55 us
    unnamed x14, local copies, waits for them, and re-layouts  2.49 us
    pallas_call x2, Pallas kernels, solve_low(): pl.pallas_call(functools.partial(low_kernel, len(terms)), grid=(1,), in_s...  1.77 us
  transfers between devices with their start and end apart: 26, of which 11 were waited for; matrix products, arithmetic and copies ran while one was open for 2% of the time, Pallas kernels for 21%

profile of v3, /device:TPU:0, one launch (start us, length us, event | category | flops | bytes accessed | tf_op | source)
XLA Modules:
  0.0 62.2 jit_solution(15237226732714973158)
XLA Ops:
  0.6 0.9 %copy-done.1 = bf16[256,512]{1,0:T(8,128)(2,1)S(1)} copy-done((bf16[256,512]{1,0:T(8,128)(2,1)S(1)}, bf16[256,512]{1,0:T(8,128)(2,1)}, u32[]{:S(2)}) %copy-start.1) | copy-done | bytes 262168
  1.6 0.8 %copy-done.5 = bf16[2,128,128]{2,1,0:T(8,128)(2,1)S(1)} copy-done((bf16[2,128,128]{2,1,0:T(8,128)(2,1)S(1)}, bf16[2,128,128]{2,1,0:T(8,128)(2,1)}, u32[]{:S(2)}) %copy-start.5) | copy-done | bytes 65560
  2.4 0.3 fwd_low.1
  2.7 3.0 %collective-permute-start.14 = (bf16[256,256]{1,0:T(8,128)(2,1)S(1)}, bf16[256,256]{1,0:T(8,128)(2,1)S(1)}, u32[]{:S(2)}, u32[]{:S(2)}) collective-permute-start(bf16[256,256]{1,0:T(8,128)(2,1)S(1)} %get-tuple-element.36.p0.fwd_ref), channel_id=1, source_target_pairs={{0,16},{8,24},{16,0},{24,8},{1,17},{9,25},{17,1},{25,9},{2,18},{10... | collective-permute-start | bytes 393224 | tf_op jit(solution)/shard_map/ppermute | solution.py:246
  6.0 0.7 %copy-done.6 = s32[16,8]{0,1:T(8,128)S(1)} copy-done((s32[16,8]{0,1:T(8,128)S(1)}, s32[16,8]{0,1:T(8,128)}, u32[]{:S(2)}) %copy-start.6) | copy-done | bytes 536
  6.7 3.3 %sum_lower.1.mat_ref = bf16[4,1024,256]{2,1,0:T(8,128)(2,1)S(1)} custom-call(s32[2]{0:T(128)S(1)} %pad_add_fusion.ids_ref, s32[8,16]{1,0:T(8,128)S(1)} %bitcast.3, bf16[16,8,128,128]{3,2,1,0:T(8,128)(2,1)} %blk_hbm.2), custom_call_target="tpu_custom_call" | custom-call | tf_op jit(solution)/shard_map/sum_lower/pallas_call | solution.py:88
  10.0 0.4 collective-permute-start.15
  10.6 1.5 %collective-permute-done.1.p2 = bf16[256,256]{1,0:T(8,128)(2,1)S(1)} collective-permute-done((bf16[256,256]{1,0:T(8,128)(2,1)S(1)}, bf16[256,256]{1,0:T(8,128)(2,1)S(1)}, u32[]{:S(2)}, u32[]{:S(2)}) %collective-permute-start.1) | collective-permute-done | bytes 131104 | tf_op jit(solution)/shard_map/ppermute | solution.py:246
  12.1 0.3 first_lower.3
  12.4 1.8 %collective-permute-start.17 = (bf16[256,256]{1,0:T(8,128)(2,1)S(1)}, bf16[256,256]{1,0:T(8,128)(2,1)S(1)}, u32[]{:S(2)}, u32[]{:S(2)}) collective-permute-start(bf16[256,256]{1,0:T(8,128)(2,1)S(1)} %first_lower.3), channel_id=1, source_target_pairs={{0,1},{1,0},{2,3},{3,2},{4,5},{5,4},{6,7},{7,6},{8,10},{9,11},{10,... | collective-permute-start | bytes 393224 | tf_op jit(solution)/shard_map/ppermute | solution.py:252
  14.2 0.6 apply_lower.3
  14.8 0.4 collective-permute-start.16
  15.1 0.3 first_lower.2
  15.5 1.9 %collective-permute-start.4 = (bf16[256,256]{1,0:T(8,128)(2,1)S(1)}, bf16[256,256]{1,0:T(8,128)(2,1)S(1)}, u32[]{:S(2)}, u32[]{:S(2)}) collective-permute-start(bf16[256,256]{1,0:T(8,128)(2,1)S(1)} %first_lower.2), channel_id=1, source_target_pairs={{0,2},{1,3},{2,0},{3,1},{4,6},{5,7},{6,4},{7,5},{8,9},{9,8},{10,11... | collective-permute-start | bytes 393224 | tf_op jit(solution)/shard_map/ppermute | solution.py:252
  17.3 0.6 apply_lower.2
  17.9 0.3 collective-permute-start.3
  18.3 1.9 %collective-permute-start.18 = (bf16[256,256]{1,0:T(8,128)(2,1)S(1)}, bf16[256,256]{1,0:T(8,128)(2,1)S(1)}, u32[]{:S(2)}, u32[]{:S(2)}) collective-permute-start(bf16[256,256]{1,0:T(8,128)(2,1)S(1)} %add_convert_fusion.2), channel_id=1, source_target_pairs={{0,2},{1,3},{2,0},{3,1},{4,6},{5,7},{6,4},{7,5},{8,9},{9,8},{10,11... | collective-permute-start | bytes 393224 | tf_op jit(solution)/shard_map/ppermute | solution.py:252
  20.1 0.4 collective-permute-done.4
  20.6 1.7 %collective-permute-start.5 = (bf16[256,256]{1,0:T(8,128)(2,1)S(1)}, bf16[256,256]{1,0:T(8,128)(2,1)S(1)}, u32[]{:S(2)}, u32[]{:S(2)}) collective-permute-start(bf16[256,256]{1,0:T(8,128)(2,1)S(1)} %add_convert_fusion.5), channel_id=1, source_target_pairs={{0,1},{1,0},{2,3},{3,2},{4,5},{5,4},{6,7},{7,6},{8,10},{9,11},{10,... | collective-permute-start | bytes 393224 | tf_op jit(solution)/shard_map/ppermute | solution.py:252
  22.3 2.8 %collective-permute-done.18 = bf16[256,256]{1,0:T(8,128)(2,1)S(1)} collective-permute-done((bf16[256,256]{1,0:T(8,128)(2,1)S(1)}, bf16[256,256]{1,0:T(8,128)(2,1)S(1)}, u32[]{:S(2)}, u32[]{:S(2)}) %collective-permute-start.18) | collective-permute-done | bytes 131104 | tf_op jit(solution)/shard_map/ppermute | solution.py:252
  25.1 2.5 %collective-permute-start.19 = (bf16[256,256]{1,0:T(8,128)(2,1)S(1)}, bf16[256,256]{1,0:T(8,128)(2,1)S(1)}, u32[]{:S(2)}, u32[]{:S(2)}) collective-permute-start(bf16[256,256]{1,0:T(8,128)(2,1)S(1)} %add_convert_fusion.1.mine_ref), channel_id=1, source_target_pairs={{0,4},{1,5},{2,6},{3,7},{4,0},{5,1},{6,2},{7,3},{8,12},{9,13},{10,... | collective-permute-start | bytes 393224 | tf_op jit(solution)/shard_map/ppermute | solution.py:246
  27.7 0.8 %collective-permute-start.6 = (bf16[256,256]{1,0:T(8,128)(2,1)S(1)}, bf16[256,256]{1,0:T(8,128)(2,1)S(1)}, u32[]{:S(2)}, u32[]{:S(2)}) collective-permute-start(bf16[256,256]{1,0:T(8,128)(2,1)S(1)} %add_convert_fusion.4.mine_ref), channel_id=1, source_target_pairs={{0,4},{1,5},{2,6},{3,7},{4,0},{5,1},{6,2},{7,3},{8,12},{9,13},{10,... | collective-permute-start | bytes 393224 | tf_op jit(solution)/shard_map/ppermute | solution.py:246
  28.5 3.3 %sum_upper.1.mat_ref = bf16[8,1024,128]{2,1,0:T(8,128)(2,1)S(1)} custom-call(s32[2]{0:T(128)S(1)} %pad_add_fusion.ids_ref, s32[8,16]{1,0:T(8,128)S(1)} %bitcast.4, bf16[16,8,128,128]{3,2,1,0:T(8,128)(2,1)} %blk_hbm.3), custom_call_target="tpu_custom_call" | custom-call | tf_op jit(solution)/shard_map/sum_upper/pallas_call | solution.py:88
  31.8 1.1 %pick_top.1 = (bf16[256,512]{1,0:T(8,128)(2,1)S(1)}, bf16[2,128,128]{2,1,0:T(8,128)(2,1)S(1)}, bf16[2,128,128]{2,1,0:T(8,128)(2,1)S(1)}) custom-call(s32[2]{0:T(128)S(1)} %pad_add_fusion.ids_ref, bf16[1024,512]{1,0:T(8,128)(2,1)S(1)} %copy-done, bf16[8,128,128]{2,1,0:T(8,128)(2,1)S(1)} %copy-done.2, bf16[8,128,128]{2,1,0:T(8,128)(2,1)S(1)} %copy-done.3), custom_call_target="tpu_custom_call" | custom-call | tf_op jit(solution)/shard_map/pick_top/pallas_call | solution.py:127
  33.0 4.0 %collective-permute-done.19.got_ref = bf16[256,256]{1,0:T(8,128)(2,1)S(1)} collective-permute-done((bf16[256,256]{1,0:T(8,128)(2,1)S(1)}, bf16[256,256]{1,0:T(8,128)(2,1)S(1)}, u32[]{:S(2)}, u32[]{:S(2)}) %collective-permute-start.19) | collective-permute-done | bytes 131104 | tf_op jit(solution)/shard_map/ppermute | solution.py:246
  36.9 0.4 solve_top.3.p0
  37.4 1.4 %collective-permute-done.6.got_ref = bf16[256,256]{1,0:T(8,128)(2,1)S(1)} collective-permute-done((bf16[256,256]{1,0:T(8,128)(2,1)S(1)}, bf16[256,256]{1,0:T(8,128)(2,1)S(1)}, u32[]{:S(2)}, u32[]{:S(2)}) %collective-permute-start.6) | collective-permute-done | bytes 131104 | tf_op jit(solution)/shard_map/ppermute | solution.py:246
  38.8 0.4 solve_top.2.p0
  39.2 1.0 %collective-permute-start.7 = (bf16[256,256]{1,0:T(8,128)(2,1)S(1)}, bf16[256,256]{1,0:T(8,128)(2,1)S(1)}, u32[]{:S(2)}, u32[]{:S(2)}) collective-permute-start(bf16[256,256]{1,0:T(8,128)(2,1)S(1)} %solve_top.2.p0), channel_id=1, source_target_pairs={{0,1},{1,0},{2,3},{3,2},{4,5},{5,4},{6,7},{7,6},{8,10},{9,11},{10,... | collective-permute-start | bytes 393224 | tf_op jit(solution)/shard_map/ppermute | solution.py:252
  40.2 1.1 %collective-permute-start.20 = (bf16[256,256]{1,0:T(8,128)(2,1)S(1)}, bf16[256,256]{1,0:T(8,128)(2,1)S(1)}, u32[]{:S(2)}, u32[]{:S(2)}) collective-permute-start(bf16[256,256]{1,0:T(8,128)(2,1)S(1)} %solve_top.3.p0), channel_id=1, source_target_pairs={{0,1},{1,0},{2,3},{3,2},{4,5},{5,4},{6,7},{7,6},{8,10},{9,11},{10,... | collective-permute-start | bytes 393224 | tf_op jit(solution)/shard_map/ppermute | solution.py:252
  41.3 2.4 %collective-permute-done.21.p2 = bf16[256,256]{1,0:T(8,128)(2,1)S(1)} collective-permute-done((bf16[256,256]{1,0:T(8,128)(2,1)S(1)}, bf16[256,256]{1,0:T(8,128)(2,1)S(1)}, u32[]{:S(2)}, u32[]{:S(2)}) %collective-permute-start.21) | collective-permute-done | bytes 131104 | tf_op jit(solution)/shard_map/ppermute | solution.py:252
  43.6 1.2 %collective-permute-start.22 = (bf16[256,256]{1,0:T(8,128)(2,1)S(1)}, bf16[256,256]{1,0:T(8,128)(2,1)S(1)}, u32[]{:S(2)}, u32[]{:S(2)}) collective-permute-start(bf16[256,256]{1,0:T(8,128)(2,1)S(1)} %collective-permute-done.21.p2), channel_id=1, source_target_pairs={{0,1},{1,0},{2,3},{3,2},{4,5},{5,4},{6,7},{7,6},{8,10},{9,11},{10,... | collective-permute-start | bytes 393224 | tf_op jit(solution)/shard_map/ppermute | solution.py:252
  45.1 1.8 %collective-permute-start.9 = (bf16[256,256]{1,0:T(8,128)(2,1)S(1)}, bf16[256,256]{1,0:T(8,128)(2,1)S(1)}, u32[]{:S(2)}, u32[]{:S(2)}) collective-permute-start(bf16[256,256]{1,0:T(8,128)(2,1)S(1)} %collective-permute-done.7.p1), channel_id=1, source_target_pairs={{0,2},{1,3},{2,0},{3,1},{4,6},{5,7},{6,4},{7,5},{8,9},{9,8},{10,11... | collective-permute-start | bytes 393224 | tf_op jit(solution)/shard_map/ppermute | solution.py:252
  46.8 0.7 %collective-permute-done.20.p1 = bf16[256,256]{1,0:T(8,128)(2,1)S(1)} collective-permute-done((bf16[256,256]{1,0:T(8,128)(2,1)S(1)}, bf16[256,256]{1,0:T(8,128)(2,1)S(1)}, u32[]{:S(2)}, u32[]{:S(2)}) %collective-permute-start.20) | collective-permute-done | bytes 131104 | tf_op jit(solution)/shard_map/ppermute | solution.py:252
  47.5 2.3 %collective-permute-done.22.p3 = bf16[256,256]{1,0:T(8,128)(2,1)S(1)} collective-permute-done((bf16[256,256]{1,0:T(8,128)(2,1)S(1)}, bf16[256,256]{1,0:T(8,128)(2,1)S(1)}, u32[]{:S(2)}, u32[]{:S(2)}) %collective-permute-start.22) | collective-permute-done | bytes 131104 | tf_op jit(solution)/shard_map/ppermute | solution.py:252
  49.8 0.3 first_upper.3
  50.2 0.6 apply_upper.3
  50.8 0.6 collective-permute-start.23
  51.4 0.3 first_upper.2
  51.8 0.6 apply_upper.2
  52.4 0.5 collective-permute-start.10
  53.0 1.6 %collective-permute-start.25 = (bf16[256,256]{1,0:T(8,128)(2,1)S(1)}, bf16[256,256]{1,0:T(8,128)(2,1)S(1)}, u32[]{:S(2)}, u32[]{:S(2)}) collective-permute-start(bf16[256,256]{1,0:T(8,128)(2,1)S(1)} %add_convert_fusion), channel_id=1, source_target_pairs={{0,16},{8,24},{16,0},{24,8},{1,17},{9,25},{17,1},{25,9},{2,18},{10... | collective-permute-start | bytes 393224 | tf_op jit(solution)/shard_map/ppermute | solution.py:246
  54.7 0.5 collective-permute-start.12
  55.2 0.7 %pad_maximum_fusion = bf16[128,512]{1,0:T(8,128)(2,1)} fusion(bf16[128,256]{1,0:T(8,128)(2,1)S(1)} %slice.9, bf16[128,256]{1,0:T(8,128)(2,1)S(1)} %slice.8), kind=kLoop, calls=%fused_computation.6 | loop fusion | flops 262144 | bytes 262144 | tf_op jit(solution)/shard_map/concatenate | solution.py:364
  55.9 3.5 %collective-permute-done.25.refs_2_ = bf16[256,256]{1,0:T(8,128)(2,1)S(1)} collective-permute-done((bf16[256,256]{1,0:T(8,128)(2,1)S(1)}, bf16[256,256]{1,0:T(8,128)(2,1)S(1)}, u32[]{:S(2)}, u32[]{:S(2)}) %collective-permute-start.25) | collective-permute-done | bytes 131104 | tf_op jit(solution)/shard_map/ppermute | solution.py:246
  59.4 0.9 %solve_low.2.refs_3_ = bf16[256,512]{1,0:T(8,128)(2,1)} custom-call(bf16[2,128,128]{2,1,0:T(8,128)(2,1)S(1)} %copy-done.4, bf16[256,256]{1,0:T(8,128)(2,1)S(1)} %get-tuple-element.36.p0.fwd_ref, bf16[256,256]{1,0:T(8,128)(2,1)S(1)} %get-tuple-element.41.refs_0_, bf16[256,256]{1,0:T(8,128)(2,1)S(1)} %collective-permute-done.23.refs_1_, ...), custom_call_target="tpu_custom_call" | custom-call | tf_op jit(solution)/shard_map/solve_low/pallas_call | solution.py:227
  60.3 1.0 %collective-permute-done.12.refs_2_ = bf16[256,256]{1,0:T(8,128)(2,1)S(1)} collective-permute-done((bf16[256,256]{1,0:T(8,128)(2,1)S(1)}, bf16[256,256]{1,0:T(8,128)(2,1)S(1)}, u32[]{:S(2)}, u32[]{:S(2)}) %collective-permute-start.12) | collective-permute-done | bytes 131104 | tf_op jit(solution)/shard_map/ppermute | solution.py:246
  61.3 0.9 %solve_low.3 = bf16[256,512]{1,0:T(8,128)(2,1)} custom-call(bf16[2,128,128]{2,1,0:T(8,128)(2,1)S(1)} %copy-done.4, bf16[256,256]{1,0:T(8,128)(2,1)S(1)} %get-tuple-element.23.p0.fwd_ref, bf16[256,256]{1,0:T(8,128)(2,1)S(1)} %get-tuple-element.33.refs_0_, bf16[256,256]{1,0:T(8,128)(2,1)S(1)} %collective-permute-done.10.refs_1_, ...), custom_call_target="tpu_custom_call", output_to_operand_aliasing={{}: (5, {})} | custom-call | tf_op jit(solution)/shard_map/solve_low/pallas_call | solution.py:227
  (44 shorter events, 1.2 us)
Async XLA Ops:
  0.6 1.0 %copy-start.1 = (bf16[256,512]{1,0:T(8,128)(2,1)S(1)}, bf16[256,512]{1,0:T(8,128)(2,1)}, u32[]{:S(2)}) copy-start(bf16[256,512]{1,0:T(8,128)(2,1)} %rhs_hbm.2) | copy-start | bytes 786436
  1.6 0.8 %copy-start.5 = (bf16[2,128,128]{2,1,0:T(8,128)(2,1)S(1)}, bf16[2,128,128]{2,1,0:T(8,128)(2,1)}, u32[]{:S(2)}) copy-start(bf16[2,128,128]{2,1,0:T(8,128)(2,1)} %inv_hbm.1) | copy-start | bytes 196612
  2.7 7.2 %collective-permute-start.14 = (bf16[256,256]{1,0:T(8,128)(2,1)S(1)}, bf16[256,256]{1,0:T(8,128)(2,1)S(1)}, u32[]{:S(2)}, u32[]{:S(2)}) collective-permute-start(bf16[256,256]{1,0:T(8,128)(2,1)S(1)} %get-tuple-element.36.p0.fwd_ref), channel_id=1, source_target_pairs={{0,16},{8,24},{16,0},{24,8},{1,17},{9,25},{17,1},{25,9},{2,18},{10... | collective-permute-start | bytes 393224 | tf_op jit(solution)/shard_map/ppermute | solution.py:246
  5.8 6.3 %collective-permute-start.13 = (bf16[256,256]{1,0:T(8,128)(2,1)S(1)}, bf16[256,256]{1,0:T(8,128)(2,1)S(1)}, u32[]{:S(2)}, u32[]{:S(2)}) collective-permute-start(bf16[256,256]{1,0:T(8,128)(2,1)S(1)} %get-tuple-element.36.p0.fwd_ref), channel_id=1, source_target_pairs={{0,8},{8,0},{16,24},{24,16},{1,9},{9,1},{17,25},{25,17},{2,10},{10... | collective-permute-start | bytes 393224 | tf_op jit(solution)/shard_map/ppermute | solution.py:246
  5.8 6.3 %collective-permute-start.1 = (bf16[256,256]{1,0:T(8,128)(2,1)S(1)}, bf16[256,256]{1,0:T(8,128)(2,1)S(1)}, u32[]{:S(2)}, u32[]{:S(2)}) collective-permute-start(bf16[256,256]{1,0:T(8,128)(2,1)S(1)} %get-tuple-element.23.p0.fwd_ref), channel_id=1, source_target_pairs={{0,16},{8,24},{16,0},{24,8},{1,17},{9,25},{17,1},{25,9},{2,18},{10... | collective-permute-start | bytes 393224 | tf_op jit(solution)/shard_map/ppermute | solution.py:246
  6.0 0.7 %copy-start.6 = (s32[16,8]{0,1:T(8,128)S(1)}, s32[16,8]{0,1:T(8,128)}, u32[]{:S(2)}) copy-start(s32[16,8]{0,1:T(8,128)} %param.13) | copy-start | bytes 1540
  10.0 2.1 %collective-permute-start.15 = (bf16[256,256]{1,0:T(8,128)(2,1)S(1)}, bf16[256,256]{1,0:T(8,128)(2,1)S(1)}, u32[]{:S(2)}, u32[]{:S(2)}) collective-permute-start(bf16[256,256]{1,0:T(8,128)(2,1)S(1)} %collective-permute-done.14.p2), channel_id=1, source_target_pairs={{0,8},{8,0},{16,24},{24,16},{1,9},{9,1},{17,25},{25,17},{2,10},{10... | collective-permute-start | bytes 393224 | tf_op jit(solution)/shard_map/ppermute | solution.py:246
  10.4 4.7 %collective-permute-start = (bf16[256,256]{1,0:T(8,128)(2,1)S(1)}, bf16[256,256]{1,0:T(8,128)(2,1)S(1)}, u32[]{:S(2)}, u32[]{:S(2)}) collective-permute-start(bf16[256,256]{1,0:T(8,128)(2,1)S(1)} %get-tuple-element.23.p0.fwd_ref), channel_id=1, source_target_pairs={{0,8},{8,0},{16,24},{24,16},{1,9},{9,1},{17,25},{25,17},{2,10},{10... | collective-permute-start | bytes 393224 | tf_op jit(solution)/shard_map/ppermute | solution.py:246
  12.1 3.1 %collective-permute-start.2 = (bf16[256,256]{1,0:T(8,128)(2,1)S(1)}, bf16[256,256]{1,0:T(8,128)(2,1)S(1)}, u32[]{:S(2)}, u32[]{:S(2)}) collective-permute-start(bf16[256,256]{1,0:T(8,128)(2,1)S(1)} %collective-permute-done.1.p2), channel_id=1, source_target_pairs={{0,8},{8,0},{16,24},{24,16},{1,9},{9,1},{17,25},{25,17},{2,10},{10... | collective-permute-start | bytes 393224 | tf_op jit(solution)/shard_map/ppermute | solution.py:246
  12.4 5.8 %collective-permute-start.17 = (bf16[256,256]{1,0:T(8,128)(2,1)S(1)}, bf16[256,256]{1,0:T(8,128)(2,1)S(1)}, u32[]{:S(2)}, u32[]{:S(2)}) collective-permute-start(bf16[256,256]{1,0:T(8,128)(2,1)S(1)} %first_lower.3), channel_id=1, source_target_pairs={{0,1},{1,0},{2,3},{3,2},{4,5},{5,4},{6,7},{7,6},{8,10},{9,11},{10,... | collective-permute-start | bytes 393224 | tf_op jit(solution)/shard_map/ppermute | solution.py:252
  14.8 7.6 %collective-permute-start.16 = (bf16[256,256]{1,0:T(8,128)(2,1)S(1)}, bf16[256,256]{1,0:T(8,128)(2,1)S(1)}, u32[]{:S(2)}, u32[]{:S(2)}) collective-permute-start(bf16[256,256]{1,0:T(8,128)(2,1)S(1)} %get-tuple-element.39), channel_id=1, source_target_pairs={{0,1},{1,0},{2,3},{3,2},{4,5},{5,4},{6,7},{7,6},{8,10},{9,11},{10,... | collective-permute-start | bytes 393224 | tf_op jit(solution)/shard_map/ppermute | solution.py:252
  15.5 5.1 %collective-permute-start.4 = (bf16[256,256]{1,0:T(8,128)(2,1)S(1)}, bf16[256,256]{1,0:T(8,128)(2,1)S(1)}, u32[]{:S(2)}, u32[]{:S(2)}) collective-permute-start(bf16[256,256]{1,0:T(8,128)(2,1)S(1)} %first_lower.2), channel_id=1, source_target_pairs={{0,2},{1,3},{2,0},{3,1},{4,6},{5,7},{6,4},{7,5},{8,9},{9,8},{10,11... | collective-permute-start | bytes 393224 | tf_op jit(solution)/shard_map/ppermute | solution.py:252
  17.9 13.9 %copy-start = (bf16[1024,512]{1,0:T(8,128)(2,1)S(1)}, bf16[1024,512]{1,0:T(8,128)(2,1)}, u32[]{:S(2)}) copy-start(bf16[1024,512]{1,0:T(8,128)(2,1)} %rhs_hbm.3) | copy-start | bytes 3145732
  17.9 13.9 %copy-start.2 = (bf16[8,128,128]{2,1,0:T(8,128)(2,1)S(1)}, bf16[8,128,128]{2,1,0:T(8,128)(2,1)}, u32[]{:S(2)}) copy-start(bf16[8,128,128]{2,1,0:T(8,128)(2,1)} %low_hbm.1) | copy-start | bytes 786436
  17.9 13.9 %copy-start.3 = (bf16[8,128,128]{2,1,0:T(8,128)(2,1)S(1)}, bf16[8,128,128]{2,1,0:T(8,128)(2,1)}, u32[]{:S(2)}) copy-start(bf16[8,128,128]{2,1,0:T(8,128)(2,1)} %up_hbm.1) | copy-start | bytes 786436
  17.9 9.7 %collective-permute-start.3 = (bf16[256,256]{1,0:T(8,128)(2,1)S(1)}, bf16[256,256]{1,0:T(8,128)(2,1)S(1)}, u32[]{:S(2)}, u32[]{:S(2)}) collective-permute-start(bf16[256,256]{1,0:T(8,128)(2,1)S(1)} %get-tuple-element.26), channel_id=1, source_target_pairs={{0,2},{1,3},{2,0},{3,1},{4,6},{5,7},{6,4},{7,5},{8,9},{9,8},{10,11... | collective-permute-start | bytes 393224 | tf_op jit(solution)/shard_map/ppermute | solution.py:252
  18.3 6.8 %collective-permute-start.18 = (bf16[256,256]{1,0:T(8,128)(2,1)S(1)}, bf16[256,256]{1,0:T(8,128)(2,1)S(1)}, u32[]{:S(2)}, u32[]{:S(2)}) collective-permute-start(bf16[256,256]{1,0:T(8,128)(2,1)S(1)} %add_convert_fusion.2), channel_id=1, source_target_pairs={{0,2},{1,3},{2,0},{3,1},{4,6},{5,7},{6,4},{7,5},{8,9},{9,8},{10,11... | collective-permute-start | bytes 393224 | tf_op jit(solution)/shard_map/ppermute | solution.py:252
  20.6 7.0 %collective-permute-start.5 = (bf16[256,256]{1,0:T(8,128)(2,1)S(1)}, bf16[256,256]{1,0:T(8,128)(2,1)S(1)}, u32[]{:S(2)}, u32[]{:S(2)}) collective-permute-start(bf16[256,256]{1,0:T(8,128)(2,1)S(1)} %add_convert_fusion.5), channel_id=1, source_target_pairs={{0,1},{1,0},{2,3},{3,2},{4,5},{5,4},{6,7},{7,6},{8,10},{9,11},{10,... | collective-permute-start | bytes 393224 | tf_op jit(solution)/shard_map/ppermute | solution.py:252
  25.1 11.8 %collective-permute-start.19 = (bf16[256,256]{1,0:T(8,128)(2,1)S(1)}, bf16[256,256]{1,0:T(8,128)(2,1)S(1)}, u32[]{:S(2)}, u32[]{:S(2)}) collective-permute-start(bf16[256,256]{1,0:T(8,128)(2,1)S(1)} %add_convert_fusion.1.mine_ref), channel_id=1, source_target_pairs={{0,4},{1,5},{2,6},{3,7},{4,0},{5,1},{6,2},{7,3},{8,12},{9,13},{10,... | collective-permute-start | bytes 393224 | tf_op jit(solution)/shard_map/ppermute | solution.py:246
  27.7 11.1 %collective-permute-start.6 = (bf16[256,256]{1,0:T(8,128)(2,1)S(1)}, bf16[256,256]{1,0:T(8,128)(2,1)S(1)}, u32[]{:S(2)}, u32[]{:S(2)}) collective-permute-start(bf16[256,256]{1,0:T(8,128)(2,1)S(1)} %add_convert_fusion.4.mine_ref), channel_id=1, source_target_pairs={{0,4},{1,5},{2,6},{3,7},{4,0},{5,1},{6,2},{7,3},{8,12},{9,13},{10,... | collective-permute-start | bytes 393224 | tf_op jit(solution)/shard_map/ppermute | solution.py:246
  37.3 6.3 %collective-permute-start.21 = (bf16[256,256]{1,0:T(8,128)(2,1)S(1)}, bf16[256,256]{1,0:T(8,128)(2,1)S(1)}, u32[]{:S(2)}, u32[]{:S(2)}) collective-permute-start(bf16[256,256]{1,0:T(8,128)(2,1)S(1)} %solve_top.3.p0), channel_id=1, source_target_pairs={{0,2},{1,3},{2,0},{3,1},{4,6},{5,7},{6,4},{7,5},{8,9},{9,8},{10,11... | collective-permute-start | bytes 393224 | tf_op jit(solution)/shard_map/ppermute | solution.py:252
  39.2 5.9 %collective-permute-start.7 = (bf16[256,256]{1,0:T(8,128)(2,1)S(1)}, bf16[256,256]{1,0:T(8,128)(2,1)S(1)}, u32[]{:S(2)}, u32[]{:S(2)}) collective-permute-start(bf16[256,256]{1,0:T(8,128)(2,1)S(1)} %solve_top.2.p0), channel_id=1, source_target_pairs={{0,1},{1,0},{2,3},{3,2},{4,5},{5,4},{6,7},{7,6},{8,10},{9,11},{10,... | collective-permute-start | bytes 393224 | tf_op jit(solution)/shard_map/ppermute | solution.py:252
  40.2 7.4 %collective-permute-start.20 = (bf16[256,256]{1,0:T(8,128)(2,1)S(1)}, bf16[256,256]{1,0:T(8,128)(2,1)S(1)}, u32[]{:S(2)}, u32[]{:S(2)}) collective-permute-start(bf16[256,256]{1,0:T(8,128)(2,1)S(1)} %solve_top.3.p0), channel_id=1, source_target_pairs={{0,1},{1,0},{2,3},{3,2},{4,5},{5,4},{6,7},{7,6},{8,10},{9,11},{10,... | collective-permute-start | bytes 393224 | tf_op jit(solution)/shard_map/ppermute | solution.py:252
  43.6 6.2 %collective-permute-start.22 = (bf16[256,256]{1,0:T(8,128)(2,1)S(1)}, bf16[256,256]{1,0:T(8,128)(2,1)S(1)}, u32[]{:S(2)}, u32[]{:S(2)}) collective-permute-start(bf16[256,256]{1,0:T(8,128)(2,1)S(1)} %collective-permute-done.21.p2), channel_id=1, source_target_pairs={{0,1},{1,0},{2,3},{3,2},{4,5},{5,4},{6,7},{7,6},{8,10},{9,11},{10,... | collective-permute-start | bytes 393224 | tf_op jit(solution)/shard_map/ppermute | solution.py:252
  44.8 6.6 %collective-permute-start.8 = (bf16[256,256]{1,0:T(8,128)(2,1)S(1)}, bf16[256,256]{1,0:T(8,128)(2,1)S(1)}, u32[]{:S(2)}, u32[]{:S(2)}) collective-permute-start(bf16[256,256]{1,0:T(8,128)(2,1)S(1)} %solve_top.2.p0), channel_id=1, source_target_pairs={{0,2},{1,3},{2,0},{3,1},{4,6},{5,7},{6,4},{7,5},{8,9},{9,8},{10,11... | collective-permute-start | bytes 393224 | tf_op jit(solution)/shard_map/ppermute | solution.py:252
  45.1 6.3 %collective-permute-start.9 = (bf16[256,256]{1,0:T(8,128)(2,1)S(1)}, bf16[256,256]{1,0:T(8,128)(2,1)S(1)}, u32[]{:S(2)}, u32[]{:S(2)}) collective-permute-start(bf16[256,256]{1,0:T(8,128)(2,1)S(1)} %collective-permute-done.7.p1), channel_id=1, source_target_pairs={{0,2},{1,3},{2,0},{3,1},{4,6},{5,7},{6,4},{7,5},{8,9},{9,8},{10,11... | collective-permute-start | bytes 393224 | tf_op jit(solution)/shard_map/ppermute | solution.py:252
  50.2 9.3 %copy-start.4 = (bf16[2,128,128]{2,1,0:T(8,128)(2,1)S(1)}, bf16[2,128,128]{2,1,0:T(8,128)(2,1)}, u32[]{:S(2)}) copy-start(bf16[2,128,128]{2,1,0:T(8,128)(2,1)} %inv_ref.3) | copy-start | bytes 196612
  50.2 2.8 %collective-permute-start.24 = (bf16[256,256]{1,0:T(8,128)(2,1)S(1)}, bf16[256,256]{1,0:T(8,128)(2,1)S(1)}, u32[]{:S(2)}, u32[]{:S(2)}) collective-permute-start(bf16[256,256]{1,0:T(8,128)(2,1)S(1)} %first_upper.3), channel_id=1, source_target_pairs={{0,8},{8,0},{16,24},{24,16},{1,9},{9,1},{17,25},{25,17},{2,10},{10... | collective-permute-start | bytes 393224 | tf_op jit(solution)/shard_map/ppermute | solution.py:246
  50.8 5.0 %collective-permute-start.23 = (bf16[256,256]{1,0:T(8,128)(2,1)S(1)}, bf16[256,256]{1,0:T(8,128)(2,1)S(1)}, u32[]{:S(2)}, u32[]{:S(2)}) collective-permute-start(bf16[256,256]{1,0:T(8,128)(2,1)S(1)} %get-tuple-element.42), channel_id=1, source_target_pairs={{0,8},{8,0},{16,24},{24,16},{1,9},{9,1},{17,25},{25,17},{2,10},{10... | collective-permute-start | bytes 393224 | tf_op jit(solution)/shard_map/ppermute | solution.py:246
  51.7 2.9 %collective-permute-start.11 = (bf16[256,256]{1,0:T(8,128)(2,1)S(1)}, bf16[256,256]{1,0:T(8,128)(2,1)S(1)}, u32[]{:S(2)}, u32[]{:S(2)}) collective-permute-start(bf16[256,256]{1,0:T(8,128)(2,1)S(1)} %first_upper.2), channel_id=1, source_target_pairs={{0,8},{8,0},{16,24},{24,16},{1,9},{9,1},{17,25},{25,17},{2,10},{10... | collective-permute-start | bytes 393224 | tf_op jit(solution)/shard_map/ppermute | solution.py:246
  52.4 7.9 %collective-permute-start.10 = (bf16[256,256]{1,0:T(8,128)(2,1)S(1)}, bf16[256,256]{1,0:T(8,128)(2,1)S(1)}, u32[]{:S(2)}, u32[]{:S(2)}) collective-permute-start(bf16[256,256]{1,0:T(8,128)(2,1)S(1)} %get-tuple-element.34), channel_id=1, source_target_pairs={{0,8},{8,0},{16,24},{24,16},{1,9},{9,1},{17,25},{25,17},{2,10},{10... | collective-permute-start | bytes 393224 | tf_op jit(solution)/shard_map/ppermute | solution.py:246
  53.0 6.4 %collective-permute-start.25 = (bf16[256,256]{1,0:T(8,128)(2,1)S(1)}, bf16[256,256]{1,0:T(8,128)(2,1)S(1)}, u32[]{:S(2)}, u32[]{:S(2)}) collective-permute-start(bf16[256,256]{1,0:T(8,128)(2,1)S(1)} %add_convert_fusion), channel_id=1, source_target_pairs={{0,16},{8,24},{16,0},{24,8},{1,17},{9,25},{17,1},{25,9},{2,18},{10... | collective-permute-start | bytes 393224 | tf_op jit(solution)/shard_map/ppermute | solution.py:246
  54.7 6.6 %collective-permute-start.12 = (bf16[256,256]{1,0:T(8,128)(2,1)S(1)}, bf16[256,256]{1,0:T(8,128)(2,1)S(1)}, u32[]{:S(2)}, u32[]{:S(2)}) collective-permute-start(bf16[256,256]{1,0:T(8,128)(2,1)S(1)} %add_convert_fusion.3), channel_id=1, source_target_pairs={{0,16},{8,24},{16,0},{24,8},{1,17},{9,25},{17,1},{25,9},{2,18},{10... | collective-permute-start | bytes 393224 | tf_op jit(solution)/shard_map/ppermute | solution.py:246

commit v4 on v3

--- a/solution.py
+++ b/solution.py
@@ -9,7 +9,7 @@
 
 BF = jnp.bfloat16
 F32 = jnp.float32
-FLIPS = (0, 1)
+FLIPS = (0, 0)
 MIB = 1 << 20
 
 
@@ -75,7 +75,7 @@
                     lanes = slice((m % own) * width, (m % own + 1) * width)
                     acc_ref[rel_row, pl.ds(at, width), lanes] += blk
                 else:
-                    at = (place_of(rel_row & 3, rel_row >> 2, rows) * own + m % own) * width
+                    at = ((((3 - rel_row) & 3) * (rows // 4) + (rel_row >> 2)) * own + m % own) * width
                     acc_ref[4 * high + low, pl.ds(pl.multiple_of(at, width), width), :] += blk
     for i in range(out_ref.shape[0]):
         out_ref[i] = acc_ref[i].astype(BF)
@@ -354,13 +354,19 @@
         if flip:
             one, two = two, one
         solved.append((zero, one, two, three))
+    begun, sent = [], []
+    for pieces in solved:
+        three, two = apply(upper_kernel, mat_u, pieces, 0, 2, "first_upper")
+        send = add(two, swap(three, "row", 0))
+        sent.append(send)
+        begun.append(swap(send, "row", 1))
     for i, pieces in enumerate(solved):
-        (three,) = apply(upper_kernel, mat_u, pieces, 0, 1, "first_upper")
-        one, two, zero = apply(upper_kernel, mat_u, pieces, 1, 4, "apply_upper")
-        got, rest = swap(three, "row", 0), swap(one, "row", 0)
-        more = swap(add(two, got), "row", 1)
-        terms = sums_row([zero, rest, more], own * width)
+        pieces = (after(pieces[0], *sent[:]), *pieces[1:])
+        one, zero = apply(upper_kernel, mat_u, pieces, 2, 4, "apply_upper")
+        part = zero.astype(F32) + begun[i].astype(F32)
+        terms = sums_row([part, swap(one, "row", 0)], own * width)
         sol_low = solve_low(inv_upper_low, fwds[i], terms, sol_low, i, len(FLIPS))
+    top_parts[0] = after(top_parts[0], *sent)
     return sol_low, jnp.concatenate(top_parts, axis=1)
 
 

time: 62.4 us -> 61.5 us (0.986)
  waiting for transfers between devices: 20.3 us -> 14.5 us
  starting transfers between devices: 23.5 us -> 28.3 us
    ppermute x14, waiting for transfers between devices: 11.5 us -> 7.42 us  [swap(): return lax.ppermute(x, axis, [(i, i ^ 1 << bit) for i in range(size)])]
    ppermute x14, starting transfers between devices: 10.5 us -> 13.4 us  [swap(): return lax.ppermute(x, axis, [(i, i ^ 1 << bit) for i in range(size)])]
    ppermute x12, starting transfers between devices: 13 us -> 14.9 us  [cross(): return lax.ppermute(x, ('row', 'col'), pairs)]
    ppermute x12, waiting for transfers between devices: 8.8 us -> 7.06 us  [cross(): return lax.ppermute(x, ('row', 'col'), pairs)]
  transfers between devices with their start and end apart: 26 -> 26, of which waited for: 11 -> 12; matrix products, arithmetic and copies ran while one was open for 2% -> 2% of each run, Pallas kernels for 21% -> 21%
where the time goes in v4:
time: 61.5 us; the launch traced here: 61.2 us
  starting transfers between devices  28.3 us (46%)
  waiting for transfers between devices  14.5 us (24%)
  Pallas kernels  13.9 us (23%)
  local copies, waits for them, and re-layouts  2.51 us (4%)
  other arithmetic  1.05 us (2%)
  between operations  0.95 us (2%)
    ppermute x12, starting transfers between devices, cross(): return lax.ppermute(x, ('row', 'col'), pairs)  14.9 us
    ppermute x14, starting transfers between devices, swap(): return lax.ppermute(x, axis, [(i, i ^ 1 << bit) for i in range(size)])  13.4 us
    ppermute x14, waiting for transfers between devices, swap(): return lax.ppermute(x, axis, [(i, i ^ 1 << bit) for i in range(size)])  7.42 us
    ppermute x12, waiting for transfers between devices, cross(): return lax.ppermute(x, ('row', 'col'), pairs)  7.06 us
    pallas_call x2, Pallas kernels, sum_blocks(): pl.pallas_call(functools.partial(sum_kernel, lower, rows, tops, own), in_...  6.57 us
    pallas_call x8, Pallas kernels, apply(): pl.pallas_call(functools.partial(kernel, begin), out_shape=[jax.ShapeDtyp...  3.5 us
    unnamed x14, local copies, waits for them, and re-layouts  2.49 us
    pallas_call x2, Pallas kernels, solve_low(): pl.pallas_call(functools.partial(low_kernel, len(terms)), grid=(1,), in_s...  1.73 us
  transfers between devices with their start and end apart: 26, of which 12 were waited for; matrix products, arithmetic and copies ran while one was open for 2% of the time, Pallas kernels for 21%

profile of v4, /device:TPU:0, one launch (start us, length us, event | category | flops | bytes accessed | tf_op | source)
XLA Modules:
  0.0 61.2 jit_solution(8340613613341453052)
XLA Ops:
  0.6 0.9 %copy-done.1 = bf16[256,512]{1,0:T(8,128)(2,1)S(1)} copy-done((bf16[256,512]{1,0:T(8,128)(2,1)S(1)}, bf16[256,512]{1,0:T(8,128)(2,1)}, u32[]{:S(2)}) %copy-start.1) | copy-done | bytes 262168
  1.6 0.8 %copy-done.5 = bf16[2,128,128]{2,1,0:T(8,128)(2,1)S(1)} copy-done((bf16[2,128,128]{2,1,0:T(8,128)(2,1)S(1)}, bf16[2,128,128]{2,1,0:T(8,128)(2,1)}, u32[]{:S(2)}) %copy-start.5) | copy-done | bytes 65560
  2.4 0.3 fwd_low.1
  2.7 3.0 %collective-permute-start.8 = (bf16[256,256]{1,0:T(8,128)(2,1)S(1)}, bf16[256,256]{1,0:T(8,128)(2,1)S(1)}, u32[]{:S(2)}, u32[]{:S(2)}) collective-permute-start(bf16[256,256]{1,0:T(8,128)(2,1)S(1)} %get-tuple-element.38.p0.fwd_ref), channel_id=1, source_target_pairs={{0,16},{8,24},{16,0},{24,8},{1,17},{9,25},{17,1},{25,9},{2,18},{10... | collective-permute-start | bytes 393224 | tf_op jit(solution)/shard_map/ppermute | solution.py:246
  6.0 0.7 %copy-done.6 = s32[16,8]{0,1:T(8,128)S(1)} copy-done((s32[16,8]{0,1:T(8,128)S(1)}, s32[16,8]{0,1:T(8,128)}, u32[]{:S(2)}) %copy-start.6) | copy-done | bytes 536
  6.7 3.3 %sum_lower.1.mat_ref = bf16[4,1024,256]{2,1,0:T(8,128)(2,1)S(1)} custom-call(s32[2]{0:T(128)S(1)} %pad_add_fusion.ids_ref, s32[8,16]{1,0:T(8,128)S(1)} %bitcast.3, bf16[16,8,128,128]{3,2,1,0:T(8,128)(2,1)} %blk_hbm.2), custom_call_target="tpu_custom_call" | custom-call | tf_op jit(solution)/shard_map/sum_lower/pallas_call | solution.py:88
  10.0 0.4 collective-permute-start.9
  10.6 1.5 %collective-permute-done.1.p2 = bf16[256,256]{1,0:T(8,128)(2,1)S(1)} collective-permute-done((bf16[256,256]{1,0:T(8,128)(2,1)S(1)}, bf16[256,256]{1,0:T(8,128)(2,1)S(1)}, u32[]{:S(2)}, u32[]{:S(2)}) %collective-permute-start.1) | collective-permute-done | bytes 131104 | tf_op jit(solution)/shard_map/ppermute | solution.py:246
  12.1 0.3 first_lower.3
  12.4 1.8 %collective-permute-start.11 = (bf16[256,256]{1,0:T(8,128)(2,1)S(1)}, bf16[256,256]{1,0:T(8,128)(2,1)S(1)}, u32[]{:S(2)}, u32[]{:S(2)}) collective-permute-start(bf16[256,256]{1,0:T(8,128)(2,1)S(1)} %first_lower.3), channel_id=1, source_target_pairs={{0,1},{1,0},{2,3},{3,2},{4,5},{5,4},{6,7},{7,6},{8,10},{9,11},{10,... | collective-permute-start | bytes 393224 | tf_op jit(solution)/shard_map/ppermute | solution.py:252
  14.2 0.6 apply_lower.3
  14.8 0.4 collective-permute-start.10
  15.1 0.3 first_lower.2
  15.5 1.8 %collective-permute-start.4 = (bf16[256,256]{1,0:T(8,128)(2,1)S(1)}, bf16[256,256]{1,0:T(8,128)(2,1)S(1)}, u32[]{:S(2)}, u32[]{:S(2)}) collective-permute-start(bf16[256,256]{1,0:T(8,128)(2,1)S(1)} %first_lower.2), channel_id=1, source_target_pairs={{0,1},{1,0},{2,3},{3,2},{4,5},{5,4},{6,7},{7,6},{8,10},{9,11},{10,... | collective-permute-start | bytes 393224 | tf_op jit(solution)/shard_map/ppermute | solution.py:252
  17.2 0.6 apply_lower.2
  17.9 0.4 collective-permute-start.3
  18.3 1.9 %collective-permute-start.12 = (bf16[256,256]{1,0:T(8,128)(2,1)S(1)}, bf16[256,256]{1,0:T(8,128)(2,1)S(1)}, u32[]{:S(2)}, u32[]{:S(2)}) collective-permute-start(bf16[256,256]{1,0:T(8,128)(2,1)S(1)} %add_convert_fusion.3), channel_id=1, source_target_pairs={{0,2},{1,3},{2,0},{3,1},{4,6},{5,7},{6,4},{7,5},{8,9},{9,8},{10,11... | collective-permute-start | bytes 393224 | tf_op jit(solution)/shard_map/ppermute | solution.py:252
  20.1 1.8 %collective-permute-done.4 = bf16[256,256]{1,0:T(8,128)(2,1)S(1)} collective-permute-done((bf16[256,256]{1,0:T(8,128)(2,1)S(1)}, bf16[256,256]{1,0:T(8,128)(2,1)S(1)}, u32[]{:S(2)}, u32[]{:S(2)}) %collective-permute-start.4) | collective-permute-done | bytes 131104 | tf_op jit(solution)/shard_map/ppermute | solution.py:252
  22.0 1.5 %collective-permute-start.5 = (bf16[256,256]{1,0:T(8,128)(2,1)S(1)}, bf16[256,256]{1,0:T(8,128)(2,1)S(1)}, u32[]{:S(2)}, u32[]{:S(2)}) collective-permute-start(bf16[256,256]{1,0:T(8,128)(2,1)S(1)} %add_convert_fusion.5), channel_id=1, source_target_pairs={{0,2},{1,3},{2,0},{3,1},{4,6},{5,7},{6,4},{7,5},{8,9},{9,8},{10,11... | collective-permute-start | bytes 393224 | tf_op jit(solution)/shard_map/ppermute | solution.py:252
  23.5 2.7 %collective-permute-start.13 = (bf16[256,256]{1,0:T(8,128)(2,1)S(1)}, bf16[256,256]{1,0:T(8,128)(2,1)S(1)}, u32[]{:S(2)}, u32[]{:S(2)}) collective-permute-start(bf16[256,256]{1,0:T(8,128)(2,1)S(1)} %add_convert_fusion.2.mine_ref), channel_id=1, source_target_pairs={{0,4},{1,5},{2,6},{3,7},{4,0},{5,1},{6,2},{7,3},{8,12},{9,13},{10,... | collective-permute-start | bytes 393224 | tf_op jit(solution)/shard_map/ppermute | solution.py:246
  26.3 0.8 %collective-permute-done.5 = bf16[256,256]{1,0:T(8,128)(2,1)S(1)} collective-permute-done((bf16[256,256]{1,0:T(8,128)(2,1)S(1)}, bf16[256,256]{1,0:T(8,128)(2,1)S(1)}, u32[]{:S(2)}, u32[]{:S(2)}) %collective-permute-start.5) | collective-permute-done | bytes 131104 | tf_op jit(solution)/shard_map/ppermute | solution.py:252
  27.1 3.3 %collective-permute-start.6 = (bf16[256,256]{1,0:T(8,128)(2,1)S(1)}, bf16[256,256]{1,0:T(8,128)(2,1)S(1)}, u32[]{:S(2)}, u32[]{:S(2)}) collective-permute-start(bf16[256,256]{1,0:T(8,128)(2,1)S(1)} %add_convert_fusion.4.mine_ref), channel_id=1, source_target_pairs={{0,4},{1,5},{2,6},{3,7},{4,0},{5,1},{6,2},{7,3},{8,12},{9,13},{10,... | collective-permute-start | bytes 393224 | tf_op jit(solution)/shard_map/ppermute | solution.py:246
  30.3 3.3 %sum_upper.1.mat_ref = bf16[8,1024,128]{2,1,0:T(8,128)(2,1)S(1)} custom-call(s32[2]{0:T(128)S(1)} %pad_add_fusion.ids_ref, s32[8,16]{1,0:T(8,128)S(1)} %bitcast.4, bf16[16,8,128,128]{3,2,1,0:T(8,128)(2,1)} %blk_hbm.3), custom_call_target="tpu_custom_call" | custom-call | tf_op jit(solution)/shard_map/sum_upper/pallas_call | solution.py:88
  33.7 1.1 %pick_top.1 = (bf16[256,512]{1,0:T(8,128)(2,1)S(1)}, bf16[2,128,128]{2,1,0:T(8,128)(2,1)S(1)}, bf16[2,128,128]{2,1,0:T(8,128)(2,1)S(1)}) custom-call(s32[2]{0:T(128)S(1)} %pad_add_fusion.ids_ref, bf16[1024,512]{1,0:T(8,128)(2,1)S(1)} %copy-done, bf16[8,128,128]{2,1,0:T(8,128)(2,1)S(1)} %copy-done.2, bf16[8,128,128]{2,1,0:T(8,128)(2,1)S(1)} %copy-done.3), custom_call_target="tpu_custom_call" | custom-call | tf_op jit(solution)/shard_map/pick_top/pallas_call | solution.py:127
  34.8 1.7 %collective-permute-done.13.got_ref = bf16[256,256]{1,0:T(8,128)(2,1)S(1)} collective-permute-done((bf16[256,256]{1,0:T(8,128)(2,1)S(1)}, bf16[256,256]{1,0:T(8,128)(2,1)S(1)}, u32[]{:S(2)}, u32[]{:S(2)}) %collective-permute-start.13) | collective-permute-done | bytes 131104 | tf_op jit(solution)/shard_map/ppermute | solution.py:246
  36.5 0.4 solve_top.3.p0
  36.9 1.4 %collective-permute-done.6.got_ref = bf16[256,256]{1,0:T(8,128)(2,1)S(1)} collective-permute-done((bf16[256,256]{1,0:T(8,128)(2,1)S(1)}, bf16[256,256]{1,0:T(8,128)(2,1)S(1)}, u32[]{:S(2)}, u32[]{:S(2)}) %collective-permute-start.6) | collective-permute-done | bytes 131104 | tf_op jit(solution)/shard_map/ppermute | solution.py:246
  38.3 0.4 solve_top.2.p0
  38.7 0.8 %collective-permute-start.19 = (bf16[256,256]{1,0:T(8,128)(2,1)S(1)}, bf16[256,256]{1,0:T(8,128)(2,1)S(1)}, u32[]{:S(2)}, u32[]{:S(2)}) collective-permute-start(bf16[256,256]{1,0:T(8,128)(2,1)S(1)} %solve_top.2.p0), channel_id=1, source_target_pairs={{0,2},{1,3},{2,0},{3,1},{4,6},{5,7},{6,4},{7,5},{8,9},{9,8},{10,11... | collective-permute-start | bytes 393224 | tf_op jit(solution)/shard_map/ppermute | solution.py:252
  39.5 1.5 %collective-permute-start.14 = (bf16[256,256]{1,0:T(8,128)(2,1)S(1)}, bf16[256,256]{1,0:T(8,128)(2,1)S(1)}, u32[]{:S(2)}, u32[]{:S(2)}) collective-permute-start(bf16[256,256]{1,0:T(8,128)(2,1)S(1)} %solve_top.3.p0), channel_id=1, source_target_pairs={{0,1},{1,0},{2,3},{3,2},{4,5},{5,4},{6,7},{7,6},{8,10},{9,11},{10,... | collective-permute-start | bytes 393224 | tf_op jit(solution)/shard_map/ppermute | solution.py:252
  40.9 1.1 %collective-permute-done.15.p2 = bf16[256,256]{1,0:T(8,128)(2,1)S(1)} collective-permute-done((bf16[256,256]{1,0:T(8,128)(2,1)S(1)}, bf16[256,256]{1,0:T(8,128)(2,1)S(1)}, u32[]{:S(2)}, u32[]{:S(2)}) %collective-permute-start.15) | collective-permute-done | bytes 131104 | tf_op jit(solution)/shard_map/ppermute | solution.py:252
  42.0 2.6 %collective-permute-start.16 = (bf16[256,256]{1,0:T(8,128)(2,1)S(1)}, bf16[256,256]{1,0:T(8,128)(2,1)S(1)}, u32[]{:S(2)}, u32[]{:S(2)}) collective-permute-start(bf16[256,256]{1,0:T(8,128)(2,1)S(1)} %collective-permute-done.15.p2), channel_id=1, source_target_pairs={{0,1},{1,0},{2,3},{3,2},{4,5},{5,4},{6,7},{7,6},{8,10},{9,11},{10,... | collective-permute-start | bytes 393224 | tf_op jit(solution)/shard_map/ppermute | solution.py:252
  44.6 0.4 collective-permute-done.19.p2
  45.1 2.3 %collective-permute-start.20 = (bf16[256,256]{1,0:T(8,128)(2,1)S(1)}, bf16[256,256]{1,0:T(8,128)(2,1)S(1)}, u32[]{:S(2)}, u32[]{:S(2)}) collective-permute-start(bf16[256,256]{1,0:T(8,128)(2,1)S(1)} %collective-permute-done.19.p2), channel_id=1, source_target_pairs={{0,1},{1,0},{2,3},{3,2},{4,5},{5,4},{6,7},{7,6},{8,10},{9,11},{10,... | collective-permute-start | bytes 393224 | tf_op jit(solution)/shard_map/ppermute | solution.py:252
  47.5 0.4 first_upper.2
  48.1 1.5 %collective-permute-done.18.p1 = bf16[256,256]{1,0:T(8,128)(2,1)S(1)} collective-permute-done((bf16[256,256]{1,0:T(8,128)(2,1)S(1)}, bf16[256,256]{1,0:T(8,128)(2,1)S(1)}, u32[]{:S(2)}, u32[]{:S(2)}) %collective-permute-start.18) | collective-permute-done | bytes 131104 | tf_op jit(solution)/shard_map/ppermute | solution.py:252
  49.6 1.4 %collective-permute-done.20.p3 = bf16[256,256]{1,0:T(8,128)(2,1)S(1)} collective-permute-done((bf16[256,256]{1,0:T(8,128)(2,1)S(1)}, bf16[256,256]{1,0:T(8,128)(2,1)S(1)}, u32[]{:S(2)}, u32[]{:S(2)}) %collective-permute-start.20) | collective-permute-done | bytes 131104 | tf_op jit(solution)/shard_map/ppermute | solution.py:252
  51.0 0.4 first_upper.3
  51.5 1.6 %collective-permute-start.24 = (bf16[256,256]{1,0:T(8,128)(2,1)S(1)}, bf16[256,256]{1,0:T(8,128)(2,1)S(1)}, u32[]{:S(2)}, u32[]{:S(2)}) collective-permute-start(bf16[256,256]{1,0:T(8,128)(2,1)S(1)} %add_convert_fusion.1), channel_id=1, source_target_pairs={{0,16},{8,24},{16,0},{24,8},{1,17},{9,25},{17,1},{25,9},{2,18},{10... | collective-permute-start | bytes 393224 | tf_op jit(solution)/shard_map/ppermute | solution.py:246
  53.2 1.3 %collective-permute-start.22 = (bf16[256,256]{1,0:T(8,128)(2,1)S(1)}, bf16[256,256]{1,0:T(8,128)(2,1)S(1)}, u32[]{:S(2)}, u32[]{:S(2)}) collective-permute-start(bf16[256,256]{1,0:T(8,128)(2,1)S(1)} %add_convert_fusion), channel_id=1, source_target_pairs={{0,16},{8,24},{16,0},{24,8},{1,17},{9,25},{17,1},{25,9},{2,18},{10... | collective-permute-start | bytes 393224 | tf_op jit(solution)/shard_map/ppermute | solution.py:246
  54.4 0.4 apply_upper.3
  55.0 0.4 apply_upper.2
  55.4 0.6 collective-permute-start.23
  55.9 0.7 %pad_maximum_fusion = bf16[128,512]{1,0:T(8,128)(2,1)} fusion(bf16[128,256]{1,0:T(8,128)(2,1)S(1)} %slice.9, bf16[128,256]{1,0:T(8,128)(2,1)S(1)} %slice.8), kind=kLoop, calls=%fused_computation.8 | loop fusion | flops 262144 | bytes 262144 | tf_op jit(solution)/shard_map/concatenate | solution.py:370
  56.6 1.3 %collective-permute-done.24 = bf16[256,256]{1,0:T(8,128)(2,1)S(1)} collective-permute-done((bf16[256,256]{1,0:T(8,128)(2,1)S(1)}, bf16[256,256]{1,0:T(8,128)(2,1)S(1)}, u32[]{:S(2)}, u32[]{:S(2)}) %collective-permute-start.24) | collective-permute-done | bytes 131104 | tf_op jit(solution)/shard_map/ppermute | solution.py:246
  58.0 0.9 %solve_low.2.refs_2_ = bf16[256,512]{1,0:T(8,128)(2,1)} custom-call(bf16[2,128,128]{2,1,0:T(8,128)(2,1)S(1)} %copy-done.4, bf16[256,256]{1,0:T(8,128)(2,1)S(1)} %get-tuple-element.38.p0.fwd_ref, f32[256,256]{1,0:T(8,128)S(1)} %convert_add_fusion.refs_0_, bf16[256,256]{1,0:T(8,128)(2,1)S(1)} %collective-permute-done.25.refs_1_), custom_call_target="tpu_custom_call" | custom-call | tf_op jit(solution)/shard_map/solve_low/pallas_call | solution.py:227
  58.8 1.5 %collective-permute-done.22 = bf16[256,256]{1,0:T(8,128)(2,1)S(1)} collective-permute-done((bf16[256,256]{1,0:T(8,128)(2,1)S(1)}, bf16[256,256]{1,0:T(8,128)(2,1)S(1)}, u32[]{:S(2)}, u32[]{:S(2)}) %collective-permute-start.22) | collective-permute-done | bytes 131104 | tf_op jit(solution)/shard_map/ppermute | solution.py:246
  60.4 0.9 %solve_low.3 = bf16[256,512]{1,0:T(8,128)(2,1)} custom-call(bf16[2,128,128]{2,1,0:T(8,128)(2,1)S(1)} %copy-done.4, bf16[256,256]{1,0:T(8,128)(2,1)S(1)} %get-tuple-element.28.p0.fwd_ref, f32[256,256]{1,0:T(8,128)S(1)} %convert_add_fusion.1.refs_0_, bf16[256,256]{1,0:T(8,128)(2,1)S(1)} %collective-permute-done.23.refs_1_, ...), custom_call_target="tpu_custom_call", output_to_operand_aliasing={{}: (4, {})} | custom-call | tf_op jit(solution)/shard_map/solve_low/pallas_call | solution.py:227
  (46 shorter events, 1.2 us)
Async XLA Ops:
  0.6 1.0 %copy-start.1 = (bf16[256,512]{1,0:T(8,128)(2,1)S(1)}, bf16[256,512]{1,0:T(8,128)(2,1)}, u32[]{:S(2)}) copy-start(bf16[256,512]{1,0:T(8,128)(2,1)} %rhs_hbm.2) | copy-start | bytes 786436
  1.6 0.8 %copy-start.5 = (bf16[2,128,128]{2,1,0:T(8,128)(2,1)S(1)}, bf16[2,128,128]{2,1,0:T(8,128)(2,1)}, u32[]{:S(2)}) copy-start(bf16[2,128,128]{2,1,0:T(8,128)(2,1)} %inv_hbm.1) | copy-start | bytes 196612
  2.7 7.2 %collective-permute-start.8 = (bf16[256,256]{1,0:T(8,128)(2,1)S(1)}, bf16[256,256]{1,0:T(8,128)(2,1)S(1)}, u32[]{:S(2)}, u32[]{:S(2)}) collective-permute-start(bf16[256,256]{1,0:T(8,128)(2,1)S(1)} %get-tuple-element.38.p0.fwd_ref), channel_id=1, source_target_pairs={{0,16},{8,24},{16,0},{24,8},{1,17},{9,25},{17,1},{25,9},{2,18},{10... | collective-permute-start | bytes 393224 | tf_op jit(solution)/shard_map/ppermute | solution.py:246
  5.8 6.3 %collective-permute-start.7 = (bf16[256,256]{1,0:T(8,128)(2,1)S(1)}, bf16[256,256]{1,0:T(8,128)(2,1)S(1)}, u32[]{:S(2)}, u32[]{:S(2)}) collective-permute-start(bf16[256,256]{1,0:T(8,128)(2,1)S(1)} %get-tuple-element.38.p0.fwd_ref), channel_id=1, source_target_pairs={{0,8},{8,0},{16,24},{24,16},{1,9},{9,1},{17,25},{25,17},{2,10},{10... | collective-permute-start | bytes 393224 | tf_op jit(solution)/shard_map/ppermute | solution.py:246
  5.8 6.3 %collective-permute-start.1 = (bf16[256,256]{1,0:T(8,128)(2,1)S(1)}, bf16[256,256]{1,0:T(8,128)(2,1)S(1)}, u32[]{:S(2)}, u32[]{:S(2)}) collective-permute-start(bf16[256,256]{1,0:T(8,128)(2,1)S(1)} %get-tuple-element.28.p0.fwd_ref), channel_id=1, source_target_pairs={{0,16},{8,24},{16,0},{24,8},{1,17},{9,25},{17,1},{25,9},{2,18},{10... | collective-permute-start | bytes 393224 | tf_op jit(solution)/shard_map/ppermute | solution.py:246
  6.0 0.7 %copy-start.6 = (s32[16,8]{0,1:T(8,128)S(1)}, s32[16,8]{0,1:T(8,128)}, u32[]{:S(2)}) copy-start(s32[16,8]{0,1:T(8,128)} %param.13) | copy-start | bytes 1540
  10.0 2.1 %collective-permute-start.9 = (bf16[256,256]{1,0:T(8,128)(2,1)S(1)}, bf16[256,256]{1,0:T(8,128)(2,1)S(1)}, u32[]{:S(2)}, u32[]{:S(2)}) collective-permute-start(bf16[256,256]{1,0:T(8,128)(2,1)S(1)} %collective-permute-done.8.p2), channel_id=1, source_target_pairs={{0,8},{8,0},{16,24},{24,16},{1,9},{9,1},{17,25},{25,17},{2,10},{10... | collective-permute-start | bytes 393224 | tf_op jit(solution)/shard_map/ppermute | solution.py:246
  10.4 4.7 %collective-permute-start = (bf16[256,256]{1,0:T(8,128)(2,1)S(1)}, bf16[256,256]{1,0:T(8,128)(2,1)S(1)}, u32[]{:S(2)}, u32[]{:S(2)}) collective-permute-start(bf16[256,256]{1,0:T(8,128)(2,1)S(1)} %get-tuple-element.28.p0.fwd_ref), channel_id=1, source_target_pairs={{0,8},{8,0},{16,24},{24,16},{1,9},{9,1},{17,25},{25,17},{2,10},{10... | collective-permute-start | bytes 393224 | tf_op jit(solution)/shard_map/ppermute | solution.py:246
  12.1 3.1 %collective-permute-start.2 = (bf16[256,256]{1,0:T(8,128)(2,1)S(1)}, bf16[256,256]{1,0:T(8,128)(2,1)S(1)}, u32[]{:S(2)}, u32[]{:S(2)}) collective-permute-start(bf16[256,256]{1,0:T(8,128)(2,1)S(1)} %collective-permute-done.1.p2), channel_id=1, source_target_pairs={{0,8},{8,0},{16,24},{24,16},{1,9},{9,1},{17,25},{25,17},{2,10},{10... | collective-permute-start | bytes 393224 | tf_op jit(solution)/shard_map/ppermute | solution.py:246
  12.4 5.8 %collective-permute-start.11 = (bf16[256,256]{1,0:T(8,128)(2,1)S(1)}, bf16[256,256]{1,0:T(8,128)(2,1)S(1)}, u32[]{:S(2)}, u32[]{:S(2)}) collective-permute-start(bf16[256,256]{1,0:T(8,128)(2,1)S(1)} %first_lower.3), channel_id=1, source_target_pairs={{0,1},{1,0},{2,3},{3,2},{4,5},{5,4},{6,7},{7,6},{8,10},{9,11},{10,... | collective-permute-start | bytes 393224 | tf_op jit(solution)/shard_map/ppermute | solution.py:252
  14.8 8.7 %collective-permute-start.10 = (bf16[256,256]{1,0:T(8,128)(2,1)S(1)}, bf16[256,256]{1,0:T(8,128)(2,1)S(1)}, u32[]{:S(2)}, u32[]{:S(2)}) collective-permute-start(bf16[256,256]{1,0:T(8,128)(2,1)S(1)} %get-tuple-element.41), channel_id=1, source_target_pairs={{0,1},{1,0},{2,3},{3,2},{4,5},{5,4},{6,7},{7,6},{8,10},{9,11},{10,... | collective-permute-start | bytes 393224 | tf_op jit(solution)/shard_map/ppermute | solution.py:252
  15.5 6.5 %collective-permute-start.4 = (bf16[256,256]{1,0:T(8,128)(2,1)S(1)}, bf16[256,256]{1,0:T(8,128)(2,1)S(1)}, u32[]{:S(2)}, u32[]{:S(2)}) collective-permute-start(bf16[256,256]{1,0:T(8,128)(2,1)S(1)} %first_lower.2), channel_id=1, source_target_pairs={{0,1},{1,0},{2,3},{3,2},{4,5},{5,4},{6,7},{7,6},{8,10},{9,11},{10,... | collective-permute-start | bytes 393224 | tf_op jit(solution)/shard_map/ppermute | solution.py:252
  17.8 15.8 %copy-start = (bf16[1024,512]{1,0:T(8,128)(2,1)S(1)}, bf16[1024,512]{1,0:T(8,128)(2,1)}, u32[]{:S(2)}) copy-start(bf16[1024,512]{1,0:T(8,128)(2,1)} %rhs_hbm.3) | copy-start | bytes 3145732
  17.8 15.8 %copy-start.2 = (bf16[8,128,128]{2,1,0:T(8,128)(2,1)S(1)}, bf16[8,128,128]{2,1,0:T(8,128)(2,1)}, u32[]{:S(2)}) copy-start(bf16[8,128,128]{2,1,0:T(8,128)(2,1)} %low_hbm.1) | copy-start | bytes 786436
  17.9 15.8 %copy-start.3 = (bf16[8,128,128]{2,1,0:T(8,128)(2,1)S(1)}, bf16[8,128,128]{2,1,0:T(8,128)(2,1)}, u32[]{:S(2)}) copy-start(bf16[8,128,128]{2,1,0:T(8,128)(2,1)} %up_hbm.1) | copy-start | bytes 786436
  17.9 8.4 %collective-permute-start.3 = (bf16[256,256]{1,0:T(8,128)(2,1)S(1)}, bf16[256,256]{1,0:T(8,128)(2,1)S(1)}, u32[]{:S(2)}, u32[]{:S(2)}) collective-permute-start(bf16[256,256]{1,0:T(8,128)(2,1)S(1)} %get-tuple-element.31), channel_id=1, source_target_pairs={{0,1},{1,0},{2,3},{3,2},{4,5},{5,4},{6,7},{7,6},{8,10},{9,11},{10,... | collective-permute-start | bytes 393224 | tf_op jit(solution)/shard_map/ppermute | solution.py:252
  18.3 5.2 %collective-permute-start.12 = (bf16[256,256]{1,0:T(8,128)(2,1)S(1)}, bf16[256,256]{1,0:T(8,128)(2,1)S(1)}, u32[]{:S(2)}, u32[]{:S(2)}) collective-permute-start(bf16[256,256]{1,0:T(8,128)(2,1)S(1)} %add_convert_fusion.3), channel_id=1, source_target_pairs={{0,2},{1,3},{2,0},{3,1},{4,6},{5,7},{6,4},{7,5},{8,9},{9,8},{10,11... | collective-permute-start | bytes 393224 | tf_op jit(solution)/shard_map/ppermute | solution.py:252
  22.0 5.0 %collective-permute-start.5 = (bf16[256,256]{1,0:T(8,128)(2,1)S(1)}, bf16[256,256]{1,0:T(8,128)(2,1)S(1)}, u32[]{:S(2)}, u32[]{:S(2)}) collective-permute-start(bf16[256,256]{1,0:T(8,128)(2,1)S(1)} %add_convert_fusion.5), channel_id=1, source_target_pairs={{0,2},{1,3},{2,0},{3,1},{4,6},{5,7},{6,4},{7,5},{8,9},{9,8},{10,11... | collective-permute-start | bytes 393224 | tf_op jit(solution)/shard_map/ppermute | solution.py:252
  23.5 12.9 %collective-permute-start.13 = (bf16[256,256]{1,0:T(8,128)(2,1)S(1)}, bf16[256,256]{1,0:T(8,128)(2,1)S(1)}, u32[]{:S(2)}, u32[]{:S(2)}) collective-permute-start(bf16[256,256]{1,0:T(8,128)(2,1)S(1)} %add_convert_fusion.2.mine_ref), channel_id=1, source_target_pairs={{0,4},{1,5},{2,6},{3,7},{4,0},{5,1},{6,2},{7,3},{8,12},{9,13},{10,... | collective-permute-start | bytes 393224 | tf_op jit(solution)/shard_map/ppermute | solution.py:246
  27.1 11.3 %collective-permute-start.6 = (bf16[256,256]{1,0:T(8,128)(2,1)S(1)}, bf16[256,256]{1,0:T(8,128)(2,1)S(1)}, u32[]{:S(2)}, u32[]{:S(2)}) collective-permute-start(bf16[256,256]{1,0:T(8,128)(2,1)S(1)} %add_convert_fusion.4.mine_ref), channel_id=1, source_target_pairs={{0,4},{1,5},{2,6},{3,7},{4,0},{5,1},{6,2},{7,3},{8,12},{9,13},{10,... | collective-permute-start | bytes 393224 | tf_op jit(solution)/shard_map/ppermute | solution.py:246
  36.8 5.2 %collective-permute-start.15 = (bf16[256,256]{1,0:T(8,128)(2,1)S(1)}, bf16[256,256]{1,0:T(8,128)(2,1)S(1)}, u32[]{:S(2)}, u32[]{:S(2)}) collective-permute-start(bf16[256,256]{1,0:T(8,128)(2,1)S(1)} %solve_top.3.p0), channel_id=1, source_target_pairs={{0,2},{1,3},{2,0},{3,1},{4,6},{5,7},{6,4},{7,5},{8,9},{9,8},{10,11... | collective-permute-start | bytes 393224 | tf_op jit(solution)/shard_map/ppermute | solution.py:252
  38.7 6.4 %collective-permute-start.19 = (bf16[256,256]{1,0:T(8,128)(2,1)S(1)}, bf16[256,256]{1,0:T(8,128)(2,1)S(1)}, u32[]{:S(2)}, u32[]{:S(2)}) collective-permute-start(bf16[256,256]{1,0:T(8,128)(2,1)S(1)} %solve_top.2.p0), channel_id=1, source_target_pairs={{0,2},{1,3},{2,0},{3,1},{4,6},{5,7},{6,4},{7,5},{8,9},{9,8},{10,11... | collective-permute-start | bytes 393224 | tf_op jit(solution)/shard_map/ppermute | solution.py:252
  39.5 7.9 %collective-permute-start.14 = (bf16[256,256]{1,0:T(8,128)(2,1)S(1)}, bf16[256,256]{1,0:T(8,128)(2,1)S(1)}, u32[]{:S(2)}, u32[]{:S(2)}) collective-permute-start(bf16[256,256]{1,0:T(8,128)(2,1)S(1)} %solve_top.3.p0), channel_id=1, source_target_pairs={{0,1},{1,0},{2,3},{3,2},{4,5},{5,4},{6,7},{7,6},{8,10},{9,11},{10,... | collective-permute-start | bytes 393224 | tf_op jit(solution)/shard_map/ppermute | solution.py:252
  42.0 5.5 %collective-permute-start.16 = (bf16[256,256]{1,0:T(8,128)(2,1)S(1)}, bf16[256,256]{1,0:T(8,128)(2,1)S(1)}, u32[]{:S(2)}, u32[]{:S(2)}) collective-permute-start(bf16[256,256]{1,0:T(8,128)(2,1)S(1)} %collective-permute-done.15.p2), channel_id=1, source_target_pairs={{0,1},{1,0},{2,3},{3,2},{4,5},{5,4},{6,7},{7,6},{8,10},{9,11},{10,... | collective-permute-start | bytes 393224 | tf_op jit(solution)/shard_map/ppermute | solution.py:252
  44.6 5.0 %collective-permute-start.18 = (bf16[256,256]{1,0:T(8,128)(2,1)S(1)}, bf16[256,256]{1,0:T(8,128)(2,1)S(1)}, u32[]{:S(2)}, u32[]{:S(2)}) collective-permute-start(bf16[256,256]{1,0:T(8,128)(2,1)S(1)} %solve_top.2.p0), channel_id=1, source_target_pairs={{0,1},{1,0},{2,3},{3,2},{4,5},{5,4},{6,7},{7,6},{8,10},{9,11},{10,... | collective-permute-start | bytes 393224 | tf_op jit(solution)/shard_map/ppermute | solution.py:252
  45.1 5.9 %collective-permute-start.20 = (bf16[256,256]{1,0:T(8,128)(2,1)S(1)}, bf16[256,256]{1,0:T(8,128)(2,1)S(1)}, u32[]{:S(2)}, u32[]{:S(2)}) collective-permute-start(bf16[256,256]{1,0:T(8,128)(2,1)S(1)} %collective-permute-done.19.p2), channel_id=1, source_target_pairs={{0,1},{1,0},{2,3},{3,2},{4,5},{5,4},{6,7},{7,6},{8,10},{9,11},{10,... | collective-permute-start | bytes 393224 | tf_op jit(solution)/shard_map/ppermute | solution.py:252
  48.0 3.5 %collective-permute-start.17 = (bf16[256,256]{1,0:T(8,128)(2,1)S(1)}, bf16[256,256]{1,0:T(8,128)(2,1)S(1)}, u32[]{:S(2)}, u32[]{:S(2)}) collective-permute-start(bf16[256,256]{1,0:T(8,128)(2,1)S(1)} %get-tuple-element.44), channel_id=1, source_target_pairs={{0,8},{8,0},{16,24},{24,16},{1,9},{9,1},{17,25},{25,17},{2,10},{10... | collective-permute-start | bytes 393224 | tf_op jit(solution)/shard_map/ppermute | solution.py:246
  48.1 9.9 %copy-start.4 = (bf16[2,128,128]{2,1,0:T(8,128)(2,1)S(1)}, bf16[2,128,128]{2,1,0:T(8,128)(2,1)}, u32[]{:S(2)}) copy-start(bf16[2,128,128]{2,1,0:T(8,128)(2,1)} %inv_ref.3) | copy-start | bytes 196612
  51.4 1.7 %collective-permute-start.21 = (bf16[256,256]{1,0:T(8,128)(2,1)S(1)}, bf16[256,256]{1,0:T(8,128)(2,1)S(1)}, u32[]{:S(2)}, u32[]{:S(2)}) collective-permute-start(bf16[256,256]{1,0:T(8,128)(2,1)S(1)} %get-tuple-element.46), channel_id=1, source_target_pairs={{0,8},{8,0},{16,24},{24,16},{1,9},{9,1},{17,25},{25,17},{2,10},{10... | collective-permute-start | bytes 393224 | tf_op jit(solution)/shard_map/ppermute | solution.py:246
  51.5 6.4 %collective-permute-start.24 = (bf16[256,256]{1,0:T(8,128)(2,1)S(1)}, bf16[256,256]{1,0:T(8,128)(2,1)S(1)}, u32[]{:S(2)}, u32[]{:S(2)}) collective-permute-start(bf16[256,256]{1,0:T(8,128)(2,1)S(1)} %add_convert_fusion.1), channel_id=1, source_target_pairs={{0,16},{8,24},{16,0},{24,8},{1,17},{9,25},{17,1},{25,9},{2,18},{10... | collective-permute-start | bytes 393224 | tf_op jit(solution)/shard_map/ppermute | solution.py:246
  53.2 7.2 %collective-permute-start.22 = (bf16[256,256]{1,0:T(8,128)(2,1)S(1)}, bf16[256,256]{1,0:T(8,128)(2,1)S(1)}, u32[]{:S(2)}, u32[]{:S(2)}) collective-permute-start(bf16[256,256]{1,0:T(8,128)(2,1)S(1)} %add_convert_fusion), channel_id=1, source_target_pairs={{0,16},{8,24},{16,0},{24,8},{1,17},{9,25},{17,1},{25,9},{2,18},{10... | collective-permute-start | bytes 393224 | tf_op jit(solution)/shard_map/ppermute | solution.py:246
  54.9 3.1 %collective-permute-start.25 = (bf16[256,256]{1,0:T(8,128)(2,1)S(1)}, bf16[256,256]{1,0:T(8,128)(2,1)S(1)}, u32[]{:S(2)}, u32[]{:S(2)}) collective-permute-start(bf16[256,256]{1,0:T(8,128)(2,1)S(1)} %get-tuple-element.52), channel_id=1, source_target_pairs={{0,8},{8,0},{16,24},{24,16},{1,9},{9,1},{17,25},{25,17},{2,10},{10... | collective-permute-start | bytes 393224 | tf_op jit(solution)/shard_map/ppermute | solution.py:246
  55.4 5.0 %collective-permute-start.23 = (bf16[256,256]{1,0:T(8,128)(2,1)S(1)}, bf16[256,256]{1,0:T(8,128)(2,1)S(1)}, u32[]{:S(2)}, u32[]{:S(2)}) collective-permute-start(bf16[256,256]{1,0:T(8,128)(2,1)S(1)} %get-tuple-element.49), channel_id=1, source_target_pairs={{0,8},{8,0},{16,24},{24,16},{1,9},{9,1},{17,25},{25,17},{2,10},{10... | collective-permute-start | bytes 393224 | tf_op jit(solution)/shard_map/ppermute | solution.py:246

commit v5 on v4

--- a/solution.py
+++ b/solution.py
@@ -350,20 +350,20 @@
         zero = widen_col(both, width)
         two = cross(zero, 1, flip)
         one = cross(zero, 0, flip)
-        three = cross(two, 0, flip)
+        three = cross(after(two, one), 0, flip)
         if flip:
             one, two = two, one
         solved.append((zero, one, two, three))
     begun, sent = [], []
     for pieces in solved:
         three, two = apply(upper_kernel, mat_u, pieces, 0, 2, "first_upper")
-        send = add(two, swap(three, "row", 0))
+        send = add(two, after(swap(three, "row", 0), *begun))
         sent.append(send)
-        begun.append(swap(send, "row", 1))
+        begun.append(swap(send, "row", 1).astype(F32))
     for i, pieces in enumerate(solved):
-        pieces = (after(pieces[0], *sent[:]), *pieces[1:])
+        pieces = (after(pieces[0], *sent[: i + 1]), *pieces[1:])
         one, zero = apply(upper_kernel, mat_u, pieces, 2, 4, "apply_upper")
-        part = zero.astype(F32) + begun[i].astype(F32)
+        part = zero.astype(F32) + begun[i]
         terms = sums_row([part, swap(one, "row", 0)], own * width)
         sol_low = solve_low(inv_upper_low, fwds[i], terms, sol_low, i, len(FLIPS))
     top_parts[0] = after(top_parts[0], *sent)

time: 61.5 us -> 61.3 us (level)
  starting transfers between devices: 28.3 us -> 27.2 us
  waiting for transfers between devices: 14.5 us -> 15.5 us
    ppermute x12, waiting for transfers between devices: 7.06 us -> 7.99 us  [cross(): return lax.ppermute(x, ('row', 'col'), pairs)]
    ppermute x14, starting transfers between devices: 13.4 us -> 12.4 us  [swap(): return lax.ppermute(x, axis, [(i, i ^ 1 << bit) for i in range(size)])]
  transfers between devices with their start and end apart: 26 -> 26, of which waited for: 12 -> 13; matrix products, arithmetic and copies ran while one was open for 2% -> 2% of each run, Pallas kernels for 21% -> 21%
where the time goes in v5:
time: 61.3 us; the launch traced here: 61.1 us
  starting transfers between devices  27.2 us (44%)
  waiting for transfers between devices  15.5 us (25%)
  Pallas kernels  13.9 us (23%)
  local copies, waits for them, and re-layouts  2.51 us (4%)
  other arithmetic  1.05 us (2%)
  between operations  0.95 us (2%)
    ppermute x12, starting transfers between devices, cross(): return lax.ppermute(x, ('row', 'col'), pairs)  14.7 us
    ppermute x14, starting transfers between devices, swap(): return lax.ppermute(x, axis, [(i, i ^ 1 << bit) for i in range(size)])  12.4 us
    ppermute x12, waiting for transfers between devices, cross(): return lax.ppermute(x, ('row', 'col'), pairs)  7.99 us
    ppermute x14, waiting for transfers between devices, swap(): return lax.ppermute(x, axis, [(i, i ^ 1 << bit) for i in range(size)])  7.51 us
    pallas_call x2, Pallas kernels, sum_blocks(): pl.pallas_call(functools.partial(sum_kernel, lower, rows, tops, own), in_...  6.57 us
    pallas_call x8, Pallas kernels, apply(): pl.pallas_call(functools.partial(kernel, begin), out_shape=[jax.ShapeDtyp...  3.49 us
    unnamed x14, local copies, waits for them, and re-layouts  2.49 us
    pallas_call x2, Pallas kernels, solve_low(): pl.pallas_call(functools.partial(low_kernel, len(terms)), grid=(1,), in_s...  1.73 us
  transfers between devices with their start and end apart: 26, of which 13 were waited for; matrix products, arithmetic and copies ran while one was open for 2% of the time, Pallas kernels for 21%

profile of v5, /device:TPU:0, one launch (start us, length us, event | category | flops | bytes accessed | tf_op | source)
XLA Modules:
  0.0 61.1 jit_solution(2844896796636586055)
XLA Ops:
  0.6 0.9 %copy-done.1 = bf16[256,512]{1,0:T(8,128)(2,1)S(1)} copy-done((bf16[256,512]{1,0:T(8,128)(2,1)S(1)}, bf16[256,512]{1,0:T(8,128)(2,1)}, u32[]{:S(2)}) %copy-start.1) | copy-done | bytes 262168
  1.6 0.8 %copy-done.5 = bf16[2,128,128]{2,1,0:T(8,128)(2,1)S(1)} copy-done((bf16[2,128,128]{2,1,0:T(8,128)(2,1)S(1)}, bf16[2,128,128]{2,1,0:T(8,128)(2,1)}, u32[]{:S(2)}) %copy-start.5) | copy-done | bytes 65560
  2.4 0.3 fwd_low.1
  2.7 3.0 %collective-permute-start.8 = (bf16[256,256]{1,0:T(8,128)(2,1)S(1)}, bf16[256,256]{1,0:T(8,128)(2,1)S(1)}, u32[]{:S(2)}, u32[]{:S(2)}) collective-permute-start(bf16[256,256]{1,0:T(8,128)(2,1)S(1)} %get-tuple-element.41.p0.fwd_ref), channel_id=1, source_target_pairs={{0,16},{8,24},{16,0},{24,8},{1,17},{9,25},{17,1},{25,9},{2,18},{10... | collective-permute-start | bytes 393224 | tf_op jit(solution)/shard_map/ppermute | solution.py:246
  6.0 0.7 %copy-done.6 = s32[16,8]{0,1:T(8,128)S(1)} copy-done((s32[16,8]{0,1:T(8,128)S(1)}, s32[16,8]{0,1:T(8,128)}, u32[]{:S(2)}) %copy-start.6) | copy-done | bytes 536
  6.7 3.3 %sum_lower.1.mat_ref = bf16[4,1024,256]{2,1,0:T(8,128)(2,1)S(1)} custom-call(s32[2]{0:T(128)S(1)} %pad_add_fusion.ids_ref, s32[8,16]{1,0:T(8,128)S(1)} %bitcast.3, bf16[16,8,128,128]{3,2,1,0:T(8,128)(2,1)} %blk_hbm.2), custom_call_target="tpu_custom_call" | custom-call | tf_op jit(solution)/shard_map/sum_lower/pallas_call | solution.py:88
  10.0 0.4 collective-permute-start.9
  10.6 1.5 %collective-permute-done.1.p2 = bf16[256,256]{1,0:T(8,128)(2,1)S(1)} collective-permute-done((bf16[256,256]{1,0:T(8,128)(2,1)S(1)}, bf16[256,256]{1,0:T(8,128)(2,1)S(1)}, u32[]{:S(2)}, u32[]{:S(2)}) %collective-permute-start.1) | collective-permute-done | bytes 131104 | tf_op jit(solution)/shard_map/ppermute | solution.py:246
  12.4 1.8 %collective-permute-start.11 = (bf16[256,256]{1,0:T(8,128)(2,1)S(1)}, bf16[256,256]{1,0:T(8,128)(2,1)S(1)}, u32[]{:S(2)}, u32[]{:S(2)}) collective-permute-start(bf16[256,256]{1,0:T(8,128)(2,1)S(1)} %first_lower.3), channel_id=1, source_target_pairs={{0,1},{1,0},{2,3},{3,2},{4,5},{5,4},{6,7},{7,6},{8,10},{9,11},{10,... | collective-permute-start | bytes 393224 | tf_op jit(solution)/shard_map/ppermute | solution.py:252
  14.2 0.6 apply_lower.2
  14.8 1.0 %collective-permute-start.3 = (bf16[256,256]{1,0:T(8,128)(2,1)S(1)}, bf16[256,256]{1,0:T(8,128)(2,1)S(1)}, u32[]{:S(2)}, u32[]{:S(2)}) collective-permute-start(bf16[256,256]{1,0:T(8,128)(2,1)S(1)} %get-tuple-element.34), channel_id=1, source_target_pairs={{0,1},{1,0},{2,3},{3,2},{4,5},{5,4},{6,7},{7,6},{8,10},{9,11},{10,... | collective-permute-start | bytes 393224 | tf_op jit(solution)/shard_map/ppermute | solution.py:252
  16.1 1.1 %collective-permute-start.4 = (bf16[256,256]{1,0:T(8,128)(2,1)S(1)}, bf16[256,256]{1,0:T(8,128)(2,1)S(1)}, u32[]{:S(2)}, u32[]{:S(2)}) collective-permute-start(bf16[256,256]{1,0:T(8,128)(2,1)S(1)} %first_lower.2), channel_id=1, source_target_pairs={{0,1},{1,0},{2,3},{3,2},{4,5},{5,4},{6,7},{7,6},{8,10},{9,11},{10,... | collective-permute-start | bytes 393224 | tf_op jit(solution)/shard_map/ppermute | solution.py:252
  17.2 0.6 apply_lower.3
  17.9 1.0 %collective-permute-start.10 = (bf16[256,256]{1,0:T(8,128)(2,1)S(1)}, bf16[256,256]{1,0:T(8,128)(2,1)S(1)}, u32[]{:S(2)}, u32[]{:S(2)}) collective-permute-start(bf16[256,256]{1,0:T(8,128)(2,1)S(1)} %get-tuple-element.44), channel_id=1, source_target_pairs={{0,1},{1,0},{2,3},{3,2},{4,5},{5,4},{6,7},{7,6},{8,10},{9,11},{10,... | collective-permute-start | bytes 393224 | tf_op jit(solution)/shard_map/ppermute | solution.py:252
  18.9 1.6 %collective-permute-start.12 = (bf16[256,256]{1,0:T(8,128)(2,1)S(1)}, bf16[256,256]{1,0:T(8,128)(2,1)S(1)}, u32[]{:S(2)}, u32[]{:S(2)}) collective-permute-start(bf16[256,256]{1,0:T(8,128)(2,1)S(1)} %add_convert_fusion.3), channel_id=1, source_target_pairs={{0,2},{1,3},{2,0},{3,1},{4,6},{5,7},{6,4},{7,5},{8,9},{9,8},{10,11... | collective-permute-start | bytes 393224 | tf_op jit(solution)/shard_map/ppermute | solution.py:252
  20.6 0.8 %collective-permute-done.4 = bf16[256,256]{1,0:T(8,128)(2,1)S(1)} collective-permute-done((bf16[256,256]{1,0:T(8,128)(2,1)S(1)}, bf16[256,256]{1,0:T(8,128)(2,1)S(1)}, u32[]{:S(2)}, u32[]{:S(2)}) %collective-permute-start.4) | collective-permute-done | bytes 131104 | tf_op jit(solution)/shard_map/ppermute | solution.py:252
  21.4 2.1 %collective-permute-start.5 = (bf16[256,256]{1,0:T(8,128)(2,1)S(1)}, bf16[256,256]{1,0:T(8,128)(2,1)S(1)}, u32[]{:S(2)}, u32[]{:S(2)}) collective-permute-start(bf16[256,256]{1,0:T(8,128)(2,1)S(1)} %add_convert_fusion.5), channel_id=1, source_target_pairs={{0,2},{1,3},{2,0},{3,1},{4,6},{5,7},{6,4},{7,5},{8,9},{9,8},{10,11... | collective-permute-start | bytes 393224 | tf_op jit(solution)/shard_map/ppermute | solution.py:252
  23.5 0.8 %collective-permute-done.10 = bf16[256,256]{1,0:T(8,128)(2,1)S(1)} collective-permute-done((bf16[256,256]{1,0:T(8,128)(2,1)S(1)}, bf16[256,256]{1,0:T(8,128)(2,1)S(1)}, u32[]{:S(2)}, u32[]{:S(2)}) %collective-permute-start.10) | collective-permute-done | bytes 131104 | tf_op jit(solution)/shard_map/ppermute | solution.py:252
  24.4 2.6 %collective-permute-start.13 = (bf16[256,256]{1,0:T(8,128)(2,1)S(1)}, bf16[256,256]{1,0:T(8,128)(2,1)S(1)}, u32[]{:S(2)}, u32[]{:S(2)}) collective-permute-start(bf16[256,256]{1,0:T(8,128)(2,1)S(1)} %add_convert_fusion.2.mine_ref), channel_id=1, source_target_pairs={{0,4},{1,5},{2,6},{3,7},{4,0},{5,1},{6,2},{7,3},{8,12},{9,13},{10,... | collective-permute-start | bytes 393224 | tf_op jit(solution)/shard_map/ppermute | solution.py:246
  27.1 2.4 %collective-permute-start.6 = (bf16[256,256]{1,0:T(8,128)(2,1)S(1)}, bf16[256,256]{1,0:T(8,128)(2,1)S(1)}, u32[]{:S(2)}, u32[]{:S(2)}) collective-permute-start(bf16[256,256]{1,0:T(8,128)(2,1)S(1)} %add_convert_fusion.4.mine_ref), channel_id=1, source_target_pairs={{0,4},{1,5},{2,6},{3,7},{4,0},{5,1},{6,2},{7,3},{8,12},{9,13},{10,... | collective-permute-start | bytes 393224 | tf_op jit(solution)/shard_map/ppermute | solution.py:246
  29.5 3.3 %sum_upper.1.mat_ref = bf16[8,1024,128]{2,1,0:T(8,128)(2,1)S(1)} custom-call(s32[2]{0:T(128)S(1)} %pad_add_fusion.ids_ref, s32[8,16]{1,0:T(8,128)S(1)} %bitcast.4, bf16[16,8,128,128]{3,2,1,0:T(8,128)(2,1)} %blk_hbm.3), custom_call_target="tpu_custom_call" | custom-call | tf_op jit(solution)/shard_map/sum_upper/pallas_call | solution.py:88
  32.8 1.1 %pick_top.1 = (bf16[256,512]{1,0:T(8,128)(2,1)S(1)}, bf16[2,128,128]{2,1,0:T(8,128)(2,1)S(1)}, bf16[2,128,128]{2,1,0:T(8,128)(2,1)S(1)}) custom-call(s32[2]{0:T(128)S(1)} %pad_add_fusion.ids_ref, bf16[1024,512]{1,0:T(8,128)(2,1)S(1)} %copy-done, bf16[8,128,128]{2,1,0:T(8,128)(2,1)S(1)} %copy-done.2, bf16[8,128,128]{2,1,0:T(8,128)(2,1)S(1)} %copy-done.3), custom_call_target="tpu_custom_call" | custom-call | tf_op jit(solution)/shard_map/pick_top/pallas_call | solution.py:127
  33.9 3.1 %collective-permute-done.13.got_ref = bf16[256,256]{1,0:T(8,128)(2,1)S(1)} collective-permute-done((bf16[256,256]{1,0:T(8,128)(2,1)S(1)}, bf16[256,256]{1,0:T(8,128)(2,1)S(1)}, u32[]{:S(2)}, u32[]{:S(2)}) %collective-permute-start.13) | collective-permute-done | bytes 131104 | tf_op jit(solution)/shard_map/ppermute | solution.py:246
  37.1 0.4 solve_top.3.p0
  37.5 1.1 %collective-permute-start.14 = (bf16[256,256]{1,0:T(8,128)(2,1)S(1)}, bf16[256,256]{1,0:T(8,128)(2,1)S(1)}, u32[]{:S(2)}, u32[]{:S(2)}) collective-permute-start(bf16[256,256]{1,0:T(8,128)(2,1)S(1)} %solve_top.3.p0), channel_id=1, source_target_pairs={{0,1},{1,0},{2,3},{3,2},{4,5},{5,4},{6,7},{7,6},{8,10},{9,11},{10,... | collective-permute-start | bytes 393224 | tf_op jit(solution)/shard_map/ppermute | solution.py:252
  38.7 0.4 solve_top.2.p0
  39.1 1.9 %collective-permute-start.19 = (bf16[256,256]{1,0:T(8,128)(2,1)S(1)}, bf16[256,256]{1,0:T(8,128)(2,1)S(1)}, u32[]{:S(2)}, u32[]{:S(2)}) collective-permute-start(bf16[256,256]{1,0:T(8,128)(2,1)S(1)} %solve_top.2.p0), channel_id=1, source_target_pairs={{0,2},{1,3},{2,0},{3,1},{4,6},{5,7},{6,4},{7,5},{8,9},{9,8},{10,11... | collective-permute-start | bytes 393224 | tf_op jit(solution)/shard_map/ppermute | solution.py:252
  40.9 1.1 %collective-permute-start.18 = (bf16[256,256]{1,0:T(8,128)(2,1)S(1)}, bf16[256,256]{1,0:T(8,128)(2,1)S(1)}, u32[]{:S(2)}, u32[]{:S(2)}) collective-permute-start(bf16[256,256]{1,0:T(8,128)(2,1)S(1)} %solve_top.2.p0), channel_id=1, source_target_pairs={{0,1},{1,0},{2,3},{3,2},{4,5},{5,4},{6,7},{7,6},{8,10},{9,11},{10,... | collective-permute-start | bytes 393224 | tf_op jit(solution)/shard_map/ppermute | solution.py:252
  42.0 0.5 collective-permute-done.15.p2
  42.5 1.3 %collective-permute-done.14.p1 = bf16[256,256]{1,0:T(8,128)(2,1)S(1)} collective-permute-done((bf16[256,256]{1,0:T(8,128)(2,1)S(1)}, bf16[256,256]{1,0:T(8,128)(2,1)S(1)}, u32[]{:S(2)}, u32[]{:S(2)}) %collective-permute-start.14) | collective-permute-done | bytes 131104 | tf_op jit(solution)/shard_map/ppermute | solution.py:252
  43.8 0.8 %collective-permute-start.16 = (bf16[256,256]{1,0:T(8,128)(2,1)S(1)}, bf16[256,256]{1,0:T(8,128)(2,1)S(1)}, u32[]{:S(2)}, u32[]{:S(2)}) collective-permute-start(bf16[256,256]{1,0:T(8,128)(2,1)S(1)} %collective-permute-done.15.p2), channel_id=1, source_target_pairs={{0,1},{1,0},{2,3},{3,2},{4,5},{5,4},{6,7},{7,6},{8,10},{9,11},{10,... | collective-permute-start | bytes 393224 | tf_op jit(solution)/shard_map/ppermute | solution.py:252
  44.6 1.0 %collective-permute-done.19.p2 = bf16[256,256]{1,0:T(8,128)(2,1)S(1)} collective-permute-done((bf16[256,256]{1,0:T(8,128)(2,1)S(1)}, bf16[256,256]{1,0:T(8,128)(2,1)S(1)}, u32[]{:S(2)}, u32[]{:S(2)}) %collective-permute-start.19) | collective-permute-done | bytes 131104 | tf_op jit(solution)/shard_map/ppermute | solution.py:252
  45.5 0.4 collective-permute-done.18.p1
  45.9 1.2 %collective-permute-start.20 = (bf16[256,256]{1,0:T(8,128)(2,1)S(1)}, bf16[256,256]{1,0:T(8,128)(2,1)S(1)}, u32[]{:S(2)}, u32[]{:S(2)}) collective-permute-start(bf16[256,256]{1,0:T(8,128)(2,1)S(1)} %collective-permute-done.19.p2), channel_id=1, source_target_pairs={{0,1},{1,0},{2,3},{3,2},{4,5},{5,4},{6,7},{7,6},{8,10},{9,11},{10,... | collective-permute-start | bytes 393224 | tf_op jit(solution)/shard_map/ppermute | solution.py:252
  47.1 1.6 %collective-permute-done.16.p3 = bf16[256,256]{1,0:T(8,128)(2,1)S(1)} collective-permute-done((bf16[256,256]{1,0:T(8,128)(2,1)S(1)}, bf16[256,256]{1,0:T(8,128)(2,1)S(1)}, u32[]{:S(2)}, u32[]{:S(2)}) %collective-permute-start.16) | collective-permute-done | bytes 131104 | tf_op jit(solution)/shard_map/ppermute | solution.py:252
  48.7 0.4 first_upper.2
  49.3 1.6 %collective-permute-done.20.p3 = bf16[256,256]{1,0:T(8,128)(2,1)S(1)} collective-permute-done((bf16[256,256]{1,0:T(8,128)(2,1)S(1)}, bf16[256,256]{1,0:T(8,128)(2,1)S(1)}, u32[]{:S(2)}, u32[]{:S(2)}) %collective-permute-start.20) | collective-permute-done | bytes 131104 | tf_op jit(solution)/shard_map/ppermute | solution.py:252
  50.9 0.4 first_upper.3
  51.4 1.6 %collective-permute-start.22 = (bf16[256,256]{1,0:T(8,128)(2,1)S(1)}, bf16[256,256]{1,0:T(8,128)(2,1)S(1)}, u32[]{:S(2)}, u32[]{:S(2)}) collective-permute-start(bf16[256,256]{1,0:T(8,128)(2,1)S(1)} %add_convert_fusion.1), channel_id=1, source_target_pairs={{0,16},{8,24},{16,0},{24,8},{1,17},{9,25},{17,1},{25,9},{2,18},{10... | collective-permute-start | bytes 393224 | tf_op jit(solution)/shard_map/ppermute | solution.py:246
  53.1 1.3 %collective-permute-start.23 = (bf16[256,256]{1,0:T(8,128)(2,1)S(1)}, bf16[256,256]{1,0:T(8,128)(2,1)S(1)}, u32[]{:S(2)}, u32[]{:S(2)}) collective-permute-start(bf16[256,256]{1,0:T(8,128)(2,1)S(1)} %add_convert_fusion), channel_id=1, source_target_pairs={{0,16},{8,24},{16,0},{24,8},{1,17},{9,25},{17,1},{25,9},{2,18},{10... | collective-permute-start | bytes 393224 | tf_op jit(solution)/shard_map/ppermute | solution.py:246
  54.3 0.4 apply_upper.3
  54.8 0.4 apply_upper.2
  55.3 0.6 collective-permute-start.24
  55.8 0.7 %pad_maximum_fusion = bf16[128,512]{1,0:T(8,128)(2,1)} fusion(bf16[128,256]{1,0:T(8,128)(2,1)S(1)} %slice.9, bf16[128,256]{1,0:T(8,128)(2,1)S(1)} %slice.8), kind=kLoop, calls=%fused_computation.8 | loop fusion | flops 262144 | bytes 262144 | tf_op jit(solution)/shard_map/concatenate | solution.py:370
  56.5 1.3 %collective-permute-done.22 = bf16[256,256]{1,0:T(8,128)(2,1)S(1)} collective-permute-done((bf16[256,256]{1,0:T(8,128)(2,1)S(1)}, bf16[256,256]{1,0:T(8,128)(2,1)S(1)}, u32[]{:S(2)}, u32[]{:S(2)}) %collective-permute-start.22) | collective-permute-done | bytes 131104 | tf_op jit(solution)/shard_map/ppermute | solution.py:246
  57.8 0.9 %solve_low.2.refs_2_ = bf16[256,512]{1,0:T(8,128)(2,1)} custom-call(bf16[2,128,128]{2,1,0:T(8,128)(2,1)S(1)} %copy-done.4, bf16[256,256]{1,0:T(8,128)(2,1)S(1)} %get-tuple-element.41.p0.fwd_ref, f32[256,256]{1,0:T(8,128)S(1)} %convert_add_fusion.refs_0_, bf16[256,256]{1,0:T(8,128)(2,1)S(1)} %collective-permute-done.25.refs_1_), custom_call_target="tpu_custom_call" | custom-call | tf_op jit(solution)/shard_map/solve_low/pallas_call | solution.py:227
  58.7 1.5 %collective-permute-done.23 = bf16[256,256]{1,0:T(8,128)(2,1)S(1)} collective-permute-done((bf16[256,256]{1,0:T(8,128)(2,1)S(1)}, bf16[256,256]{1,0:T(8,128)(2,1)S(1)}, u32[]{:S(2)}, u32[]{:S(2)}) %collective-permute-start.23) | collective-permute-done | bytes 131104 | tf_op jit(solution)/shard_map/ppermute | solution.py:246
  60.2 0.9 %solve_low.3 = bf16[256,512]{1,0:T(8,128)(2,1)} custom-call(bf16[2,128,128]{2,1,0:T(8,128)(2,1)S(1)} %copy-done.4, bf16[256,256]{1,0:T(8,128)(2,1)S(1)} %get-tuple-element.31.p0.fwd_ref, f32[256,256]{1,0:T(8,128)S(1)} %convert_add_fusion.1.refs_0_, bf16[256,256]{1,0:T(8,128)(2,1)S(1)} %collective-permute-done.24.refs_1_, ...), custom_call_target="tpu_custom_call", output_to_operand_aliasing={{}: (4, {})} | custom-call | tf_op jit(solution)/shard_map/solve_low/pallas_call | solution.py:227
  (46 shorter events, 1.8 us)
Async XLA Ops:
  0.6 1.0 %copy-start.1 = (bf16[256,512]{1,0:T(8,128)(2,1)S(1)}, bf16[256,512]{1,0:T(8,128)(2,1)}, u32[]{:S(2)}) copy-start(bf16[256,512]{1,0:T(8,128)(2,1)} %rhs_hbm.2) | copy-start | bytes 786436
  1.6 0.8 %copy-start.5 = (bf16[2,128,128]{2,1,0:T(8,128)(2,1)S(1)}, bf16[2,128,128]{2,1,0:T(8,128)(2,1)}, u32[]{:S(2)}) copy-start(bf16[2,128,128]{2,1,0:T(8,128)(2,1)} %inv_hbm.1) | copy-start | bytes 196612
  2.7 7.2 %collective-permute-start.8 = (bf16[256,256]{1,0:T(8,128)(2,1)S(1)}, bf16[256,256]{1,0:T(8,128)(2,1)S(1)}, u32[]{:S(2)}, u32[]{:S(2)}) collective-permute-start(bf16[256,256]{1,0:T(8,128)(2,1)S(1)} %get-tuple-element.41.p0.fwd_ref), channel_id=1, source_target_pairs={{0,16},{8,24},{16,0},{24,8},{1,17},{9,25},{17,1},{25,9},{2,18},{10... | collective-permute-start | bytes 393224 | tf_op jit(solution)/shard_map/ppermute | solution.py:246
  5.8 6.3 %collective-permute-start.7 = (bf16[256,256]{1,0:T(8,128)(2,1)S(1)}, bf16[256,256]{1,0:T(8,128)(2,1)S(1)}, u32[]{:S(2)}, u32[]{:S(2)}) collective-permute-start(bf16[256,256]{1,0:T(8,128)(2,1)S(1)} %get-tuple-element.41.p0.fwd_ref), channel_id=1, source_target_pairs={{0,8},{8,0},{16,24},{24,16},{1,9},{9,1},{17,25},{25,17},{2,10},{10... | collective-permute-start | bytes 393224 | tf_op jit(solution)/shard_map/ppermute | solution.py:246
  5.8 6.3 %collective-permute-start.1 = (bf16[256,256]{1,0:T(8,128)(2,1)S(1)}, bf16[256,256]{1,0:T(8,128)(2,1)S(1)}, u32[]{:S(2)}, u32[]{:S(2)}) collective-permute-start(bf16[256,256]{1,0:T(8,128)(2,1)S(1)} %get-tuple-element.31.p0.fwd_ref), channel_id=1, source_target_pairs={{0,16},{8,24},{16,0},{24,8},{1,17},{9,25},{17,1},{25,9},{2,18},{10... | collective-permute-start | bytes 393224 | tf_op jit(solution)/shard_map/ppermute | solution.py:246
  6.0 0.7 %copy-start.6 = (s32[16,8]{0,1:T(8,128)S(1)}, s32[16,8]{0,1:T(8,128)}, u32[]{:S(2)}) copy-start(s32[16,8]{0,1:T(8,128)} %param.13) | copy-start | bytes 1540
  10.0 2.1 %collective-permute-start.9 = (bf16[256,256]{1,0:T(8,128)(2,1)S(1)}, bf16[256,256]{1,0:T(8,128)(2,1)S(1)}, u32[]{:S(2)}, u32[]{:S(2)}) collective-permute-start(bf16[256,256]{1,0:T(8,128)(2,1)S(1)} %collective-permute-done.8.p2), channel_id=1, source_target_pairs={{0,8},{8,0},{16,24},{24,16},{1,9},{9,1},{17,25},{25,17},{2,10},{10... | collective-permute-start | bytes 393224 | tf_op jit(solution)/shard_map/ppermute | solution.py:246
  10.4 3.8 %collective-permute-start = (bf16[256,256]{1,0:T(8,128)(2,1)S(1)}, bf16[256,256]{1,0:T(8,128)(2,1)S(1)}, u32[]{:S(2)}, u32[]{:S(2)}) collective-permute-start(bf16[256,256]{1,0:T(8,128)(2,1)S(1)} %get-tuple-element.31.p0.fwd_ref), channel_id=1, source_target_pairs={{0,8},{8,0},{16,24},{24,16},{1,9},{9,1},{17,25},{25,17},{2,10},{10... | collective-permute-start | bytes 393224 | tf_op jit(solution)/shard_map/ppermute | solution.py:246
  12.1 2.1 %collective-permute-start.2 = (bf16[256,256]{1,0:T(8,128)(2,1)S(1)}, bf16[256,256]{1,0:T(8,128)(2,1)S(1)}, u32[]{:S(2)}, u32[]{:S(2)}) collective-permute-start(bf16[256,256]{1,0:T(8,128)(2,1)S(1)} %collective-permute-done.1.p2), channel_id=1, source_target_pairs={{0,8},{8,0},{16,24},{24,16},{1,9},{9,1},{17,25},{25,17},{2,10},{10... | collective-permute-start | bytes 393224 | tf_op jit(solution)/shard_map/ppermute | solution.py:246
  12.4 6.5 %collective-permute-start.11 = (bf16[256,256]{1,0:T(8,128)(2,1)S(1)}, bf16[256,256]{1,0:T(8,128)(2,1)S(1)}, u32[]{:S(2)}, u32[]{:S(2)}) collective-permute-start(bf16[256,256]{1,0:T(8,128)(2,1)S(1)} %first_lower.3), channel_id=1, source_target_pairs={{0,1},{1,0},{2,3},{3,2},{4,5},{5,4},{6,7},{7,6},{8,10},{9,11},{10,... | collective-permute-start | bytes 393224 | tf_op jit(solution)/shard_map/ppermute | solution.py:252
  14.8 12.2 %collective-permute-start.3 = (bf16[256,256]{1,0:T(8,128)(2,1)S(1)}, bf16[256,256]{1,0:T(8,128)(2,1)S(1)}, u32[]{:S(2)}, u32[]{:S(2)}) collective-permute-start(bf16[256,256]{1,0:T(8,128)(2,1)S(1)} %get-tuple-element.34), channel_id=1, source_target_pairs={{0,1},{1,0},{2,3},{3,2},{4,5},{5,4},{6,7},{7,6},{8,10},{9,11},{10,... | collective-permute-start | bytes 393224 | tf_op jit(solution)/shard_map/ppermute | solution.py:252
  16.1 5.3 %collective-permute-start.4 = (bf16[256,256]{1,0:T(8,128)(2,1)S(1)}, bf16[256,256]{1,0:T(8,128)(2,1)S(1)}, u32[]{:S(2)}, u32[]{:S(2)}) collective-permute-start(bf16[256,256]{1,0:T(8,128)(2,1)S(1)} %first_lower.2), channel_id=1, source_target_pairs={{0,1},{1,0},{2,3},{3,2},{4,5},{5,4},{6,7},{7,6},{8,10},{9,11},{10,... | collective-permute-start | bytes 393224 | tf_op jit(solution)/shard_map/ppermute | solution.py:252
  17.8 14.9 %copy-start = (bf16[1024,512]{1,0:T(8,128)(2,1)S(1)}, bf16[1024,512]{1,0:T(8,128)(2,1)}, u32[]{:S(2)}) copy-start(bf16[1024,512]{1,0:T(8,128)(2,1)} %rhs_hbm.3) | copy-start | bytes 3145732
  17.8 14.9 %copy-start.2 = (bf16[8,128,128]{2,1,0:T(8,128)(2,1)S(1)}, bf16[8,128,128]{2,1,0:T(8,128)(2,1)}, u32[]{:S(2)}) copy-start(bf16[8,128,128]{2,1,0:T(8,128)(2,1)} %low_hbm.1) | copy-start | bytes 786436
  17.9 14.9 %copy-start.3 = (bf16[8,128,128]{2,1,0:T(8,128)(2,1)S(1)}, bf16[8,128,128]{2,1,0:T(8,128)(2,1)}, u32[]{:S(2)}) copy-start(bf16[8,128,128]{2,1,0:T(8,128)(2,1)} %up_hbm.1) | copy-start | bytes 786436
  17.9 6.4 %collective-permute-start.10 = (bf16[256,256]{1,0:T(8,128)(2,1)S(1)}, bf16[256,256]{1,0:T(8,128)(2,1)S(1)}, u32[]{:S(2)}, u32[]{:S(2)}) collective-permute-start(bf16[256,256]{1,0:T(8,128)(2,1)S(1)} %get-tuple-element.44), channel_id=1, source_target_pairs={{0,1},{1,0},{2,3},{3,2},{4,5},{5,4},{6,7},{7,6},{8,10},{9,11},{10,... | collective-permute-start | bytes 393224 | tf_op jit(solution)/shard_map/ppermute | solution.py:252
  18.9 5.4 %collective-permute-start.12 = (bf16[256,256]{1,0:T(8,128)(2,1)S(1)}, bf16[256,256]{1,0:T(8,128)(2,1)S(1)}, u32[]{:S(2)}, u32[]{:S(2)}) collective-permute-start(bf16[256,256]{1,0:T(8,128)(2,1)S(1)} %add_convert_fusion.3), channel_id=1, source_target_pairs={{0,2},{1,3},{2,0},{3,1},{4,6},{5,7},{6,4},{7,5},{8,9},{9,8},{10,11... | collective-permute-start | bytes 393224 | tf_op jit(solution)/shard_map/ppermute | solution.py:252
  21.4 5.6 %collective-permute-start.5 = (bf16[256,256]{1,0:T(8,128)(2,1)S(1)}, bf16[256,256]{1,0:T(8,128)(2,1)S(1)}, u32[]{:S(2)}, u32[]{:S(2)}) collective-permute-start(bf16[256,256]{1,0:T(8,128)(2,1)S(1)} %add_convert_fusion.5), channel_id=1, source_target_pairs={{0,2},{1,3},{2,0},{3,1},{4,6},{5,7},{6,4},{7,5},{8,9},{9,8},{10,11... | collective-permute-start | bytes 393224 | tf_op jit(solution)/shard_map/ppermute | solution.py:252
  24.4 12.7 %collective-permute-start.13 = (bf16[256,256]{1,0:T(8,128)(2,1)S(1)}, bf16[256,256]{1,0:T(8,128)(2,1)S(1)}, u32[]{:S(2)}, u32[]{:S(2)}) collective-permute-start(bf16[256,256]{1,0:T(8,128)(2,1)S(1)} %add_convert_fusion.2.mine_ref), channel_id=1, source_target_pairs={{0,4},{1,5},{2,6},{3,7},{4,0},{5,1},{6,2},{7,3},{8,12},{9,13},{10,... | collective-permute-start | bytes 393224 | tf_op jit(solution)/shard_map/ppermute | solution.py:246
  27.1 11.6 %collective-permute-start.6 = (bf16[256,256]{1,0:T(8,128)(2,1)S(1)}, bf16[256,256]{1,0:T(8,128)(2,1)S(1)}, u32[]{:S(2)}, u32[]{:S(2)}) collective-permute-start(bf16[256,256]{1,0:T(8,128)(2,1)S(1)} %add_convert_fusion.4.mine_ref), channel_id=1, source_target_pairs={{0,4},{1,5},{2,6},{3,7},{4,0},{5,1},{6,2},{7,3},{8,12},{9,13},{10,... | collective-permute-start | bytes 393224 | tf_op jit(solution)/shard_map/ppermute | solution.py:246
  37.4 5.0 %collective-permute-start.15 = (bf16[256,256]{1,0:T(8,128)(2,1)S(1)}, bf16[256,256]{1,0:T(8,128)(2,1)S(1)}, u32[]{:S(2)}, u32[]{:S(2)}) collective-permute-start(bf16[256,256]{1,0:T(8,128)(2,1)S(1)} %solve_top.3.p0), channel_id=1, source_target_pairs={{0,2},{1,3},{2,0},{3,1},{4,6},{5,7},{6,4},{7,5},{8,9},{9,8},{10,11... | collective-permute-start | bytes 393224 | tf_op jit(solution)/shard_map/ppermute | solution.py:252
  37.5 6.3 %collective-permute-start.14 = (bf16[256,256]{1,0:T(8,128)(2,1)S(1)}, bf16[256,256]{1,0:T(8,128)(2,1)S(1)}, u32[]{:S(2)}, u32[]{:S(2)}) collective-permute-start(bf16[256,256]{1,0:T(8,128)(2,1)S(1)} %solve_top.3.p0), channel_id=1, source_target_pairs={{0,1},{1,0},{2,3},{3,2},{4,5},{5,4},{6,7},{7,6},{8,10},{9,11},{10,... | collective-permute-start | bytes 393224 | tf_op jit(solution)/shard_map/ppermute | solution.py:252
  39.1 6.4 %collective-permute-start.19 = (bf16[256,256]{1,0:T(8,128)(2,1)S(1)}, bf16[256,256]{1,0:T(8,128)(2,1)S(1)}, u32[]{:S(2)}, u32[]{:S(2)}) collective-permute-start(bf16[256,256]{1,0:T(8,128)(2,1)S(1)} %solve_top.2.p0), channel_id=1, source_target_pairs={{0,2},{1,3},{2,0},{3,1},{4,6},{5,7},{6,4},{7,5},{8,9},{9,8},{10,11... | collective-permute-start | bytes 393224 | tf_op jit(solution)/shard_map/ppermute | solution.py:252
  40.9 5.0 %collective-permute-start.18 = (bf16[256,256]{1,0:T(8,128)(2,1)S(1)}, bf16[256,256]{1,0:T(8,128)(2,1)S(1)}, u32[]{:S(2)}, u32[]{:S(2)}) collective-permute-start(bf16[256,256]{1,0:T(8,128)(2,1)S(1)} %solve_top.2.p0), channel_id=1, source_target_pairs={{0,1},{1,0},{2,3},{3,2},{4,5},{5,4},{6,7},{7,6},{8,10},{9,11},{10,... | collective-permute-start | bytes 393224 | tf_op jit(solution)/shard_map/ppermute | solution.py:252
  43.8 5.0 %collective-permute-start.16 = (bf16[256,256]{1,0:T(8,128)(2,1)S(1)}, bf16[256,256]{1,0:T(8,128)(2,1)S(1)}, u32[]{:S(2)}, u32[]{:S(2)}) collective-permute-start(bf16[256,256]{1,0:T(8,128)(2,1)S(1)} %collective-permute-done.15.p2), channel_id=1, source_target_pairs={{0,1},{1,0},{2,3},{3,2},{4,5},{5,4},{6,7},{7,6},{8,10},{9,11},{10,... | collective-permute-start | bytes 393224 | tf_op jit(solution)/shard_map/ppermute | solution.py:252
  45.9 5.0 %collective-permute-start.20 = (bf16[256,256]{1,0:T(8,128)(2,1)S(1)}, bf16[256,256]{1,0:T(8,128)(2,1)S(1)}, u32[]{:S(2)}, u32[]{:S(2)}) collective-permute-start(bf16[256,256]{1,0:T(8,128)(2,1)S(1)} %collective-permute-done.19.p2), channel_id=1, source_target_pairs={{0,1},{1,0},{2,3},{3,2},{4,5},{5,4},{6,7},{7,6},{8,10},{9,11},{10,... | collective-permute-start | bytes 393224 | tf_op jit(solution)/shard_map/ppermute | solution.py:252
  49.2 2.2 %collective-permute-start.17 = (bf16[256,256]{1,0:T(8,128)(2,1)S(1)}, bf16[256,256]{1,0:T(8,128)(2,1)S(1)}, u32[]{:S(2)}, u32[]{:S(2)}) collective-permute-start(bf16[256,256]{1,0:T(8,128)(2,1)S(1)} %get-tuple-element.48), channel_id=1, source_target_pairs={{0,8},{8,0},{16,24},{24,16},{1,9},{9,1},{17,25},{25,17},{2,10},{10... | collective-permute-start | bytes 393224 | tf_op jit(solution)/shard_map/ppermute | solution.py:246
  49.3 8.6 %copy-start.4 = (bf16[2,128,128]{2,1,0:T(8,128)(2,1)S(1)}, bf16[2,128,128]{2,1,0:T(8,128)(2,1)}, u32[]{:S(2)}) copy-start(bf16[2,128,128]{2,1,0:T(8,128)(2,1)} %inv_ref.3) | copy-start | bytes 196612
  51.3 1.7 %collective-permute-start.21 = (bf16[256,256]{1,0:T(8,128)(2,1)S(1)}, bf16[256,256]{1,0:T(8,128)(2,1)S(1)}, u32[]{:S(2)}, u32[]{:S(2)}) collective-permute-start(bf16[256,256]{1,0:T(8,128)(2,1)S(1)} %get-tuple-element.51), channel_id=1, source_target_pairs={{0,8},{8,0},{16,24},{24,16},{1,9},{9,1},{17,25},{25,17},{2,10},{10... | collective-permute-start | bytes 393224 | tf_op jit(solution)/shard_map/ppermute | solution.py:246
  51.4 6.4 %collective-permute-start.22 = (bf16[256,256]{1,0:T(8,128)(2,1)S(1)}, bf16[256,256]{1,0:T(8,128)(2,1)S(1)}, u32[]{:S(2)}, u32[]{:S(2)}) collective-permute-start(bf16[256,256]{1,0:T(8,128)(2,1)S(1)} %add_convert_fusion.1), channel_id=1, source_target_pairs={{0,16},{8,24},{16,0},{24,8},{1,17},{9,25},{17,1},{25,9},{2,18},{10... | collective-permute-start | bytes 393224 | tf_op jit(solution)/shard_map/ppermute | solution.py:246
  53.1 7.1 %collective-permute-start.23 = (bf16[256,256]{1,0:T(8,128)(2,1)S(1)}, bf16[256,256]{1,0:T(8,128)(2,1)S(1)}, u32[]{:S(2)}, u32[]{:S(2)}) collective-permute-start(bf16[256,256]{1,0:T(8,128)(2,1)S(1)} %add_convert_fusion), channel_id=1, source_target_pairs={{0,16},{8,24},{16,0},{24,8},{1,17},{9,25},{17,1},{25,9},{2,18},{10... | collective-permute-start | bytes 393224 | tf_op jit(solution)/shard_map/ppermute | solution.py:246
  54.8 3.1 %collective-permute-start.25 = (bf16[256,256]{1,0:T(8,128)(2,1)S(1)}, bf16[256,256]{1,0:T(8,128)(2,1)S(1)}, u32[]{:S(2)}, u32[]{:S(2)}) collective-permute-start(bf16[256,256]{1,0:T(8,128)(2,1)S(1)} %get-tuple-element.58), channel_id=1, source_target_pairs={{0,8},{8,0},{16,24},{24,16},{1,9},{9,1},{17,25},{25,17},{2,10},{10... | collective-permute-start | bytes 393224 | tf_op jit(solution)/shard_map/ppermute | solution.py:246
  55.3 4.9 %collective-permute-start.24 = (bf16[256,256]{1,0:T(8,128)(2,1)S(1)}, bf16[256,256]{1,0:T(8,128)(2,1)S(1)}, u32[]{:S(2)}, u32[]{:S(2)}) collective-permute-start(bf16[256,256]{1,0:T(8,128)(2,1)S(1)} %get-tuple-element.55), channel_id=1, source_target_pairs={{0,8},{8,0},{16,24},{24,16},{1,9},{9,1},{17,25},{25,17},{2,10},{10... | collective-permute-start | bytes 393224 | tf_op jit(solution)/shard_map/ppermute | solution.py:246

commit v6 on v5

--- a/solution.py
+++ b/solution.py
@@ -14,7 +14,7 @@
 
 
 def params(mib, **kw):
-    return pltpu.CompilerParams(vmem_limit_bytes=mib * MIB, **kw)
+    return pltpu.CompilerParams(vmem_limit_bytes=int(mib * MIB), **kw)
 
 
 def place_of(low, high, count):
@@ -46,7 +46,7 @@
         in_specs=[pl.BlockSpec(memory_space=pltpu.HBM)] * 2,
         out_shape=[jax.ShapeDtypeStruct((rhs.shape[0], rhs.shape[1] // len(FLIPS)), BF)] * len(FLIPS),
         scratch_shapes=[pltpu.VMEM(inv.shape, BF), pltpu.VMEM(rhs.shape, BF), pltpu.SemaphoreType.DMA((2,))],
-        compiler_params=params(8),
+        compiler_params=params(63.75),
         name="fwd_low",
     )(inv, rhs)
 

time: 61.3 us -> 61.3 us (level)
  local copies, waits for them, and re-layouts: 2.51 us -> 0.74 us
  Pallas kernels: 13.9 us -> 15.5 us
    unnamed x14, local copies, waits for them, and re-layouts: 2.49 us -> 0.72 us
    pallas_call x1, Pallas kernels: 0.31 us -> 1.88 us  [solve_fwd(): pl.pallas_call(fwd_kernel, in_specs=[pl.BlockSpec(memory_space=pltpu.HBM)...]
where the time goes in v6:
time: 61.3 us; the launch traced here: 61.2 us
  starting transfers between devices  27.2 us (44%)
  waiting for transfers between devices  15.7 us (26%)
  Pallas kernels  15.5 us (25%)
  other arithmetic  1.05 us (2%)
  between operations  0.96 us (2%)
  local copies, waits for them, and re-layouts  0.74 us (1%)
    ppermute x12, starting transfers between devices, cross(): return lax.ppermute(x, ('row', 'col'), pairs)  14.8 us
    ppermute x14, starting transfers between devices, swap(): return lax.ppermute(x, axis, [(i, i ^ 1 << bit) for i in range(size)])  12.4 us
    ppermute x12, waiting for transfers between devices, cross(): return lax.ppermute(x, ('row', 'col'), pairs)  7.95 us
    ppermute x14, waiting for transfers between devices, swap(): return lax.ppermute(x, axis, [(i, i ^ 1 << bit) for i in range(size)])  7.7 us
    pallas_call x2, Pallas kernels, sum_blocks(): pl.pallas_call(functools.partial(sum_kernel, lower, rows, tops, own), in_...  6.57 us
    pallas_call x8, Pallas kernels, apply(): pl.pallas_call(functools.partial(kernel, begin), out_shape=[jax.ShapeDtyp...  3.5 us
    pallas_call x1, Pallas kernels, solve_fwd(): pl.pallas_call(fwd_kernel, in_specs=[pl.BlockSpec(memory_space=pltpu.HBM)...  1.88 us
    pallas_call x2, Pallas kernels, solve_low(): pl.pallas_call(functools.partial(low_kernel, len(terms)), grid=(1,), in_s...  1.73 us
  transfers between devices with their start and end apart: 26, of which 13 were waited for; matrix products, arithmetic and copies ran while one was open for 2% of the time, Pallas kernels for 21%

profile of v6, /device:TPU:0, one launch (start us, length us, event | category | flops | bytes accessed | tf_op | source)
XLA Modules:
  0.0 61.2 jit_solution(5753404857566016475)
XLA Ops:
  0.6 1.9 %fwd_low.1 = (bf16[256,256]{1,0:T(8,128)(2,1)}, bf16[256,256]{1,0:T(8,128)(2,1)}) custom-call(bf16[2,128,128]{2,1,0:T(8,128)(2,1)} %inv_hbm.1, bf16[256,512]{1,0:T(8,128)(2,1)} %rhs_hbm.2), custom_call_target="tpu_custom_call" | custom-call | tf_op jit(solution)/shard_map/fwd_low/pallas_call | solution.py:44
  2.5 3.0 %collective-permute-start.8 = (bf16[256,256]{1,0:T(8,128)(2,1)}, bf16[256,256]{1,0:T(8,128)(2,1)S(1)}, u32[]{:S(2)}, u32[]{:S(2)}) collective-permute-start(bf16[256,256]{1,0:T(8,128)(2,1)} %get-tuple-element.41.p0.fwd_ref), channel_id=1, source_target_pairs={{0,16},{8,24},{16,0},{24,8},{1,17},{9,25},{17,1},{25,9},{2,18},{10... | collective-permute-start | bytes 393224 | tf_op jit(solution)/shard_map/ppermute | solution.py:246
  5.8 0.7 %copy-done.6 = s32[16,8]{0,1:T(8,128)S(1)} copy-done((s32[16,8]{0,1:T(8,128)S(1)}, s32[16,8]{0,1:T(8,128)}, u32[]{:S(2)}) %copy-start.6) | copy-done | bytes 536
  6.5 3.3 %sum_lower.1.mat_ref = bf16[4,1024,256]{2,1,0:T(8,128)(2,1)S(1)} custom-call(s32[2]{0:T(128)S(1)} %pad_add_fusion.ids_ref, s32[8,16]{1,0:T(8,128)S(1)} %bitcast.3, bf16[16,8,128,128]{3,2,1,0:T(8,128)(2,1)} %blk_hbm.2), custom_call_target="tpu_custom_call" | custom-call | tf_op jit(solution)/shard_map/sum_lower/pallas_call | solution.py:88
  9.8 0.4 collective-permute-start.9
  10.4 1.7 %collective-permute-done.1.p2 = bf16[256,256]{1,0:T(8,128)(2,1)S(1)} collective-permute-done((bf16[256,256]{1,0:T(8,128)(2,1)}, bf16[256,256]{1,0:T(8,128)(2,1)S(1)}, u32[]{:S(2)}, u32[]{:S(2)}) %collective-permute-start.1) | collective-permute-done | bytes 131104 | tf_op jit(solution)/shard_map/ppermute | solution.py:246
  12.1 0.3 first_lower.3
  12.4 1.8 %collective-permute-start.11 = (bf16[256,256]{1,0:T(8,128)(2,1)S(1)}, bf16[256,256]{1,0:T(8,128)(2,1)S(1)}, u32[]{:S(2)}, u32[]{:S(2)}) collective-permute-start(bf16[256,256]{1,0:T(8,128)(2,1)S(1)} %first_lower.3), channel_id=1, source_target_pairs={{0,1},{1,0},{2,3},{3,2},{4,5},{5,4},{6,7},{7,6},{8,10},{9,11},{10,... | collective-permute-start | bytes 393224 | tf_op jit(solution)/shard_map/ppermute | solution.py:252
  14.2 0.6 apply_lower.2
  14.8 1.0 %collective-permute-start.3 = (bf16[256,256]{1,0:T(8,128)(2,1)S(1)}, bf16[256,256]{1,0:T(8,128)(2,1)S(1)}, u32[]{:S(2)}, u32[]{:S(2)}) collective-permute-start(bf16[256,256]{1,0:T(8,128)(2,1)S(1)} %get-tuple-element.34), channel_id=1, source_target_pairs={{0,1},{1,0},{2,3},{3,2},{4,5},{5,4},{6,7},{7,6},{8,10},{9,11},{10,... | collective-permute-start | bytes 393224 | tf_op jit(solution)/shard_map/ppermute | solution.py:252
  15.8 0.3 first_lower.2
  16.1 1.2 %collective-permute-start.4 = (bf16[256,256]{1,0:T(8,128)(2,1)S(1)}, bf16[256,256]{1,0:T(8,128)(2,1)S(1)}, u32[]{:S(2)}, u32[]{:S(2)}) collective-permute-start(bf16[256,256]{1,0:T(8,128)(2,1)S(1)} %first_lower.2), channel_id=1, source_target_pairs={{0,1},{1,0},{2,3},{3,2},{4,5},{5,4},{6,7},{7,6},{8,10},{9,11},{10,... | collective-permute-start | bytes 393224 | tf_op jit(solution)/shard_map/ppermute | solution.py:252
  17.3 0.6 apply_lower.3
  17.9 1.0 %collective-permute-start.10 = (bf16[256,256]{1,0:T(8,128)(2,1)S(1)}, bf16[256,256]{1,0:T(8,128)(2,1)S(1)}, u32[]{:S(2)}, u32[]{:S(2)}) collective-permute-start(bf16[256,256]{1,0:T(8,128)(2,1)S(1)} %get-tuple-element.44), channel_id=1, source_target_pairs={{0,1},{1,0},{2,3},{3,2},{4,5},{5,4},{6,7},{7,6},{8,10},{9,11},{10,... | collective-permute-start | bytes 393224 | tf_op jit(solution)/shard_map/ppermute | solution.py:252
  18.9 1.6 %collective-permute-start.12 = (bf16[256,256]{1,0:T(8,128)(2,1)S(1)}, bf16[256,256]{1,0:T(8,128)(2,1)S(1)}, u32[]{:S(2)}, u32[]{:S(2)}) collective-permute-start(bf16[256,256]{1,0:T(8,128)(2,1)S(1)} %add_convert_fusion.3), channel_id=1, source_target_pairs={{0,2},{1,3},{2,0},{3,1},{4,6},{5,7},{6,4},{7,5},{8,9},{9,8},{10,11... | collective-permute-start | bytes 393224 | tf_op jit(solution)/shard_map/ppermute | solution.py:252
  20.6 0.8 %collective-permute-done.4 = bf16[256,256]{1,0:T(8,128)(2,1)S(1)} collective-permute-done((bf16[256,256]{1,0:T(8,128)(2,1)S(1)}, bf16[256,256]{1,0:T(8,128)(2,1)S(1)}, u32[]{:S(2)}, u32[]{:S(2)}) %collective-permute-start.4) | collective-permute-done | bytes 131104 | tf_op jit(solution)/shard_map/ppermute | solution.py:252
  21.5 2.1 %collective-permute-start.5 = (bf16[256,256]{1,0:T(8,128)(2,1)S(1)}, bf16[256,256]{1,0:T(8,128)(2,1)S(1)}, u32[]{:S(2)}, u32[]{:S(2)}) collective-permute-start(bf16[256,256]{1,0:T(8,128)(2,1)S(1)} %add_convert_fusion.5), channel_id=1, source_target_pairs={{0,2},{1,3},{2,0},{3,1},{4,6},{5,7},{6,4},{7,5},{8,9},{9,8},{10,11... | collective-permute-start | bytes 393224 | tf_op jit(solution)/shard_map/ppermute | solution.py:252
  23.5 0.8 %collective-permute-done.10 = bf16[256,256]{1,0:T(8,128)(2,1)S(1)} collective-permute-done((bf16[256,256]{1,0:T(8,128)(2,1)S(1)}, bf16[256,256]{1,0:T(8,128)(2,1)S(1)}, u32[]{:S(2)}, u32[]{:S(2)}) %collective-permute-start.10) | collective-permute-done | bytes 131104 | tf_op jit(solution)/shard_map/ppermute | solution.py:252
  24.4 2.7 %collective-permute-start.13 = (bf16[256,256]{1,0:T(8,128)(2,1)S(1)}, bf16[256,256]{1,0:T(8,128)(2,1)S(1)}, u32[]{:S(2)}, u32[]{:S(2)}) collective-permute-start(bf16[256,256]{1,0:T(8,128)(2,1)S(1)} %add_convert_fusion.2.mine_ref), channel_id=1, source_target_pairs={{0,4},{1,5},{2,6},{3,7},{4,0},{5,1},{6,2},{7,3},{8,12},{9,13},{10,... | collective-permute-start | bytes 393224 | tf_op jit(solution)/shard_map/ppermute | solution.py:246
  27.1 2.4 %collective-permute-start.6 = (bf16[256,256]{1,0:T(8,128)(2,1)S(1)}, bf16[256,256]{1,0:T(8,128)(2,1)S(1)}, u32[]{:S(2)}, u32[]{:S(2)}) collective-permute-start(bf16[256,256]{1,0:T(8,128)(2,1)S(1)} %add_convert_fusion.4.mine_ref), channel_id=1, source_target_pairs={{0,4},{1,5},{2,6},{3,7},{4,0},{5,1},{6,2},{7,3},{8,12},{9,13},{10,... | collective-permute-start | bytes 393224 | tf_op jit(solution)/shard_map/ppermute | solution.py:246
  29.5 3.3 %sum_upper.1.mat_ref = bf16[8,1024,128]{2,1,0:T(8,128)(2,1)S(1)} custom-call(s32[2]{0:T(128)S(1)} %pad_add_fusion.ids_ref, s32[8,16]{1,0:T(8,128)S(1)} %bitcast.4, bf16[16,8,128,128]{3,2,1,0:T(8,128)(2,1)} %blk_hbm.3), custom_call_target="tpu_custom_call" | custom-call | tf_op jit(solution)/shard_map/sum_upper/pallas_call | solution.py:88
  32.8 1.1 %pick_top.1 = (bf16[256,512]{1,0:T(8,128)(2,1)S(1)}, bf16[2,128,128]{2,1,0:T(8,128)(2,1)S(1)}, bf16[2,128,128]{2,1,0:T(8,128)(2,1)S(1)}) custom-call(s32[2]{0:T(128)S(1)} %pad_add_fusion.ids_ref, bf16[1024,512]{1,0:T(8,128)(2,1)S(1)} %copy-done.2, bf16[8,128,128]{2,1,0:T(8,128)(2,1)S(1)} %copy-done.3, bf16[8,128,128]{2,1,0:T(8,128)(2,1)S(1)} %copy-done.4), custom_call_target="tpu_custom_call" | custom-call | tf_op jit(solution)/shard_map/pick_top/pallas_call | solution.py:127
  34.0 3.1 %collective-permute-done.13.got_ref = bf16[256,256]{1,0:T(8,128)(2,1)S(1)} collective-permute-done((bf16[256,256]{1,0:T(8,128)(2,1)S(1)}, bf16[256,256]{1,0:T(8,128)(2,1)S(1)}, u32[]{:S(2)}, u32[]{:S(2)}) %collective-permute-start.13) | collective-permute-done | bytes 131104 | tf_op jit(solution)/shard_map/ppermute | solution.py:246
  37.1 0.4 solve_top.3.p0
  37.5 1.1 %collective-permute-start.14 = (bf16[256,256]{1,0:T(8,128)(2,1)S(1)}, bf16[256,256]{1,0:T(8,128)(2,1)S(1)}, u32[]{:S(2)}, u32[]{:S(2)}) collective-permute-start(bf16[256,256]{1,0:T(8,128)(2,1)S(1)} %solve_top.3.p0), channel_id=1, source_target_pairs={{0,1},{1,0},{2,3},{3,2},{4,5},{5,4},{6,7},{7,6},{8,10},{9,11},{10,... | collective-permute-start | bytes 393224 | tf_op jit(solution)/shard_map/ppermute | solution.py:252
  38.7 0.4 solve_top.2.p0
  39.1 1.9 %collective-permute-start.19 = (bf16[256,256]{1,0:T(8,128)(2,1)S(1)}, bf16[256,256]{1,0:T(8,128)(2,1)S(1)}, u32[]{:S(2)}, u32[]{:S(2)}) collective-permute-start(bf16[256,256]{1,0:T(8,128)(2,1)S(1)} %solve_top.2.p0), channel_id=1, source_target_pairs={{0,2},{1,3},{2,0},{3,1},{4,6},{5,7},{6,4},{7,5},{8,9},{9,8},{10,11... | collective-permute-start | bytes 393224 | tf_op jit(solution)/shard_map/ppermute | solution.py:252
  41.0 1.0 %collective-permute-start.18 = (bf16[256,256]{1,0:T(8,128)(2,1)S(1)}, bf16[256,256]{1,0:T(8,128)(2,1)S(1)}, u32[]{:S(2)}, u32[]{:S(2)}) collective-permute-start(bf16[256,256]{1,0:T(8,128)(2,1)S(1)} %solve_top.2.p0), channel_id=1, source_target_pairs={{0,1},{1,0},{2,3},{3,2},{4,5},{5,4},{6,7},{7,6},{8,10},{9,11},{10,... | collective-permute-start | bytes 393224 | tf_op jit(solution)/shard_map/ppermute | solution.py:252
  42.0 0.5 collective-permute-done.15.p2
  42.5 1.2 %collective-permute-done.14.p1 = bf16[256,256]{1,0:T(8,128)(2,1)S(1)} collective-permute-done((bf16[256,256]{1,0:T(8,128)(2,1)S(1)}, bf16[256,256]{1,0:T(8,128)(2,1)S(1)}, u32[]{:S(2)}, u32[]{:S(2)}) %collective-permute-start.14) | collective-permute-done | bytes 131104 | tf_op jit(solution)/shard_map/ppermute | solution.py:252
  43.7 0.9 %collective-permute-start.16 = (bf16[256,256]{1,0:T(8,128)(2,1)S(1)}, bf16[256,256]{1,0:T(8,128)(2,1)S(1)}, u32[]{:S(2)}, u32[]{:S(2)}) collective-permute-start(bf16[256,256]{1,0:T(8,128)(2,1)S(1)} %collective-permute-done.15.p2), channel_id=1, source_target_pairs={{0,1},{1,0},{2,3},{3,2},{4,5},{5,4},{6,7},{7,6},{8,10},{9,11},{10,... | collective-permute-start | bytes 393224 | tf_op jit(solution)/shard_map/ppermute | solution.py:252
  44.6 0.9 %collective-permute-done.19.p2 = bf16[256,256]{1,0:T(8,128)(2,1)S(1)} collective-permute-done((bf16[256,256]{1,0:T(8,128)(2,1)S(1)}, bf16[256,256]{1,0:T(8,128)(2,1)S(1)}, u32[]{:S(2)}, u32[]{:S(2)}) %collective-permute-start.19) | collective-permute-done | bytes 131104 | tf_op jit(solution)/shard_map/ppermute | solution.py:252
  45.5 0.4 collective-permute-done.18.p1
  45.9 1.2 %collective-permute-start.20 = (bf16[256,256]{1,0:T(8,128)(2,1)S(1)}, bf16[256,256]{1,0:T(8,128)(2,1)S(1)}, u32[]{:S(2)}, u32[]{:S(2)}) collective-permute-start(bf16[256,256]{1,0:T(8,128)(2,1)S(1)} %collective-permute-done.19.p2), channel_id=1, source_target_pairs={{0,1},{1,0},{2,3},{3,2},{4,5},{5,4},{6,7},{7,6},{8,10},{9,11},{10,... | collective-permute-start | bytes 393224 | tf_op jit(solution)/shard_map/ppermute | solution.py:252
  47.1 1.6 %collective-permute-done.16.p3 = bf16[256,256]{1,0:T(8,128)(2,1)S(1)} collective-permute-done((bf16[256,256]{1,0:T(8,128)(2,1)S(1)}, bf16[256,256]{1,0:T(8,128)(2,1)S(1)}, u32[]{:S(2)}, u32[]{:S(2)}) %collective-permute-start.16) | collective-permute-done | bytes 131104 | tf_op jit(solution)/shard_map/ppermute | solution.py:252
  48.7 0.4 first_upper.2
  49.3 1.6 %collective-permute-done.20.p3 = bf16[256,256]{1,0:T(8,128)(2,1)S(1)} collective-permute-done((bf16[256,256]{1,0:T(8,128)(2,1)S(1)}, bf16[256,256]{1,0:T(8,128)(2,1)S(1)}, u32[]{:S(2)}, u32[]{:S(2)}) %collective-permute-start.20) | collective-permute-done | bytes 131104 | tf_op jit(solution)/shard_map/ppermute | solution.py:252
  50.9 0.4 first_upper.3
  51.5 1.6 %collective-permute-start.22 = (bf16[256,256]{1,0:T(8,128)(2,1)S(1)}, bf16[256,256]{1,0:T(8,128)(2,1)S(1)}, u32[]{:S(2)}, u32[]{:S(2)}) collective-permute-start(bf16[256,256]{1,0:T(8,128)(2,1)S(1)} %add_convert_fusion.1), channel_id=1, source_target_pairs={{0,16},{8,24},{16,0},{24,8},{1,17},{9,25},{17,1},{25,9},{2,18},{10... | collective-permute-start | bytes 393224 | tf_op jit(solution)/shard_map/ppermute | solution.py:246
  53.1 1.3 %collective-permute-start.23 = (bf16[256,256]{1,0:T(8,128)(2,1)S(1)}, bf16[256,256]{1,0:T(8,128)(2,1)S(1)}, u32[]{:S(2)}, u32[]{:S(2)}) collective-permute-start(bf16[256,256]{1,0:T(8,128)(2,1)S(1)} %add_convert_fusion), channel_id=1, source_target_pairs={{0,16},{8,24},{16,0},{24,8},{1,17},{9,25},{17,1},{25,9},{2,18},{10... | collective-permute-start | bytes 393224 | tf_op jit(solution)/shard_map/ppermute | solution.py:246
  54.4 0.4 apply_upper.3
  54.9 0.4 apply_upper.2
  55.3 0.6 collective-permute-start.24
  55.9 0.7 %pad_maximum_fusion = bf16[128,512]{1,0:T(8,128)(2,1)} fusion(bf16[128,256]{1,0:T(8,128)(2,1)S(1)} %slice.9, bf16[128,256]{1,0:T(8,128)(2,1)S(1)} %slice.8), kind=kLoop, calls=%fused_computation.8 | loop fusion | flops 262144 | bytes 262144 | tf_op jit(solution)/shard_map/concatenate | solution.py:370
  56.5 1.3 %collective-permute-done.22 = bf16[256,256]{1,0:T(8,128)(2,1)S(1)} collective-permute-done((bf16[256,256]{1,0:T(8,128)(2,1)S(1)}, bf16[256,256]{1,0:T(8,128)(2,1)S(1)}, u32[]{:S(2)}, u32[]{:S(2)}) %collective-permute-start.22) | collective-permute-done | bytes 131104 | tf_op jit(solution)/shard_map/ppermute | solution.py:246
  57.9 0.9 %solve_low.2.refs_2_ = bf16[256,512]{1,0:T(8,128)(2,1)} custom-call(bf16[2,128,128]{2,1,0:T(8,128)(2,1)S(1)} %copy-done.5, bf16[256,256]{1,0:T(8,128)(2,1)S(1)} %copy-done.1, f32[256,256]{1,0:T(8,128)S(1)} %convert_add_fusion.refs_0_, bf16[256,256]{1,0:T(8,128)(2,1)S(1)} %collective-permute-done.25.refs_1_), custom_call_target="tpu_custom_call" | custom-call | tf_op jit(solution)/shard_map/solve_low/pallas_call | solution.py:227
  58.8 1.5 %collective-permute-done.23 = bf16[256,256]{1,0:T(8,128)(2,1)S(1)} collective-permute-done((bf16[256,256]{1,0:T(8,128)(2,1)S(1)}, bf16[256,256]{1,0:T(8,128)(2,1)S(1)}, u32[]{:S(2)}, u32[]{:S(2)}) %collective-permute-start.23) | collective-permute-done | bytes 131104 | tf_op jit(solution)/shard_map/ppermute | solution.py:246
  60.3 0.9 %solve_low.3 = bf16[256,512]{1,0:T(8,128)(2,1)} custom-call(bf16[2,128,128]{2,1,0:T(8,128)(2,1)S(1)} %copy-done.5, bf16[256,256]{1,0:T(8,128)(2,1)S(1)} %copy-done, f32[256,256]{1,0:T(8,128)S(1)} %convert_add_fusion.1.refs_0_, bf16[256,256]{1,0:T(8,128)(2,1)S(1)} %collective-permute-done.24.refs_1_, ...), custom_call_target="tpu_custom_call", output_to_operand_aliasing={{}: (4, {})} | custom-call | tf_op jit(solution)/shard_map/solve_low/pallas_call | solution.py:227
  (46 shorter events, 1.2 us)
Async XLA Ops:
  2.5 7.7 %copy-start = (bf16[256,256]{1,0:T(8,128)(2,1)S(1)}, bf16[256,256]{1,0:T(8,128)(2,1)}, u32[]{:S(2)}) copy-start(bf16[256,256]{1,0:T(8,128)(2,1)} %get-tuple-element.31.p0.fwd_ref) | copy-start | bytes 393220
  2.5 9.6 %copy-start.1 = (bf16[256,256]{1,0:T(8,128)(2,1)S(1)}, bf16[256,256]{1,0:T(8,128)(2,1)}, u32[]{:S(2)}) copy-start(bf16[256,256]{1,0:T(8,128)(2,1)} %get-tuple-element.41.p0.fwd_ref) | copy-start | bytes 393220
  2.5 7.3 %collective-permute-start.8 = (bf16[256,256]{1,0:T(8,128)(2,1)}, bf16[256,256]{1,0:T(8,128)(2,1)S(1)}, u32[]{:S(2)}, u32[]{:S(2)}) collective-permute-start(bf16[256,256]{1,0:T(8,128)(2,1)} %get-tuple-element.41.p0.fwd_ref), channel_id=1, source_target_pairs={{0,16},{8,24},{16,0},{24,8},{1,17},{9,25},{17,1},{25,9},{2,18},{10... | collective-permute-start | bytes 393224 | tf_op jit(solution)/shard_map/ppermute | solution.py:246
  5.6 6.5 %collective-permute-start.7 = (bf16[256,256]{1,0:T(8,128)(2,1)}, bf16[256,256]{1,0:T(8,128)(2,1)S(1)}, u32[]{:S(2)}, u32[]{:S(2)}) collective-permute-start(bf16[256,256]{1,0:T(8,128)(2,1)} %get-tuple-element.41.p0.fwd_ref), channel_id=1, source_target_pairs={{0,8},{8,0},{16,24},{24,16},{1,9},{9,1},{17,25},{25,17},{2,10},{10... | collective-permute-start | bytes 393224 | tf_op jit(solution)/shard_map/ppermute | solution.py:246
  5.6 6.5 %collective-permute-start.1 = (bf16[256,256]{1,0:T(8,128)(2,1)}, bf16[256,256]{1,0:T(8,128)(2,1)S(1)}, u32[]{:S(2)}, u32[]{:S(2)}) collective-permute-start(bf16[256,256]{1,0:T(8,128)(2,1)} %get-tuple-element.31.p0.fwd_ref), channel_id=1, source_target_pairs={{0,16},{8,24},{16,0},{24,8},{1,17},{9,25},{17,1},{25,9},{2,18},{10... | collective-permute-start | bytes 393224 | tf_op jit(solution)/shard_map/ppermute | solution.py:246
  5.8 0.7 %copy-start.6 = (s32[16,8]{0,1:T(8,128)S(1)}, s32[16,8]{0,1:T(8,128)}, u32[]{:S(2)}) copy-start(s32[16,8]{0,1:T(8,128)} %param.13) | copy-start | bytes 1540
  9.8 2.3 %collective-permute-start.9 = (bf16[256,256]{1,0:T(8,128)(2,1)S(1)}, bf16[256,256]{1,0:T(8,128)(2,1)S(1)}, u32[]{:S(2)}, u32[]{:S(2)}) collective-permute-start(bf16[256,256]{1,0:T(8,128)(2,1)S(1)} %collective-permute-done.8.p2), channel_id=1, source_target_pairs={{0,8},{8,0},{16,24},{24,16},{1,9},{9,1},{17,25},{25,17},{2,10},{10... | collective-permute-start | bytes 393224 | tf_op jit(solution)/shard_map/ppermute | solution.py:246
  10.2 4.0 %collective-permute-start = (bf16[256,256]{1,0:T(8,128)(2,1)S(1)}, bf16[256,256]{1,0:T(8,128)(2,1)S(1)}, u32[]{:S(2)}, u32[]{:S(2)}) collective-permute-start(bf16[256,256]{1,0:T(8,128)(2,1)S(1)} %copy-done), channel_id=1, source_target_pairs={{0,8},{8,0},{16,24},{24,16},{1,9},{9,1},{17,25},{25,17},{2,10},{10... | collective-permute-start | bytes 393224 | tf_op jit(solution)/shard_map/ppermute | solution.py:246
  12.1 2.1 %collective-permute-start.2 = (bf16[256,256]{1,0:T(8,128)(2,1)S(1)}, bf16[256,256]{1,0:T(8,128)(2,1)S(1)}, u32[]{:S(2)}, u32[]{:S(2)}) collective-permute-start(bf16[256,256]{1,0:T(8,128)(2,1)S(1)} %collective-permute-done.1.p2), channel_id=1, source_target_pairs={{0,8},{8,0},{16,24},{24,16},{1,9},{9,1},{17,25},{25,17},{2,10},{10... | collective-permute-start | bytes 393224 | tf_op jit(solution)/shard_map/ppermute | solution.py:246
  12.4 6.5 %collective-permute-start.11 = (bf16[256,256]{1,0:T(8,128)(2,1)S(1)}, bf16[256,256]{1,0:T(8,128)(2,1)S(1)}, u32[]{:S(2)}, u32[]{:S(2)}) collective-permute-start(bf16[256,256]{1,0:T(8,128)(2,1)S(1)} %first_lower.3), channel_id=1, source_target_pairs={{0,1},{1,0},{2,3},{3,2},{4,5},{5,4},{6,7},{7,6},{8,10},{9,11},{10,... | collective-permute-start | bytes 393224 | tf_op jit(solution)/shard_map/ppermute | solution.py:252
  14.8 12.2 %collective-permute-start.3 = (bf16[256,256]{1,0:T(8,128)(2,1)S(1)}, bf16[256,256]{1,0:T(8,128)(2,1)S(1)}, u32[]{:S(2)}, u32[]{:S(2)}) collective-permute-start(bf16[256,256]{1,0:T(8,128)(2,1)S(1)} %get-tuple-element.34), channel_id=1, source_target_pairs={{0,1},{1,0},{2,3},{3,2},{4,5},{5,4},{6,7},{7,6},{8,10},{9,11},{10,... | collective-permute-start | bytes 393224 | tf_op jit(solution)/shard_map/ppermute | solution.py:252
  16.1 5.3 %collective-permute-start.4 = (bf16[256,256]{1,0:T(8,128)(2,1)S(1)}, bf16[256,256]{1,0:T(8,128)(2,1)S(1)}, u32[]{:S(2)}, u32[]{:S(2)}) collective-permute-start(bf16[256,256]{1,0:T(8,128)(2,1)S(1)} %first_lower.2), channel_id=1, source_target_pairs={{0,1},{1,0},{2,3},{3,2},{4,5},{5,4},{6,7},{7,6},{8,10},{9,11},{10,... | collective-permute-start | bytes 393224 | tf_op jit(solution)/shard_map/ppermute | solution.py:252
  17.9 15.0 %copy-start.2 = (bf16[1024,512]{1,0:T(8,128)(2,1)S(1)}, bf16[1024,512]{1,0:T(8,128)(2,1)}, u32[]{:S(2)}) copy-start(bf16[1024,512]{1,0:T(8,128)(2,1)} %rhs_hbm.3) | copy-start | bytes 3145732
  17.9 15.0 %copy-start.3 = (bf16[8,128,128]{2,1,0:T(8,128)(2,1)S(1)}, bf16[8,128,128]{2,1,0:T(8,128)(2,1)}, u32[]{:S(2)}) copy-start(bf16[8,128,128]{2,1,0:T(8,128)(2,1)} %low_hbm.1) | copy-start | bytes 786436
  17.9 15.0 %copy-start.4 = (bf16[8,128,128]{2,1,0:T(8,128)(2,1)S(1)}, bf16[8,128,128]{2,1,0:T(8,128)(2,1)}, u32[]{:S(2)}) copy-start(bf16[8,128,128]{2,1,0:T(8,128)(2,1)} %up_hbm.1) | copy-start | bytes 786436
  17.9 6.4 %collective-permute-start.10 = (bf16[256,256]{1,0:T(8,128)(2,1)S(1)}, bf16[256,256]{1,0:T(8,128)(2,1)S(1)}, u32[]{:S(2)}, u32[]{:S(2)}) collective-permute-start(bf16[256,256]{1,0:T(8,128)(2,1)S(1)} %get-tuple-element.44), channel_id=1, source_target_pairs={{0,1},{1,0},{2,3},{3,2},{4,5},{5,4},{6,7},{7,6},{8,10},{9,11},{10,... | collective-permute-start | bytes 393224 | tf_op jit(solution)/shard_map/ppermute | solution.py:252
  18.9 5.4 %collective-permute-start.12 = (bf16[256,256]{1,0:T(8,128)(2,1)S(1)}, bf16[256,256]{1,0:T(8,128)(2,1)S(1)}, u32[]{:S(2)}, u32[]{:S(2)}) collective-permute-start(bf16[256,256]{1,0:T(8,128)(2,1)S(1)} %add_convert_fusion.3), channel_id=1, source_target_pairs={{0,2},{1,3},{2,0},{3,1},{4,6},{5,7},{6,4},{7,5},{8,9},{9,8},{10,11... | collective-permute-start | bytes 393224 | tf_op jit(solution)/shard_map/ppermute | solution.py:252
  21.5 5.6 %collective-permute-start.5 = (bf16[256,256]{1,0:T(8,128)(2,1)S(1)}, bf16[256,256]{1,0:T(8,128)(2,1)S(1)}, u32[]{:S(2)}, u32[]{:S(2)}) collective-permute-start(bf16[256,256]{1,0:T(8,128)(2,1)S(1)} %add_convert_fusion.5), channel_id=1, source_target_pairs={{0,2},{1,3},{2,0},{3,1},{4,6},{5,7},{6,4},{7,5},{8,9},{9,8},{10,11... | collective-permute-start | bytes 393224 | tf_op jit(solution)/shard_map/ppermute | solution.py:252
  24.4 12.7 %collective-permute-start.13 = (bf16[256,256]{1,0:T(8,128)(2,1)S(1)}, bf16[256,256]{1,0:T(8,128)(2,1)S(1)}, u32[]{:S(2)}, u32[]{:S(2)}) collective-permute-start(bf16[256,256]{1,0:T(8,128)(2,1)S(1)} %add_convert_fusion.2.mine_ref), channel_id=1, source_target_pairs={{0,4},{1,5},{2,6},{3,7},{4,0},{5,1},{6,2},{7,3},{8,12},{9,13},{10,... | collective-permute-start | bytes 393224 | tf_op jit(solution)/shard_map/ppermute | solution.py:246
  27.1 11.6 %collective-permute-start.6 = (bf16[256,256]{1,0:T(8,128)(2,1)S(1)}, bf16[256,256]{1,0:T(8,128)(2,1)S(1)}, u32[]{:S(2)}, u32[]{:S(2)}) collective-permute-start(bf16[256,256]{1,0:T(8,128)(2,1)S(1)} %add_convert_fusion.4.mine_ref), channel_id=1, source_target_pairs={{0,4},{1,5},{2,6},{3,7},{4,0},{5,1},{6,2},{7,3},{8,12},{9,13},{10,... | collective-permute-start | bytes 393224 | tf_op jit(solution)/shard_map/ppermute | solution.py:246
  37.4 5.1 %collective-permute-start.15 = (bf16[256,256]{1,0:T(8,128)(2,1)S(1)}, bf16[256,256]{1,0:T(8,128)(2,1)S(1)}, u32[]{:S(2)}, u32[]{:S(2)}) collective-permute-start(bf16[256,256]{1,0:T(8,128)(2,1)S(1)} %solve_top.3.p0), channel_id=1, source_target_pairs={{0,2},{1,3},{2,0},{3,1},{4,6},{5,7},{6,4},{7,5},{8,9},{9,8},{10,11... | collective-permute-start | bytes 393224 | tf_op jit(solution)/shard_map/ppermute | solution.py:252
  37.5 6.2 %collective-permute-start.14 = (bf16[256,256]{1,0:T(8,128)(2,1)S(1)}, bf16[256,256]{1,0:T(8,128)(2,1)S(1)}, u32[]{:S(2)}, u32[]{:S(2)}) collective-permute-start(bf16[256,256]{1,0:T(8,128)(2,1)S(1)} %solve_top.3.p0), channel_id=1, source_target_pairs={{0,1},{1,0},{2,3},{3,2},{4,5},{5,4},{6,7},{7,6},{8,10},{9,11},{10,... | collective-permute-start | bytes 393224 | tf_op jit(solution)/shard_map/ppermute | solution.py:252
  39.1 6.4 %collective-permute-start.19 = (bf16[256,256]{1,0:T(8,128)(2,1)S(1)}, bf16[256,256]{1,0:T(8,128)(2,1)S(1)}, u32[]{:S(2)}, u32[]{:S(2)}) collective-permute-start(bf16[256,256]{1,0:T(8,128)(2,1)S(1)} %solve_top.2.p0), channel_id=1, source_target_pairs={{0,2},{1,3},{2,0},{3,1},{4,6},{5,7},{6,4},{7,5},{8,9},{9,8},{10,11... | collective-permute-start | bytes 393224 | tf_op jit(solution)/shard_map/ppermute | solution.py:252
  41.0 5.0 %collective-permute-start.18 = (bf16[256,256]{1,0:T(8,128)(2,1)S(1)}, bf16[256,256]{1,0:T(8,128)(2,1)S(1)}, u32[]{:S(2)}, u32[]{:S(2)}) collective-permute-start(bf16[256,256]{1,0:T(8,128)(2,1)S(1)} %solve_top.2.p0), channel_id=1, source_target_pairs={{0,1},{1,0},{2,3},{3,2},{4,5},{5,4},{6,7},{7,6},{8,10},{9,11},{10,... | collective-permute-start | bytes 393224 | tf_op jit(solution)/shard_map/ppermute | solution.py:252
  43.7 5.0 %collective-permute-start.16 = (bf16[256,256]{1,0:T(8,128)(2,1)S(1)}, bf16[256,256]{1,0:T(8,128)(2,1)S(1)}, u32[]{:S(2)}, u32[]{:S(2)}) collective-permute-start(bf16[256,256]{1,0:T(8,128)(2,1)S(1)} %collective-permute-done.15.p2), channel_id=1, source_target_pairs={{0,1},{1,0},{2,3},{3,2},{4,5},{5,4},{6,7},{7,6},{8,10},{9,11},{10,... | collective-permute-start | bytes 393224 | tf_op jit(solution)/shard_map/ppermute | solution.py:252
  45.9 5.0 %collective-permute-start.20 = (bf16[256,256]{1,0:T(8,128)(2,1)S(1)}, bf16[256,256]{1,0:T(8,128)(2,1)S(1)}, u32[]{:S(2)}, u32[]{:S(2)}) collective-permute-start(bf16[256,256]{1,0:T(8,128)(2,1)S(1)} %collective-permute-done.19.p2), channel_id=1, source_target_pairs={{0,1},{1,0},{2,3},{3,2},{4,5},{5,4},{6,7},{7,6},{8,10},{9,11},{10,... | collective-permute-start | bytes 393224 | tf_op jit(solution)/shard_map/ppermute | solution.py:252
  49.1 2.3 %collective-permute-start.17 = (bf16[256,256]{1,0:T(8,128)(2,1)S(1)}, bf16[256,256]{1,0:T(8,128)(2,1)S(1)}, u32[]{:S(2)}, u32[]{:S(2)}) collective-permute-start(bf16[256,256]{1,0:T(8,128)(2,1)S(1)} %get-tuple-element.48), channel_id=1, source_target_pairs={{0,8},{8,0},{16,24},{24,16},{1,9},{9,1},{17,25},{25,17},{2,10},{10... | collective-permute-start | bytes 393224 | tf_op jit(solution)/shard_map/ppermute | solution.py:246
  49.3 8.6 %copy-start.5 = (bf16[2,128,128]{2,1,0:T(8,128)(2,1)S(1)}, bf16[2,128,128]{2,1,0:T(8,128)(2,1)}, u32[]{:S(2)}) copy-start(bf16[2,128,128]{2,1,0:T(8,128)(2,1)} %inv_ref.3) | copy-start | bytes 196612
  51.3 1.7 %collective-permute-start.21 = (bf16[256,256]{1,0:T(8,128)(2,1)S(1)}, bf16[256,256]{1,0:T(8,128)(2,1)S(1)}, u32[]{:S(2)}, u32[]{:S(2)}) collective-permute-start(bf16[256,256]{1,0:T(8,128)(2,1)S(1)} %get-tuple-element.51), channel_id=1, source_target_pairs={{0,8},{8,0},{16,24},{24,16},{1,9},{9,1},{17,25},{25,17},{2,10},{10... | collective-permute-start | bytes 393224 | tf_op jit(solution)/shard_map/ppermute | solution.py:246
  51.5 6.4 %collective-permute-start.22 = (bf16[256,256]{1,0:T(8,128)(2,1)S(1)}, bf16[256,256]{1,0:T(8,128)(2,1)S(1)}, u32[]{:S(2)}, u32[]{:S(2)}) collective-permute-start(bf16[256,256]{1,0:T(8,128)(2,1)S(1)} %add_convert_fusion.1), channel_id=1, source_target_pairs={{0,16},{8,24},{16,0},{24,8},{1,17},{9,25},{17,1},{25,9},{2,18},{10... | collective-permute-start | bytes 393224 | tf_op jit(solution)/shard_map/ppermute | solution.py:246
  53.1 7.1 %collective-permute-start.23 = (bf16[256,256]{1,0:T(8,128)(2,1)S(1)}, bf16[256,256]{1,0:T(8,128)(2,1)S(1)}, u32[]{:S(2)}, u32[]{:S(2)}) collective-permute-start(bf16[256,256]{1,0:T(8,128)(2,1)S(1)} %add_convert_fusion), channel_id=1, source_target_pairs={{0,16},{8,24},{16,0},{24,8},{1,17},{9,25},{17,1},{25,9},{2,18},{10... | collective-permute-start | bytes 393224 | tf_op jit(solution)/shard_map/ppermute | solution.py:246
  54.8 3.1 %collective-permute-start.25 = (bf16[256,256]{1,0:T(8,128)(2,1)S(1)}, bf16[256,256]{1,0:T(8,128)(2,1)S(1)}, u32[]{:S(2)}, u32[]{:S(2)}) collective-permute-start(bf16[256,256]{1,0:T(8,128)(2,1)S(1)} %get-tuple-element.58), channel_id=1, source_target_pairs={{0,8},{8,0},{16,24},{24,16},{1,9},{9,1},{17,25},{25,17},{2,10},{10... | collective-permute-start | bytes 393224 | tf_op jit(solution)/shard_map/ppermute | solution.py:246
  55.3 5.0 %collective-permute-start.24 = (bf16[256,256]{1,0:T(8,128)(2,1)S(1)}, bf16[256,256]{1,0:T(8,128)(2,1)S(1)}, u32[]{:S(2)}, u32[]{:S(2)}) collective-permute-start(bf16[256,256]{1,0:T(8,128)(2,1)S(1)} %get-tuple-element.55), channel_id=1, source_target_pairs={{0,8},{8,0},{16,24},{24,16},{1,9},{9,1},{17,25},{25,17},{2,10},{10... | collective-permute-start | bytes 393224 | tf_op jit(solution)/shard_map/ppermute | solution.py:246
